TPU v7x, 256 devices: a whole 4x4x8 slice. The times are simulated.
256 devices in a mesh: group: 4 (over x_hi, core), blk: 64 (over y, x_lo, z).
Axes of the slice: x: 4 (x_hi: 2, x_lo: 2; x = x_hi * 2 + x_lo), y: 4, z: 8, core: 2. Of those that a mesh axis runs over, the one named last changes fastest.
Arguments:
- images: bfloat16 [16384, 1152], P(('group', 'blk')), may hold values from -0.72 to 0.72
- texts: bfloat16 [16384, 1152], P(('group', 'blk')), may hold values from -0.72 to 0.72
- logit_scale: float32 [1], replicated, may hold values from 3 to 8
- bias: float32 [1], replicated, may hold values from -3 to -1
Outputs:
- image_grads: float32 [16384, 1152], P(('group', 'blk'))
- text_grads: float32 [16384, 1152], P(('group', 'blk'))
All inputs are finite; a program needn't handle non-finite values.
Results may differ from a plain program's by a relative error of at most 0.00067.
Values may be sent and summed in bfloat16 or wider, within the bound.
No kernel may reach another device: no remote copies, remote signals or barrier semaphores. Data moves between devices by JAX's collectives and lax.ppermute only.
A program may use at most 128 MiB of HBM per device.

v0:
```python
import jax
import jax.numpy as jnp
from jax import lax
from jax.sharding import PartitionSpec as P

epsilon = 1e-06


def from_behind(array, axis, by):
    devices = lax.axis_size(axis)
    return lax.ppermute(array, axis, [(i, (i + by) % devices) for i in range(devices)])


def normalize(embedding):
    values = embedding.astype(jnp.float32)
    inverse = lax.rsqrt(jnp.sum(values * values, axis=-1, keepdims=True) + epsilon)
    return (values * inverse, inverse)


def unit_grad(unit_vec, inverse, grad_sum):
    return (grad_sum - unit_vec * jnp.sum(unit_vec * grad_sum, axis=-1, keepdims=True)) * inverse


def pair_grads(text_block, text_ids, image_low, image_ids, factor, offset):
    logits = (
        factor
        * lax.dot_general(
            text_block, image_low, (((1,), (1,)), ((), ())), preferred_element_type=jnp.float32
        )
        + offset
    )
    positive = (text_ids[:, None] == image_ids[None, :]).astype(jnp.float32)
    weights_tile = (factor * (jax.nn.sigmoid(logits) - positive)).astype(jnp.bfloat16)
    text_part = jnp.dot(weights_tile, image_low, preferred_element_type=jnp.float32)
    image_part = lax.dot_general(
        weights_tile, text_block, (((0,), (0,)), ((), ())), preferred_element_type=jnp.float32
    )
    return (text_part, image_part)


def body(images, texts, logit_scale, bias):
    image_unit, image_inv = normalize(images)
    text_unit, text_inv = normalize(texts)
    gathered = lax.all_gather(image_unit.astype(jnp.bfloat16), "group", axis=0, tiled=True)
    text_low = text_unit.astype(jnp.bfloat16)
    factor = logit_scale[0]
    offset = bias[0]
    local_rows = texts.shape[0]
    width_cols = texts.shape[1]
    group_pos = lax.axis_index("group")
    cycle_pos = lax.axis_index("blk")
    cycle_size = lax.axis_size("blk")
    group_size = lax.axis_size("group")
    reach = 1
    image_ids = (
        (
            jnp.arange(group_size, dtype=jnp.int32)[:, None] * cycle_size
            + (cycle_pos + 0) % cycle_size
        )
        * local_rows
        + jnp.arange(local_rows, dtype=jnp.int32)[None, :]
    ).reshape(-1)
    hop_count = cycle_size // reach
    layout = ((0, local_rows, 1),)
    blocks = tuple((text_low for row_from, row_count, heading in layout))
    partials = tuple(
        (jnp.zeros((row_count, width_cols), jnp.float32) for row_from, row_count, heading in layout)
    )
    image_start = jnp.zeros(gathered.shape, jnp.float32)

    def visit(hop_number, carried_state):
        text_blocks, partial_state, image_sum = carried_state
        text_parts = []
        sources = []
        for position, (row_from, row_count, heading) in enumerate(layout):
            source = (cycle_pos - heading * reach * hop_number) % cycle_size
            text_ids = (
                (group_pos * cycle_size + source) * local_rows
                + row_from
                + jnp.arange(row_count, dtype=jnp.int32)
            )
            text_part, image_part = pair_grads(
                text_blocks[position], text_ids, gathered, image_ids, factor, offset
            )
            image_sum = image_sum + image_part
            text_parts.append(text_part)
            sources.append(source)
        moved_up = from_behind(text_blocks[0], "blk", reach)
        next_blocks = (moved_up,)
        sum_up = from_behind(partial_state[0] + text_parts[0], "blk", reach)
        new_state = (sum_up,)
        return (next_blocks, new_state, image_sum)

    final_blocks, partial_state, image_sum = lax.fori_loop(
        0, hop_count, visit, (blocks, partials, image_start)
    )
    text_sum = partial_state[0]
    image_own = lax.psum_scatter(image_sum, "group", scatter_dimension=0, tiled=True)
    return (unit_grad(image_unit, image_inv, image_own), unit_grad(text_unit, text_inv, text_sum))


def solution(mesh):
    return jax.shard_map(
        body,
        mesh=mesh,
        in_specs=(P(("group", "blk"), None), P(("group", "blk"), None), P(), P()),
        out_specs=(P(("group", "blk"), None), P(("group", "blk"), None)),
        check_vma=False,
    )
```

profile of v0, /device:TPU:24, one launch (start us, length us, event | category | flops | bytes accessed | tf_op | source)
XLA Modules:
  0.0 1104.0 jit_solution(16422715674132117617)
XLA Ops:
  20.5 981.1 %while.20 = (s32[]{:T(128)}, bf16[64,1152]{1,0:T(8,128)(2,1)S(1)}, f32[64,1152]{1,0:T(8,128)S(1)}, f32[256,1152]{1,0:T(8,128)S(1)}, f32[]{:T(128)}, /*index=5*/b...) while((s32[]{:T(128)}, bf16[64,1152]{1,0:T(8,128)(2,1)S(1)}, ...), condition=%wide.region_3.4_spmd.clone, body=%wide.region_2.3_spmd.clone.sunk | while | flops 114073936 | bytes 6591372 | solution.py:94
  27.0 12.9 %collective-permute-done = bf16[64,1152]{1,0:T(8,128)(2,1)S(1)} collective-permute-done((bf16[64,1152]{1,0:T(8,128)(2,1)S(1)}, bf16[64,1152]{1,0:T(8,128)(2,1)S(1)}, u32[]{:S(2)}, u32[]{:S(2)}) %collective-permute-start) | collective-permute-done | bytes 147488 | tf_op jit(solution)/shard_map/while/body/eval_jaxpr/ppermute | solution.py:11
  42.6 14.2 %collective-permute-done = bf16[64,1152]{1,0:T(8,128)(2,1)S(1)} collective-permute-done((bf16[64,1152]{1,0:T(8,128)(2,1)S(1)}, bf16[64,1152]{1,0:T(8,128)(2,1)S(1)}, u32[]{:S(2)}, u32[]{:S(2)}) %collective-permute-start) | collective-permute-done | bytes 147488 | tf_op jit(solution)/shard_map/while/body/eval_jaxpr/ppermute | solution.py:11
  59.6 13.3 %collective-permute-done = bf16[64,1152]{1,0:T(8,128)(2,1)S(1)} collective-permute-done((bf16[64,1152]{1,0:T(8,128)(2,1)S(1)}, bf16[64,1152]{1,0:T(8,128)(2,1)S(1)}, u32[]{:S(2)}, u32[]{:S(2)}) %collective-permute-start) | collective-permute-done | bytes 147488 | tf_op jit(solution)/shard_map/while/body/eval_jaxpr/ppermute | solution.py:11
  75.7 12.4 %collective-permute-done = bf16[64,1152]{1,0:T(8,128)(2,1)S(1)} collective-permute-done((bf16[64,1152]{1,0:T(8,128)(2,1)S(1)}, bf16[64,1152]{1,0:T(8,128)(2,1)S(1)}, u32[]{:S(2)}, u32[]{:S(2)}) %collective-permute-start) | collective-permute-done | bytes 147488 | tf_op jit(solution)/shard_map/while/body/eval_jaxpr/ppermute | solution.py:11
  90.8 11.5 %collective-permute-done = bf16[64,1152]{1,0:T(8,128)(2,1)S(1)} collective-permute-done((bf16[64,1152]{1,0:T(8,128)(2,1)S(1)}, bf16[64,1152]{1,0:T(8,128)(2,1)S(1)}, u32[]{:S(2)}, u32[]{:S(2)}) %collective-permute-start) | collective-permute-done | bytes 147488 | tf_op jit(solution)/shard_map/while/body/eval_jaxpr/ppermute | solution.py:11
  105.1 10.7 collective-permute-done
  145.3 11.4 %collective-permute-done = bf16[64,1152]{1,0:T(8,128)(2,1)S(1)} collective-permute-done((bf16[64,1152]{1,0:T(8,128)(2,1)S(1)}, bf16[64,1152]{1,0:T(8,128)(2,1)S(1)}, u32[]{:S(2)}, u32[]{:S(2)}) %collective-permute-start) | collective-permute-done | bytes 147488 | tf_op jit(solution)/shard_map/while/body/eval_jaxpr/ppermute | solution.py:11
  159.5 12.5 %collective-permute-done = bf16[64,1152]{1,0:T(8,128)(2,1)S(1)} collective-permute-done((bf16[64,1152]{1,0:T(8,128)(2,1)S(1)}, bf16[64,1152]{1,0:T(8,128)(2,1)S(1)}, u32[]{:S(2)}, u32[]{:S(2)}) %collective-permute-start) | collective-permute-done | bytes 147488 | tf_op jit(solution)/shard_map/while/body/eval_jaxpr/ppermute | solution.py:11
  174.7 13.5 %collective-permute-done = bf16[64,1152]{1,0:T(8,128)(2,1)S(1)} collective-permute-done((bf16[64,1152]{1,0:T(8,128)(2,1)S(1)}, bf16[64,1152]{1,0:T(8,128)(2,1)S(1)}, u32[]{:S(2)}, u32[]{:S(2)}) %collective-permute-start) | collective-permute-done | bytes 147488 | tf_op jit(solution)/shard_map/while/body/eval_jaxpr/ppermute | solution.py:11
  191.0 14.7 %collective-permute-done = bf16[64,1152]{1,0:T(8,128)(2,1)S(1)} collective-permute-done((bf16[64,1152]{1,0:T(8,128)(2,1)S(1)}, bf16[64,1152]{1,0:T(8,128)(2,1)S(1)}, u32[]{:S(2)}, u32[]{:S(2)}) %collective-permute-start) | collective-permute-done | bytes 147488 | tf_op jit(solution)/shard_map/while/body/eval_jaxpr/ppermute | solution.py:11
  208.4 15.0 %collective-permute-done = bf16[64,1152]{1,0:T(8,128)(2,1)S(1)} collective-permute-done((bf16[64,1152]{1,0:T(8,128)(2,1)S(1)}, bf16[64,1152]{1,0:T(8,128)(2,1)S(1)}, u32[]{:S(2)}, u32[]{:S(2)}) %collective-permute-start) | collective-permute-done | bytes 147488 | tf_op jit(solution)/shard_map/while/body/eval_jaxpr/ppermute | solution.py:11
  226.1 14.2 %collective-permute-done = bf16[64,1152]{1,0:T(8,128)(2,1)S(1)} collective-permute-done((bf16[64,1152]{1,0:T(8,128)(2,1)S(1)}, bf16[64,1152]{1,0:T(8,128)(2,1)S(1)}, u32[]{:S(2)}, u32[]{:S(2)}) %collective-permute-start) | collective-permute-done | bytes 147488 | tf_op jit(solution)/shard_map/while/body/eval_jaxpr/ppermute | solution.py:11
  243.1 13.3 %collective-permute-done = bf16[64,1152]{1,0:T(8,128)(2,1)S(1)} collective-permute-done((bf16[64,1152]{1,0:T(8,128)(2,1)S(1)}, bf16[64,1152]{1,0:T(8,128)(2,1)S(1)}, u32[]{:S(2)}, u32[]{:S(2)}) %collective-permute-start) | collective-permute-done | bytes 147488 | tf_op jit(solution)/shard_map/while/body/eval_jaxpr/ppermute | solution.py:11
  259.2 12.4 %collective-permute-done = bf16[64,1152]{1,0:T(8,128)(2,1)S(1)} collective-permute-done((bf16[64,1152]{1,0:T(8,128)(2,1)S(1)}, bf16[64,1152]{1,0:T(8,128)(2,1)S(1)}, u32[]{:S(2)}, u32[]{:S(2)}) %collective-permute-start) | collective-permute-done | bytes 147488 | tf_op jit(solution)/shard_map/while/body/eval_jaxpr/ppermute | solution.py:11
  274.3 11.5 %collective-permute-done = bf16[64,1152]{1,0:T(8,128)(2,1)S(1)} collective-permute-done((bf16[64,1152]{1,0:T(8,128)(2,1)S(1)}, bf16[64,1152]{1,0:T(8,128)(2,1)S(1)}, u32[]{:S(2)}, u32[]{:S(2)}) %collective-permute-start) | collective-permute-done | bytes 147488 | tf_op jit(solution)/shard_map/while/body/eval_jaxpr/ppermute | solution.py:11
  302.0 10.7 collective-permute-done
  328.8 11.4 %collective-permute-done = bf16[64,1152]{1,0:T(8,128)(2,1)S(1)} collective-permute-done((bf16[64,1152]{1,0:T(8,128)(2,1)S(1)}, bf16[64,1152]{1,0:T(8,128)(2,1)S(1)}, u32[]{:S(2)}, u32[]{:S(2)}) %collective-permute-start) | collective-permute-done | bytes 147488 | tf_op jit(solution)/shard_map/while/body/eval_jaxpr/ppermute | solution.py:11
  342.9 12.5 %collective-permute-done = bf16[64,1152]{1,0:T(8,128)(2,1)S(1)} collective-permute-done((bf16[64,1152]{1,0:T(8,128)(2,1)S(1)}, bf16[64,1152]{1,0:T(8,128)(2,1)S(1)}, u32[]{:S(2)}, u32[]{:S(2)}) %collective-permute-start) | collective-permute-done | bytes 147488 | tf_op jit(solution)/shard_map/while/body/eval_jaxpr/ppermute | solution.py:11
  358.2 13.5 %collective-permute-done = bf16[64,1152]{1,0:T(8,128)(2,1)S(1)} collective-permute-done((bf16[64,1152]{1,0:T(8,128)(2,1)S(1)}, bf16[64,1152]{1,0:T(8,128)(2,1)S(1)}, u32[]{:S(2)}, u32[]{:S(2)}) %collective-permute-start) | collective-permute-done | bytes 147488 | tf_op jit(solution)/shard_map/while/body/eval_jaxpr/ppermute | solution.py:11
  374.5 14.7 %collective-permute-done = bf16[64,1152]{1,0:T(8,128)(2,1)S(1)} collective-permute-done((bf16[64,1152]{1,0:T(8,128)(2,1)S(1)}, bf16[64,1152]{1,0:T(8,128)(2,1)S(1)}, u32[]{:S(2)}, u32[]{:S(2)}) %collective-permute-start) | collective-permute-done | bytes 147488 | tf_op jit(solution)/shard_map/while/body/eval_jaxpr/ppermute | solution.py:11
  391.9 15.0 %collective-permute-done = bf16[64,1152]{1,0:T(8,128)(2,1)S(1)} collective-permute-done((bf16[64,1152]{1,0:T(8,128)(2,1)S(1)}, bf16[64,1152]{1,0:T(8,128)(2,1)S(1)}, u32[]{:S(2)}, u32[]{:S(2)}) %collective-permute-start) | collective-permute-done | bytes 147488 | tf_op jit(solution)/shard_map/while/body/eval_jaxpr/ppermute | solution.py:11
  409.7 14.2 %collective-permute-done = bf16[64,1152]{1,0:T(8,128)(2,1)S(1)} collective-permute-done((bf16[64,1152]{1,0:T(8,128)(2,1)S(1)}, bf16[64,1152]{1,0:T(8,128)(2,1)S(1)}, u32[]{:S(2)}, u32[]{:S(2)}) %collective-permute-start) | collective-permute-done | bytes 147488 | tf_op jit(solution)/shard_map/while/body/eval_jaxpr/ppermute | solution.py:11
  426.6 13.3 %collective-permute-done = bf16[64,1152]{1,0:T(8,128)(2,1)S(1)} collective-permute-done((bf16[64,1152]{1,0:T(8,128)(2,1)S(1)}, bf16[64,1152]{1,0:T(8,128)(2,1)S(1)}, u32[]{:S(2)}, u32[]{:S(2)}) %collective-permute-start) | collective-permute-done | bytes 147488 | tf_op jit(solution)/shard_map/while/body/eval_jaxpr/ppermute | solution.py:11
  442.6 12.4 %collective-permute-done = bf16[64,1152]{1,0:T(8,128)(2,1)S(1)} collective-permute-done((bf16[64,1152]{1,0:T(8,128)(2,1)S(1)}, bf16[64,1152]{1,0:T(8,128)(2,1)S(1)}, u32[]{:S(2)}, u32[]{:S(2)}) %collective-permute-start) | collective-permute-done | bytes 147488 | tf_op jit(solution)/shard_map/while/body/eval_jaxpr/ppermute | solution.py:11
  457.7 11.4 %collective-permute-done = bf16[64,1152]{1,0:T(8,128)(2,1)S(1)} collective-permute-done((bf16[64,1152]{1,0:T(8,128)(2,1)S(1)}, bf16[64,1152]{1,0:T(8,128)(2,1)S(1)}, u32[]{:S(2)}, u32[]{:S(2)}) %collective-permute-start) | collective-permute-done | bytes 147488 | tf_op jit(solution)/shard_map/while/body/eval_jaxpr/ppermute | solution.py:11
  485.4 10.7 collective-permute-done
  498.8 10.7 collective-permute-done
  512.2 11.4 %collective-permute-done = bf16[64,1152]{1,0:T(8,128)(2,1)S(1)} collective-permute-done((bf16[64,1152]{1,0:T(8,128)(2,1)S(1)}, bf16[64,1152]{1,0:T(8,128)(2,1)S(1)}, u32[]{:S(2)}, u32[]{:S(2)}) %collective-permute-start) | collective-permute-done | bytes 147488 | tf_op jit(solution)/shard_map/while/body/eval_jaxpr/ppermute | solution.py:11
  526.4 12.5 %collective-permute-done = bf16[64,1152]{1,0:T(8,128)(2,1)S(1)} collective-permute-done((bf16[64,1152]{1,0:T(8,128)(2,1)S(1)}, bf16[64,1152]{1,0:T(8,128)(2,1)S(1)}, u32[]{:S(2)}, u32[]{:S(2)}) %collective-permute-start) | collective-permute-done | bytes 147488 | tf_op jit(solution)/shard_map/while/body/eval_jaxpr/ppermute | solution.py:11
  541.6 13.6 %collective-permute-done = bf16[64,1152]{1,0:T(8,128)(2,1)S(1)} collective-permute-done((bf16[64,1152]{1,0:T(8,128)(2,1)S(1)}, bf16[64,1152]{1,0:T(8,128)(2,1)S(1)}, u32[]{:S(2)}, u32[]{:S(2)}) %collective-permute-start) | collective-permute-done | bytes 147488 | tf_op jit(solution)/shard_map/while/body/eval_jaxpr/ppermute | solution.py:11
  557.9 14.8 %collective-permute-done = bf16[64,1152]{1,0:T(8,128)(2,1)S(1)} collective-permute-done((bf16[64,1152]{1,0:T(8,128)(2,1)S(1)}, bf16[64,1152]{1,0:T(8,128)(2,1)S(1)}, u32[]{:S(2)}, u32[]{:S(2)}) %collective-permute-start) | collective-permute-done | bytes 147488 | tf_op jit(solution)/shard_map/while/body/eval_jaxpr/ppermute | solution.py:11
  575.4 14.9 %collective-permute-done = bf16[64,1152]{1,0:T(8,128)(2,1)S(1)} collective-permute-done((bf16[64,1152]{1,0:T(8,128)(2,1)S(1)}, bf16[64,1152]{1,0:T(8,128)(2,1)S(1)}, u32[]{:S(2)}, u32[]{:S(2)}) %collective-permute-start) | collective-permute-done | bytes 147488 | tf_op jit(solution)/shard_map/while/body/eval_jaxpr/ppermute | solution.py:11
  593.1 14.1 %collective-permute-done = bf16[64,1152]{1,0:T(8,128)(2,1)S(1)} collective-permute-done((bf16[64,1152]{1,0:T(8,128)(2,1)S(1)}, bf16[64,1152]{1,0:T(8,128)(2,1)S(1)}, u32[]{:S(2)}, u32[]{:S(2)}) %collective-permute-start) | collective-permute-done | bytes 147488 | tf_op jit(solution)/shard_map/while/body/eval_jaxpr/ppermute | solution.py:11
  610.0 13.2 %collective-permute-done = bf16[64,1152]{1,0:T(8,128)(2,1)S(1)} collective-permute-done((bf16[64,1152]{1,0:T(8,128)(2,1)S(1)}, bf16[64,1152]{1,0:T(8,128)(2,1)S(1)}, u32[]{:S(2)}, u32[]{:S(2)}) %collective-permute-start) | collective-permute-done | bytes 147488 | tf_op jit(solution)/shard_map/while/body/eval_jaxpr/ppermute | solution.py:11
  626.0 12.3 %collective-permute-done = bf16[64,1152]{1,0:T(8,128)(2,1)S(1)} collective-permute-done((bf16[64,1152]{1,0:T(8,128)(2,1)S(1)}, bf16[64,1152]{1,0:T(8,128)(2,1)S(1)}, u32[]{:S(2)}, u32[]{:S(2)}) %collective-permute-start) | collective-permute-done | bytes 147488 | tf_op jit(solution)/shard_map/while/body/eval_jaxpr/ppermute | solution.py:11
  641.1 11.4 %collective-permute-done = bf16[64,1152]{1,0:T(8,128)(2,1)S(1)} collective-permute-done((bf16[64,1152]{1,0:T(8,128)(2,1)S(1)}, bf16[64,1152]{1,0:T(8,128)(2,1)S(1)}, u32[]{:S(2)}, u32[]{:S(2)}) %collective-permute-start) | collective-permute-done | bytes 147488 | tf_op jit(solution)/shard_map/while/body/eval_jaxpr/ppermute | solution.py:11
  668.6 10.7 collective-permute-done
  695.5 11.5 %collective-permute-done = bf16[64,1152]{1,0:T(8,128)(2,1)S(1)} collective-permute-done((bf16[64,1152]{1,0:T(8,128)(2,1)S(1)}, bf16[64,1152]{1,0:T(8,128)(2,1)S(1)}, u32[]{:S(2)}, u32[]{:S(2)}) %collective-permute-start) | collective-permute-done | bytes 147488 | tf_op jit(solution)/shard_map/while/body/eval_jaxpr/ppermute | solution.py:11
  709.7 12.5 %collective-permute-done = bf16[64,1152]{1,0:T(8,128)(2,1)S(1)} collective-permute-done((bf16[64,1152]{1,0:T(8,128)(2,1)S(1)}, bf16[64,1152]{1,0:T(8,128)(2,1)S(1)}, u32[]{:S(2)}, u32[]{:S(2)}) %collective-permute-start) | collective-permute-done | bytes 147488 | tf_op jit(solution)/shard_map/while/body/eval_jaxpr/ppermute | solution.py:11
  725.0 13.6 %collective-permute-done = bf16[64,1152]{1,0:T(8,128)(2,1)S(1)} collective-permute-done((bf16[64,1152]{1,0:T(8,128)(2,1)S(1)}, bf16[64,1152]{1,0:T(8,128)(2,1)S(1)}, u32[]{:S(2)}, u32[]{:S(2)}) %collective-permute-start) | collective-permute-done | bytes 147488 | tf_op jit(solution)/shard_map/while/body/eval_jaxpr/ppermute | solution.py:11
  741.4 14.8 %collective-permute-done = bf16[64,1152]{1,0:T(8,128)(2,1)S(1)} collective-permute-done((bf16[64,1152]{1,0:T(8,128)(2,1)S(1)}, bf16[64,1152]{1,0:T(8,128)(2,1)S(1)}, u32[]{:S(2)}, u32[]{:S(2)}) %collective-permute-start) | collective-permute-done | bytes 147488 | tf_op jit(solution)/shard_map/while/body/eval_jaxpr/ppermute | solution.py:11
  758.9 14.9 %collective-permute-done = bf16[64,1152]{1,0:T(8,128)(2,1)S(1)} collective-permute-done((bf16[64,1152]{1,0:T(8,128)(2,1)S(1)}, bf16[64,1152]{1,0:T(8,128)(2,1)S(1)}, u32[]{:S(2)}, u32[]{:S(2)}) %collective-permute-start) | collective-permute-done | bytes 147488 | tf_op jit(solution)/shard_map/while/body/eval_jaxpr/ppermute | solution.py:11
  776.6 14.1 %collective-permute-done = bf16[64,1152]{1,0:T(8,128)(2,1)S(1)} collective-permute-done((bf16[64,1152]{1,0:T(8,128)(2,1)S(1)}, bf16[64,1152]{1,0:T(8,128)(2,1)S(1)}, u32[]{:S(2)}, u32[]{:S(2)}) %collective-permute-start) | collective-permute-done | bytes 147488 | tf_op jit(solution)/shard_map/while/body/eval_jaxpr/ppermute | solution.py:11
  793.4 13.2 %collective-permute-done = bf16[64,1152]{1,0:T(8,128)(2,1)S(1)} collective-permute-done((bf16[64,1152]{1,0:T(8,128)(2,1)S(1)}, bf16[64,1152]{1,0:T(8,128)(2,1)S(1)}, u32[]{:S(2)}, u32[]{:S(2)}) %collective-permute-start) | collective-permute-done | bytes 147488 | tf_op jit(solution)/shard_map/while/body/eval_jaxpr/ppermute | solution.py:11
  809.3 12.3 %collective-permute-done = bf16[64,1152]{1,0:T(8,128)(2,1)S(1)} collective-permute-done((bf16[64,1152]{1,0:T(8,128)(2,1)S(1)}, bf16[64,1152]{1,0:T(8,128)(2,1)S(1)}, u32[]{:S(2)}, u32[]{:S(2)}) %collective-permute-start) | collective-permute-done | bytes 147488 | tf_op jit(solution)/shard_map/while/body/eval_jaxpr/ppermute | solution.py:11
  824.3 11.3 %collective-permute-done = bf16[64,1152]{1,0:T(8,128)(2,1)S(1)} collective-permute-done((bf16[64,1152]{1,0:T(8,128)(2,1)S(1)}, bf16[64,1152]{1,0:T(8,128)(2,1)S(1)}, u32[]{:S(2)}, u32[]{:S(2)}) %collective-permute-start) | collective-permute-done | bytes 147488 | tf_op jit(solution)/shard_map/while/body/eval_jaxpr/ppermute | solution.py:11
  1003.7 90.4 %reduce-scatter.2.cloned.1.call-done = f32[64,1152]{1,0:T(8,128)} async-done(((f32[256,1152]{1,0:T(8,128)}), f32[64,1152]{1,0:T(8,128)}) %reduce-scatter.2.cloned.1.call-update) | async-done | bytes 294928 | tf_op jit(solution)/shard_map/reduce_scatter | solution.py:98
  (680 shorter events, 406.0 us)
Async XLA Ops:
  7.2 1087.0 %reduce-scatter.2.cloned.1.call-start = ((), (), s32[]{:S(2)}) async-start(), calls=%async_computation.1 | async-start | bytes 1474560 | tf_op jit(solution)/shard_map/reduce_scatter | solution.py:98
  22.6 17.3 %collective-permute-start.1 = (f32[64,1152]{1,0:T(8,128)S(1)}, f32[64,1152]{1,0:T(8,128)S(1)}, u32[]{:S(2)}, u32[]{:S(2)}) collective-permute-start(f32[64,1152]{1,0:T(8,128)S(1)} %convolution_add_fusion.4), channel_id=1, source_target_pairs={{0,1},{1,2},{2,3},{3,4},{4,5},{5,6},{6,7},{7,8},{8,9},{9,10},{10,1... | collective-permute-start | bytes 884744 | tf_op jit(solution)/shard_map/while/body/eval_jaxpr/ppermute | solution.py:11
  24.6 15.3 %collective-permute-start = (bf16[64,1152]{1,0:T(8,128)(2,1)S(1)}, bf16[64,1152]{1,0:T(8,128)(2,1)S(1)}, u32[]{:S(2)}, u32[]{:S(2)}) collective-permute-start(bf16[64,1152]{1,0:T(8,128)(2,1)S(1)} %copy.11), channel_id=1, source_target_pairs={{0,1},{1,2},{2,3},{3,4},{4,5},{5,6},{6,7},{7,8},{8,9},{9,10},{10,1... | collective-permute-start | bytes 442376 | tf_op jit(solution)/shard_map/while/body/eval_jaxpr/ppermute | solution.py:11
  41.9 14.9 %collective-permute-start.1 = (f32[64,1152]{1,0:T(8,128)S(1)}, f32[64,1152]{1,0:T(8,128)S(1)}, u32[]{:S(2)}, u32[]{:S(2)}) collective-permute-start(f32[64,1152]{1,0:T(8,128)S(1)} %convolution_add_fusion.4), channel_id=1, source_target_pairs={{0,1},{1,2},{2,3},{3,4},{4,5},{5,6},{6,7},{7,8},{8,9},{9,10},{10,1... | collective-permute-start | bytes 884744 | tf_op jit(solution)/shard_map/while/body/eval_jaxpr/ppermute | solution.py:11
  42.0 14.8 %collective-permute-start = (bf16[64,1152]{1,0:T(8,128)(2,1)S(1)}, bf16[64,1152]{1,0:T(8,128)(2,1)S(1)}, u32[]{:S(2)}, u32[]{:S(2)}) collective-permute-start(bf16[64,1152]{1,0:T(8,128)(2,1)S(1)} %copy.11), channel_id=1, source_target_pairs={{0,1},{1,2},{2,3},{3,4},{4,5},{5,6},{6,7},{7,8},{8,9},{9,10},{10,1... | collective-permute-start | bytes 442376 | tf_op jit(solution)/shard_map/while/body/eval_jaxpr/ppermute | solution.py:11
  58.9 14.0 %collective-permute-start.1 = (f32[64,1152]{1,0:T(8,128)S(1)}, f32[64,1152]{1,0:T(8,128)S(1)}, u32[]{:S(2)}, u32[]{:S(2)}) collective-permute-start(f32[64,1152]{1,0:T(8,128)S(1)} %convolution_add_fusion.4), channel_id=1, source_target_pairs={{0,1},{1,2},{2,3},{3,4},{4,5},{5,6},{6,7},{7,8},{8,9},{9,10},{10,1... | collective-permute-start | bytes 884744 | tf_op jit(solution)/shard_map/while/body/eval_jaxpr/ppermute | solution.py:11
  59.0 14.0 %collective-permute-start = (bf16[64,1152]{1,0:T(8,128)(2,1)S(1)}, bf16[64,1152]{1,0:T(8,128)(2,1)S(1)}, u32[]{:S(2)}, u32[]{:S(2)}) collective-permute-start(bf16[64,1152]{1,0:T(8,128)(2,1)S(1)} %copy.11), channel_id=1, source_target_pairs={{0,1},{1,2},{2,3},{3,4},{4,5},{5,6},{6,7},{7,8},{8,9},{9,10},{10,1... | collective-permute-start | bytes 442376 | tf_op jit(solution)/shard_map/while/body/eval_jaxpr/ppermute | solution.py:11
  174.0 14.2 %collective-permute-start.1 = (f32[64,1152]{1,0:T(8,128)S(1)}, f32[64,1152]{1,0:T(8,128)S(1)}, u32[]{:S(2)}, u32[]{:S(2)}) collective-permute-start(f32[64,1152]{1,0:T(8,128)S(1)} %convolution_add_fusion.4), channel_id=1, source_target_pairs={{0,1},{1,2},{2,3},{3,4},{4,5},{5,6},{6,7},{7,8},{8,9},{9,10},{10,1... | collective-permute-start | bytes 884744 | tf_op jit(solution)/shard_map/while/body/eval_jaxpr/ppermute | solution.py:11
  174.0 14.2 %collective-permute-start = (bf16[64,1152]{1,0:T(8,128)(2,1)S(1)}, bf16[64,1152]{1,0:T(8,128)(2,1)S(1)}, u32[]{:S(2)}, u32[]{:S(2)}) collective-permute-start(bf16[64,1152]{1,0:T(8,128)(2,1)S(1)} %copy.11), channel_id=1, source_target_pairs={{0,1},{1,2},{2,3},{3,4},{4,5},{5,6},{6,7},{7,8},{8,9},{9,10},{10,1... | collective-permute-start | bytes 442376 | tf_op jit(solution)/shard_map/while/body/eval_jaxpr/ppermute | solution.py:11
  190.2 15.4 %collective-permute-start.1 = (f32[64,1152]{1,0:T(8,128)S(1)}, f32[64,1152]{1,0:T(8,128)S(1)}, u32[]{:S(2)}, u32[]{:S(2)}) collective-permute-start(f32[64,1152]{1,0:T(8,128)S(1)} %convolution_add_fusion.4), channel_id=1, source_target_pairs={{0,1},{1,2},{2,3},{3,4},{4,5},{5,6},{6,7},{7,8},{8,9},{9,10},{10,1... | collective-permute-start | bytes 884744 | tf_op jit(solution)/shard_map/while/body/eval_jaxpr/ppermute | solution.py:11
  190.3 15.3 %collective-permute-start = (bf16[64,1152]{1,0:T(8,128)(2,1)S(1)}, bf16[64,1152]{1,0:T(8,128)(2,1)S(1)}, u32[]{:S(2)}, u32[]{:S(2)}) collective-permute-start(bf16[64,1152]{1,0:T(8,128)(2,1)S(1)} %copy.11), channel_id=1, source_target_pairs={{0,1},{1,2},{2,3},{3,4},{4,5},{5,6},{6,7},{7,8},{8,9},{9,10},{10,1... | collective-permute-start | bytes 442376 | tf_op jit(solution)/shard_map/while/body/eval_jaxpr/ppermute | solution.py:11
  207.7 15.7 %collective-permute-start.1 = (f32[64,1152]{1,0:T(8,128)S(1)}, f32[64,1152]{1,0:T(8,128)S(1)}, u32[]{:S(2)}, u32[]{:S(2)}) collective-permute-start(f32[64,1152]{1,0:T(8,128)S(1)} %convolution_add_fusion.4), channel_id=1, source_target_pairs={{0,1},{1,2},{2,3},{3,4},{4,5},{5,6},{6,7},{7,8},{8,9},{9,10},{10,1... | collective-permute-start | bytes 884744 | tf_op jit(solution)/shard_map/while/body/eval_jaxpr/ppermute | solution.py:11
  207.8 15.6 %collective-permute-start = (bf16[64,1152]{1,0:T(8,128)(2,1)S(1)}, bf16[64,1152]{1,0:T(8,128)(2,1)S(1)}, u32[]{:S(2)}, u32[]{:S(2)}) collective-permute-start(bf16[64,1152]{1,0:T(8,128)(2,1)S(1)} %copy.11), channel_id=1, source_target_pairs={{0,1},{1,2},{2,3},{3,4},{4,5},{5,6},{6,7},{7,8},{8,9},{9,10},{10,1... | collective-permute-start | bytes 442376 | tf_op jit(solution)/shard_map/while/body/eval_jaxpr/ppermute | solution.py:11
  225.4 14.9 %collective-permute-start.1 = (f32[64,1152]{1,0:T(8,128)S(1)}, f32[64,1152]{1,0:T(8,128)S(1)}, u32[]{:S(2)}, u32[]{:S(2)}) collective-permute-start(f32[64,1152]{1,0:T(8,128)S(1)} %convolution_add_fusion.4), channel_id=1, source_target_pairs={{0,1},{1,2},{2,3},{3,4},{4,5},{5,6},{6,7},{7,8},{8,9},{9,10},{10,1... | collective-permute-start | bytes 884744 | tf_op jit(solution)/shard_map/while/body/eval_jaxpr/ppermute | solution.py:11
  225.5 14.8 %collective-permute-start = (bf16[64,1152]{1,0:T(8,128)(2,1)S(1)}, bf16[64,1152]{1,0:T(8,128)(2,1)S(1)}, u32[]{:S(2)}, u32[]{:S(2)}) collective-permute-start(bf16[64,1152]{1,0:T(8,128)(2,1)S(1)} %copy.11), channel_id=1, source_target_pairs={{0,1},{1,2},{2,3},{3,4},{4,5},{5,6},{6,7},{7,8},{8,9},{9,10},{10,1... | collective-permute-start | bytes 442376 | tf_op jit(solution)/shard_map/while/body/eval_jaxpr/ppermute | solution.py:11
  242.4 14.0 %collective-permute-start.1 = (f32[64,1152]{1,0:T(8,128)S(1)}, f32[64,1152]{1,0:T(8,128)S(1)}, u32[]{:S(2)}, u32[]{:S(2)}) collective-permute-start(f32[64,1152]{1,0:T(8,128)S(1)} %convolution_add_fusion.4), channel_id=1, source_target_pairs={{0,1},{1,2},{2,3},{3,4},{4,5},{5,6},{6,7},{7,8},{8,9},{9,10},{10,1... | collective-permute-start | bytes 884744 | tf_op jit(solution)/shard_map/while/body/eval_jaxpr/ppermute | solution.py:11
  242.5 13.9 %collective-permute-start = (bf16[64,1152]{1,0:T(8,128)(2,1)S(1)}, bf16[64,1152]{1,0:T(8,128)(2,1)S(1)}, u32[]{:S(2)}, u32[]{:S(2)}) collective-permute-start(bf16[64,1152]{1,0:T(8,128)(2,1)S(1)} %copy.11), channel_id=1, source_target_pairs={{0,1},{1,2},{2,3},{3,4},{4,5},{5,6},{6,7},{7,8},{8,9},{9,10},{10,1... | collective-permute-start | bytes 442376 | tf_op jit(solution)/shard_map/while/body/eval_jaxpr/ppermute | solution.py:11
  357.4 14.3 %collective-permute-start.1 = (f32[64,1152]{1,0:T(8,128)S(1)}, f32[64,1152]{1,0:T(8,128)S(1)}, u32[]{:S(2)}, u32[]{:S(2)}) collective-permute-start(f32[64,1152]{1,0:T(8,128)S(1)} %convolution_add_fusion.4), channel_id=1, source_target_pairs={{0,1},{1,2},{2,3},{3,4},{4,5},{5,6},{6,7},{7,8},{8,9},{9,10},{10,1... | collective-permute-start | bytes 884744 | tf_op jit(solution)/shard_map/while/body/eval_jaxpr/ppermute | solution.py:11
  357.5 14.2 %collective-permute-start = (bf16[64,1152]{1,0:T(8,128)(2,1)S(1)}, bf16[64,1152]{1,0:T(8,128)(2,1)S(1)}, u32[]{:S(2)}, u32[]{:S(2)}) collective-permute-start(bf16[64,1152]{1,0:T(8,128)(2,1)S(1)} %copy.11), channel_id=1, source_target_pairs={{0,1},{1,2},{2,3},{3,4},{4,5},{5,6},{6,7},{7,8},{8,9},{9,10},{10,1... | collective-permute-start | bytes 442376 | tf_op jit(solution)/shard_map/while/body/eval_jaxpr/ppermute | solution.py:11
  373.7 15.4 %collective-permute-start.1 = (f32[64,1152]{1,0:T(8,128)S(1)}, f32[64,1152]{1,0:T(8,128)S(1)}, u32[]{:S(2)}, u32[]{:S(2)}) collective-permute-start(f32[64,1152]{1,0:T(8,128)S(1)} %convolution_add_fusion.4), channel_id=1, source_target_pairs={{0,1},{1,2},{2,3},{3,4},{4,5},{5,6},{6,7},{7,8},{8,9},{9,10},{10,1... | collective-permute-start | bytes 884744 | tf_op jit(solution)/shard_map/while/body/eval_jaxpr/ppermute | solution.py:11
  373.8 15.4 %collective-permute-start = (bf16[64,1152]{1,0:T(8,128)(2,1)S(1)}, bf16[64,1152]{1,0:T(8,128)(2,1)S(1)}, u32[]{:S(2)}, u32[]{:S(2)}) collective-permute-start(bf16[64,1152]{1,0:T(8,128)(2,1)S(1)} %copy.11), channel_id=1, source_target_pairs={{0,1},{1,2},{2,3},{3,4},{4,5},{5,6},{6,7},{7,8},{8,9},{9,10},{10,1... | collective-permute-start | bytes 442376 | tf_op jit(solution)/shard_map/while/body/eval_jaxpr/ppermute | solution.py:11
  391.2 15.7 %collective-permute-start.1 = (f32[64,1152]{1,0:T(8,128)S(1)}, f32[64,1152]{1,0:T(8,128)S(1)}, u32[]{:S(2)}, u32[]{:S(2)}) collective-permute-start(f32[64,1152]{1,0:T(8,128)S(1)} %convolution_add_fusion.4), channel_id=1, source_target_pairs={{0,1},{1,2},{2,3},{3,4},{4,5},{5,6},{6,7},{7,8},{8,9},{9,10},{10,1... | collective-permute-start | bytes 884744 | tf_op jit(solution)/shard_map/while/body/eval_jaxpr/ppermute | solution.py:11
  391.3 15.6 %collective-permute-start = (bf16[64,1152]{1,0:T(8,128)(2,1)S(1)}, bf16[64,1152]{1,0:T(8,128)(2,1)S(1)}, u32[]{:S(2)}, u32[]{:S(2)}) collective-permute-start(bf16[64,1152]{1,0:T(8,128)(2,1)S(1)} %copy.11), channel_id=1, source_target_pairs={{0,1},{1,2},{2,3},{3,4},{4,5},{5,6},{6,7},{7,8},{8,9},{9,10},{10,1... | collective-permute-start | bytes 442376 | tf_op jit(solution)/shard_map/while/body/eval_jaxpr/ppermute | solution.py:11
  408.9 14.9 %collective-permute-start.1 = (f32[64,1152]{1,0:T(8,128)S(1)}, f32[64,1152]{1,0:T(8,128)S(1)}, u32[]{:S(2)}, u32[]{:S(2)}) collective-permute-start(f32[64,1152]{1,0:T(8,128)S(1)} %convolution_add_fusion.4), channel_id=1, source_target_pairs={{0,1},{1,2},{2,3},{3,4},{4,5},{5,6},{6,7},{7,8},{8,9},{9,10},{10,1... | collective-permute-start | bytes 884744 | tf_op jit(solution)/shard_map/while/body/eval_jaxpr/ppermute | solution.py:11
  409.0 14.8 %collective-permute-start = (bf16[64,1152]{1,0:T(8,128)(2,1)S(1)}, bf16[64,1152]{1,0:T(8,128)(2,1)S(1)}, u32[]{:S(2)}, u32[]{:S(2)}) collective-permute-start(bf16[64,1152]{1,0:T(8,128)(2,1)S(1)} %copy.11), channel_id=1, source_target_pairs={{0,1},{1,2},{2,3},{3,4},{4,5},{5,6},{6,7},{7,8},{8,9},{9,10},{10,1... | collective-permute-start | bytes 442376 | tf_op jit(solution)/shard_map/while/body/eval_jaxpr/ppermute | solution.py:11
  425.9 14.0 %collective-permute-start.1 = (f32[64,1152]{1,0:T(8,128)S(1)}, f32[64,1152]{1,0:T(8,128)S(1)}, u32[]{:S(2)}, u32[]{:S(2)}) collective-permute-start(f32[64,1152]{1,0:T(8,128)S(1)} %convolution_add_fusion.4), channel_id=1, source_target_pairs={{0,1},{1,2},{2,3},{3,4},{4,5},{5,6},{6,7},{7,8},{8,9},{9,10},{10,1... | collective-permute-start | bytes 884744 | tf_op jit(solution)/shard_map/while/body/eval_jaxpr/ppermute | solution.py:11
  426.0 13.9 %collective-permute-start = (bf16[64,1152]{1,0:T(8,128)(2,1)S(1)}, bf16[64,1152]{1,0:T(8,128)(2,1)S(1)}, u32[]{:S(2)}, u32[]{:S(2)}) collective-permute-start(bf16[64,1152]{1,0:T(8,128)(2,1)S(1)} %copy.11), channel_id=1, source_target_pairs={{0,1},{1,2},{2,3},{3,4},{4,5},{5,6},{6,7},{7,8},{8,9},{9,10},{10,1... | collective-permute-start | bytes 442376 | tf_op jit(solution)/shard_map/while/body/eval_jaxpr/ppermute | solution.py:11
  540.9 14.3 %collective-permute-start.1 = (f32[64,1152]{1,0:T(8,128)S(1)}, f32[64,1152]{1,0:T(8,128)S(1)}, u32[]{:S(2)}, u32[]{:S(2)}) collective-permute-start(f32[64,1152]{1,0:T(8,128)S(1)} %convolution_add_fusion.4), channel_id=1, source_target_pairs={{0,1},{1,2},{2,3},{3,4},{4,5},{5,6},{6,7},{7,8},{8,9},{9,10},{10,1... | collective-permute-start | bytes 884744 | tf_op jit(solution)/shard_map/while/body/eval_jaxpr/ppermute | solution.py:11
  541.0 14.2 %collective-permute-start = (bf16[64,1152]{1,0:T(8,128)(2,1)S(1)}, bf16[64,1152]{1,0:T(8,128)(2,1)S(1)}, u32[]{:S(2)}, u32[]{:S(2)}) collective-permute-start(bf16[64,1152]{1,0:T(8,128)(2,1)S(1)} %copy.11), channel_id=1, source_target_pairs={{0,1},{1,2},{2,3},{3,4},{4,5},{5,6},{6,7},{7,8},{8,9},{9,10},{10,1... | collective-permute-start | bytes 442376 | tf_op jit(solution)/shard_map/while/body/eval_jaxpr/ppermute | solution.py:11
  557.2 15.5 %collective-permute-start.1 = (f32[64,1152]{1,0:T(8,128)S(1)}, f32[64,1152]{1,0:T(8,128)S(1)}, u32[]{:S(2)}, u32[]{:S(2)}) collective-permute-start(f32[64,1152]{1,0:T(8,128)S(1)} %convolution_add_fusion.4), channel_id=1, source_target_pairs={{0,1},{1,2},{2,3},{3,4},{4,5},{5,6},{6,7},{7,8},{8,9},{9,10},{10,1... | collective-permute-start | bytes 884744 | tf_op jit(solution)/shard_map/while/body/eval_jaxpr/ppermute | solution.py:11
  557.3 15.4 %collective-permute-start = (bf16[64,1152]{1,0:T(8,128)(2,1)S(1)}, bf16[64,1152]{1,0:T(8,128)(2,1)S(1)}, u32[]{:S(2)}, u32[]{:S(2)}) collective-permute-start(bf16[64,1152]{1,0:T(8,128)(2,1)S(1)} %copy.11), channel_id=1, source_target_pairs={{0,1},{1,2},{2,3},{3,4},{4,5},{5,6},{6,7},{7,8},{8,9},{9,10},{10,1... | collective-permute-start | bytes 442376 | tf_op jit(solution)/shard_map/while/body/eval_jaxpr/ppermute | solution.py:11
  574.7 15.6 %collective-permute-start.1 = (f32[64,1152]{1,0:T(8,128)S(1)}, f32[64,1152]{1,0:T(8,128)S(1)}, u32[]{:S(2)}, u32[]{:S(2)}) collective-permute-start(f32[64,1152]{1,0:T(8,128)S(1)} %convolution_add_fusion.4), channel_id=1, source_target_pairs={{0,1},{1,2},{2,3},{3,4},{4,5},{5,6},{6,7},{7,8},{8,9},{9,10},{10,1... | collective-permute-start | bytes 884744 | tf_op jit(solution)/shard_map/while/body/eval_jaxpr/ppermute | solution.py:11
  574.8 15.5 %collective-permute-start = (bf16[64,1152]{1,0:T(8,128)(2,1)S(1)}, bf16[64,1152]{1,0:T(8,128)(2,1)S(1)}, u32[]{:S(2)}, u32[]{:S(2)}) collective-permute-start(bf16[64,1152]{1,0:T(8,128)(2,1)S(1)} %copy.11), channel_id=1, source_target_pairs={{0,1},{1,2},{2,3},{3,4},{4,5},{5,6},{6,7},{7,8},{8,9},{9,10},{10,1... | collective-permute-start | bytes 442376 | tf_op jit(solution)/shard_map/while/body/eval_jaxpr/ppermute | solution.py:11
  592.4 14.9 %collective-permute-start.1 = (f32[64,1152]{1,0:T(8,128)S(1)}, f32[64,1152]{1,0:T(8,128)S(1)}, u32[]{:S(2)}, u32[]{:S(2)}) collective-permute-start(f32[64,1152]{1,0:T(8,128)S(1)} %convolution_add_fusion.4), channel_id=1, source_target_pairs={{0,1},{1,2},{2,3},{3,4},{4,5},{5,6},{6,7},{7,8},{8,9},{9,10},{10,1... | collective-permute-start | bytes 884744 | tf_op jit(solution)/shard_map/while/body/eval_jaxpr/ppermute | solution.py:11
  592.5 14.8 %collective-permute-start = (bf16[64,1152]{1,0:T(8,128)(2,1)S(1)}, bf16[64,1152]{1,0:T(8,128)(2,1)S(1)}, u32[]{:S(2)}, u32[]{:S(2)}) collective-permute-start(bf16[64,1152]{1,0:T(8,128)(2,1)S(1)} %copy.11), channel_id=1, source_target_pairs={{0,1},{1,2},{2,3},{3,4},{4,5},{5,6},{6,7},{7,8},{8,9},{9,10},{10,1... | collective-permute-start | bytes 442376 | tf_op jit(solution)/shard_map/while/body/eval_jaxpr/ppermute | solution.py:11
  609.3 14.0 %collective-permute-start.1 = (f32[64,1152]{1,0:T(8,128)S(1)}, f32[64,1152]{1,0:T(8,128)S(1)}, u32[]{:S(2)}, u32[]{:S(2)}) collective-permute-start(f32[64,1152]{1,0:T(8,128)S(1)} %convolution_add_fusion.4), channel_id=1, source_target_pairs={{0,1},{1,2},{2,3},{3,4},{4,5},{5,6},{6,7},{7,8},{8,9},{9,10},{10,1... | collective-permute-start | bytes 884744 | tf_op jit(solution)/shard_map/while/body/eval_jaxpr/ppermute | solution.py:11
  724.3 14.3 %collective-permute-start.1 = (f32[64,1152]{1,0:T(8,128)S(1)}, f32[64,1152]{1,0:T(8,128)S(1)}, u32[]{:S(2)}, u32[]{:S(2)}) collective-permute-start(f32[64,1152]{1,0:T(8,128)S(1)} %convolution_add_fusion.4), channel_id=1, source_target_pairs={{0,1},{1,2},{2,3},{3,4},{4,5},{5,6},{6,7},{7,8},{8,9},{9,10},{10,1... | collective-permute-start | bytes 884744 | tf_op jit(solution)/shard_map/while/body/eval_jaxpr/ppermute | solution.py:11
  724.4 14.2 %collective-permute-start = (bf16[64,1152]{1,0:T(8,128)(2,1)S(1)}, bf16[64,1152]{1,0:T(8,128)(2,1)S(1)}, u32[]{:S(2)}, u32[]{:S(2)}) collective-permute-start(bf16[64,1152]{1,0:T(8,128)(2,1)S(1)} %copy.11), channel_id=1, source_target_pairs={{0,1},{1,2},{2,3},{3,4},{4,5},{5,6},{6,7},{7,8},{8,9},{9,10},{10,1... | collective-permute-start | bytes 442376 | tf_op jit(solution)/shard_map/while/body/eval_jaxpr/ppermute | solution.py:11
  740.6 15.5 %collective-permute-start.1 = (f32[64,1152]{1,0:T(8,128)S(1)}, f32[64,1152]{1,0:T(8,128)S(1)}, u32[]{:S(2)}, u32[]{:S(2)}) collective-permute-start(f32[64,1152]{1,0:T(8,128)S(1)} %convolution_add_fusion.4), channel_id=1, source_target_pairs={{0,1},{1,2},{2,3},{3,4},{4,5},{5,6},{6,7},{7,8},{8,9},{9,10},{10,1... | collective-permute-start | bytes 884744 | tf_op jit(solution)/shard_map/while/body/eval_jaxpr/ppermute | solution.py:11
  740.7 15.4 %collective-permute-start = (bf16[64,1152]{1,0:T(8,128)(2,1)S(1)}, bf16[64,1152]{1,0:T(8,128)(2,1)S(1)}, u32[]{:S(2)}, u32[]{:S(2)}) collective-permute-start(bf16[64,1152]{1,0:T(8,128)(2,1)S(1)} %copy.11), channel_id=1, source_target_pairs={{0,1},{1,2},{2,3},{3,4},{4,5},{5,6},{6,7},{7,8},{8,9},{9,10},{10,1... | collective-permute-start | bytes 442376 | tf_op jit(solution)/shard_map/while/body/eval_jaxpr/ppermute | solution.py:11
  758.2 15.6 %collective-permute-start.1 = (f32[64,1152]{1,0:T(8,128)S(1)}, f32[64,1152]{1,0:T(8,128)S(1)}, u32[]{:S(2)}, u32[]{:S(2)}) collective-permute-start(f32[64,1152]{1,0:T(8,128)S(1)} %convolution_add_fusion.4), channel_id=1, source_target_pairs={{0,1},{1,2},{2,3},{3,4},{4,5},{5,6},{6,7},{7,8},{8,9},{9,10},{10,1... | collective-permute-start | bytes 884744 | tf_op jit(solution)/shard_map/while/body/eval_jaxpr/ppermute | solution.py:11
  758.3 15.5 %collective-permute-start = (bf16[64,1152]{1,0:T(8,128)(2,1)S(1)}, bf16[64,1152]{1,0:T(8,128)(2,1)S(1)}, u32[]{:S(2)}, u32[]{:S(2)}) collective-permute-start(bf16[64,1152]{1,0:T(8,128)(2,1)S(1)} %copy.11), channel_id=1, source_target_pairs={{0,1},{1,2},{2,3},{3,4},{4,5},{5,6},{6,7},{7,8},{8,9},{9,10},{10,1... | collective-permute-start | bytes 442376 | tf_op jit(solution)/shard_map/while/body/eval_jaxpr/ppermute | solution.py:11
  775.8 14.8 %collective-permute-start.1 = (f32[64,1152]{1,0:T(8,128)S(1)}, f32[64,1152]{1,0:T(8,128)S(1)}, u32[]{:S(2)}, u32[]{:S(2)}) collective-permute-start(f32[64,1152]{1,0:T(8,128)S(1)} %convolution_add_fusion.4), channel_id=1, source_target_pairs={{0,1},{1,2},{2,3},{3,4},{4,5},{5,6},{6,7},{7,8},{8,9},{9,10},{10,1... | collective-permute-start | bytes 884744 | tf_op jit(solution)/shard_map/while/body/eval_jaxpr/ppermute | solution.py:11
  775.9 14.7 %collective-permute-start = (bf16[64,1152]{1,0:T(8,128)(2,1)S(1)}, bf16[64,1152]{1,0:T(8,128)(2,1)S(1)}, u32[]{:S(2)}, u32[]{:S(2)}) collective-permute-start(bf16[64,1152]{1,0:T(8,128)(2,1)S(1)} %copy.11), channel_id=1, source_target_pairs={{0,1},{1,2},{2,3},{3,4},{4,5},{5,6},{6,7},{7,8},{8,9},{9,10},{10,1... | collective-permute-start | bytes 442376 | tf_op jit(solution)/shard_map/while/body/eval_jaxpr/ppermute | solution.py:11
  792.7 13.9 %collective-permute-start.1 = (f32[64,1152]{1,0:T(8,128)S(1)}, f32[64,1152]{1,0:T(8,128)S(1)}, u32[]{:S(2)}, u32[]{:S(2)}) collective-permute-start(f32[64,1152]{1,0:T(8,128)S(1)} %convolution_add_fusion.4), channel_id=1, source_target_pairs={{0,1},{1,2},{2,3},{3,4},{4,5},{5,6},{6,7},{7,8},{8,9},{9,10},{10,1... | collective-permute-start | bytes 884744 | tf_op jit(solution)/shard_map/while/body/eval_jaxpr/ppermute | solution.py:11
  951.9 16.1 %collective-permute-start.1 = (f32[64,1152]{1,0:T(8,128)S(1)}, f32[64,1152]{1,0:T(8,128)S(1)}, u32[]{:S(2)}, u32[]{:S(2)}) collective-permute-start(f32[64,1152]{1,0:T(8,128)S(1)} %convolution_add_fusion.4), channel_id=1, source_target_pairs={{0,1},{1,2},{2,3},{3,4},{4,5},{5,6},{6,7},{7,8},{8,9},{9,10},{10,1... | collective-permute-start | bytes 884744 | tf_op jit(solution)/shard_map/while/body/eval_jaxpr/ppermute | solution.py:11
  970.0 15.3 %collective-permute-start.1 = (f32[64,1152]{1,0:T(8,128)S(1)}, f32[64,1152]{1,0:T(8,128)S(1)}, u32[]{:S(2)}, u32[]{:S(2)}) collective-permute-start(f32[64,1152]{1,0:T(8,128)S(1)} %convolution_add_fusion.4), channel_id=1, source_target_pairs={{0,1},{1,2},{2,3},{3,4},{4,5},{5,6},{6,7},{7,8},{8,9},{9,10},{10,1... | collective-permute-start | bytes 884744 | tf_op jit(solution)/shard_map/while/body/eval_jaxpr/ppermute | solution.py:11
  987.3 14.3 %collective-permute-start.1 = (f32[64,1152]{1,0:T(8,128)S(1)}, f32[64,1152]{1,0:T(8,128)S(1)}, u32[]{:S(2)}, u32[]{:S(2)}) collective-permute-start(f32[64,1152]{1,0:T(8,128)S(1)} %convolution_add_fusion.4), channel_id=1, source_target_pairs={{0,1},{1,2},{2,3},{3,4},{4,5},{5,6},{6,7},{7,8},{8,9},{9,10},{10,1... | collective-permute-start | bytes 884744 | tf_op jit(solution)/shard_map/while/body/eval_jaxpr/ppermute | solution.py:11
  (84 other events, 1052.9 us)
Sparse Core Ops, SparseCore 0:
  1002.8 91.3 reduce-scatter.1
where the time goes:
time: 1110 us; the launch traced here: 1100 us
  waiting for transfers between devices  802 us (72%)
  matrix products  152 us (14%)
  starting transfers between devices  104 us (9%)
  between operations  14.1 us (1%)
  other arithmetic  12.9 us (1%)
    ppermute x128, waiting for transfers between devices, from_behind(): lax.ppermute(array, axis, [(i, (i + by) % devices) for i in range(devices)])  712 us
    dot_general x64, matrix products, pair_grads(): lax.dot_general(text_block, image_low, (((1,), (1,)), ((), ())), preferre...  104 us
    ppermute x128, starting transfers between devices, from_behind(): lax.ppermute(array, axis, [(i, (i + by) % devices) for i in range(devices)])  104 us
    reduce_scatter x1, waiting for transfers between devices, body(): lax.psum_scatter(image_sum, 'group', scatter_dimension=0, tiled=True)  90.4 us
    dot_general x64, matrix products, pair_grads(): lax.dot_general(weights_tile, text_block, (((0,), (0,)), ((), ())), prefe...  33.3 us
  transfers between devices with their start and end apart: 129, of which 65 were waited for; matrix products, arithmetic and copies ran while one was open for 3% of the time, Pallas kernels for 0%

commit v1 on v0

v1 whole, which is shorter than its diff:
```python
import jax
import jax.numpy as jnp
import numpy as np
from jax import lax
from jax.sharding import PartitionSpec as P

epsilon = 1e-06

SHAPE = (2, 2, 4, 2, 8)
AXES = ("group", "blk")
SHRINK = 0.25


def neighbour_pairs(axis, phase):
    perm = []
    for i, (xh, core, y, xl, z) in enumerate(np.ndindex(*SHAPE)):
        at = {"x": 2 * xh + xl, "y": y, "z": z}
        n = {"x": 4, "y": 4, "z": 8}[axis]
        p = at[axis]
        if (phase + core) % 2 == 0:
            at[axis] = p ^ 1
        else:
            at[axis] = (p + 1) % n if p % 2 else (p - 1) % n
        there = (at["x"] // 2, core, at["y"], at["x"] % 2, at["z"])
        perm.append((i, int(np.ravel_multi_index(there, SHAPE))))
    return perm


PX, PY, PZ = ([neighbour_pairs(axis, 0), neighbour_pairs(axis, 1)] for axis in "xyz")
PC = [(i, i ^ 64) for i in range(256)]


def swap(array, perm):
    return lax.ppermute(array, AXES, perm)


def join(*arrays):
    return jnp.concatenate(arrays, axis=0)


def normalize(embedding):
    values = embedding.astype(jnp.float32)
    inverse = lax.rsqrt(jnp.sum(values * values, axis=-1, keepdims=True) + epsilon)
    return (values * inverse, inverse)


def unit_grad(unit_vec, inverse, grad_sum):
    return (grad_sum - unit_vec * jnp.sum(unit_vec * grad_sum, axis=-1, keepdims=True)) * inverse


def gather_doubling(own, perms):
    held = own
    for perm in perms:
        held = join(held, swap(held, perm))
    return held


def gather_z(own):
    first = join(own, swap(own, PZ[0]))
    second = swap(first, PZ[1])
    third = swap(second, PZ[0])
    fourth = swap(third, PZ[1])
    return join(first, second, third, fourth)


def send_sum(part, perm):
    return swap((part * SHRINK).astype(jnp.float16), perm).astype(jnp.float32) * (1 / SHRINK)


def scatter_doubling(total, perms):
    for perm in reversed(perms):
        n = total.shape[0] // 2
        total = total[:n] + send_sum(total[n:], perm)
    return total


def scatter_z(total):
    n = total.shape[0] // 4
    first, second, third, fourth = (total[i * n : (i + 1) * n] for i in range(4))
    third = third + send_sum(fourth, PZ[1])
    second = second + send_sum(third, PZ[0])
    first = first + send_sum(second, PZ[1])
    return first[: n // 2] + send_sum(first[n // 2 :], PZ[0])


def body(images, texts, logit_scale, bias):
    image_unit, image_inv = normalize(images)
    text_unit, text_inv = normalize(texts)
    image_low = image_unit.astype(jnp.bfloat16)
    text_low = text_unit.astype(jnp.bfloat16)
    factor = logit_scale[0]
    offset = bias[0]
    rows = images.shape[0]
    half = rows // 2
    images_a = gather_doubling(image_low[:half], PX + PY)
    images_b = gather_doubling(image_low[half:], PY + PX)
    texts_core = gather_z(text_low)
    texts_other = swap(texts_core, PC)
    image_all = join(images_a, images_b)
    text_all = join(texts_core, texts_other)
    logits = (
        factor
        * lax.dot_general(
            text_all, image_all, (((1,), (1,)), ((), ())), preferred_element_type=jnp.float32
        )
        + offset
    )
    n = image_all.shape[0]
    row = lax.broadcasted_iota(jnp.int32, (n, n), 0)
    col = lax.broadcasted_iota(jnp.int32, (n, n), 1)
    image_id = jnp.where(
        col < half, col, jnp.where((col >= n // 2) & (col < n // 2 + half), col - n // 2 + half, n)
    )
    positive = (row == image_id).astype(jnp.float32)
    weights = (factor * (jax.nn.sigmoid(logits) - positive)).astype(jnp.bfloat16)
    text_sum = jnp.dot(weights, image_all, preferred_element_type=jnp.float32)
    image_sum = lax.dot_general(
        weights, text_all, (((0,), (0,)), ((), ())), preferred_element_type=jnp.float32
    )
    image_own = join(
        scatter_doubling(image_sum[: n // 2], PX + PY), scatter_doubling(image_sum[n // 2 :], PY + PX)
    )
    text_core = text_sum[: n // 2] + swap(text_sum[n // 2 :], PC)
    text_own = scatter_z(text_core)
    return (unit_grad(image_unit, image_inv, image_own), unit_grad(text_unit, text_inv, text_own))


def solution(mesh):
    return jax.shard_map(
        body,
        mesh=mesh,
        in_specs=(P(("group", "blk"), None), P(("group", "blk"), None), P(), P()),
        out_specs=(P(("group", "blk"), None), P(("group", "blk"), None)),
        check_vma=False,
    )
```

time: 1110 us -> 134 us (0.12)
  waiting for transfers between devices: 802 us -> 70.3 us
  matrix products: 152 us -> 10 us
  starting transfers between devices: 104 us -> 42.5 us
  between operations: 14.1 us -> 2.34 us
    ppermute x128 -> x26, waiting for transfers between devices: 712 us -> 70.3 us  [swap(): return lax.ppermute(array, AXES, perm)]
    dot_general x192 -> x3, matrix products: 152 us -> 10 us  [the longest x1 4.1 us: body(): lax.dot_general(text_all, image_all, (((1,), (1,)), ((), ())), preferred_...]
    reduce_scatter x1 -> x0, waiting for transfers between devices: 90.4 us -> none  [body(): lax.psum_scatter(image_sum, 'group', scatter_dimension=0, tiled=True)]
    ppermute x128 -> x26, starting transfers between devices: 104 us -> 42.5 us  [swap(): return lax.ppermute(array, AXES, perm)]
  transfers between devices with their start and end apart: 129 -> 26, of which waited for: 65 -> 14; matrix products, arithmetic and copies ran while one was open for 3% -> 6% of each run, Pallas kernels for 0% -> 0%
where the time goes in v1:
time: 134 us
  waiting for transfers between devices  70.3 us (52%)
  starting transfers between devices  42.5 us (32%)
  matrix products  10 us (7%)
  other arithmetic  8 us (6%)
  between operations  2.34 us (2%)
    ppermute x26, waiting for transfers between devices, swap(): return lax.ppermute(array, AXES, perm)  70.3 us
    ppermute x26, starting transfers between devices, swap(): return lax.ppermute(array, AXES, perm)  42.5 us
    dot_general x1, matrix products, body(): lax.dot_general(text_all, image_all, (((1,), (1,)), ((), ())), preferred_...  4.1 us
    dot_general x1, matrix products, body(): lax.dot_general(weights, text_all, (((0,), (0,)), ((), ())), preferred_el...  3.06 us
    dot_general x1, matrix products, body(): text_sum = jnp.dot(weights, image_all, preferred_element_type=jnp.float32)  2.87 us
  transfers between devices with their start and end apart: 26, of which 14 were waited for; matrix products, arithmetic and copies ran while one was open for 6% of the time, Pallas kernels for 0%

profile of v1, /device:TPU:24, one launch (start us, length us, event | category | flops | bytes accessed | tf_op | source)
XLA Modules:
  0.0 134.1 jit_solution(7454178228547193148)
XLA Ops:
  0.6 1.0 fusion.18
  1.7 1.0 constant_dynamic-update-slice_fusion.4
  2.7 2.0 %collective-permute-start = (bf16[64,1152]{1,0:T(8,128)(2,1)S(1)}, bf16[64,1152]{1,0:T(8,128)(2,1)S(1)}, u32[]{:S(2)}, u32[]{:S(2)}) collective-permute-start(bf16[64,1152]{1,0:T(8,128)(2,1)S(1)} %get-tuple-element.3), channel_id=1, source_target_pairs={{0,1},{1,0},{2,3},{3,2},{4,5},{5,4},{6,7},{7,6},{8,9},{9,8},{10,11... | collective-permute-start | bytes 442376 | tf_op jit(solution)/shard_map/ppermute | solution.py:34
  4.7 1.0 fusion.22
  5.8 1.0 fusion.11
  6.8 1.6 %collective-permute-start.5 = (bf16[32,1152]{1,0:T(8,128)(2,1)S(1)}, bf16[32,1152]{1,0:T(8,128)(2,1)S(1)}, u32[]{:S(2)}, u32[]{:S(2)}) collective-permute-start(bf16[32,1152]{1,0:T(8,128)(2,1)S(1)} %get-tuple-element.14), channel_id=1, source_target_pairs={{0,8},{1,9},{2,10},{3,11},{4,12},{5,13},{6,14},{7,15},{8,0},{9,1},... | collective-permute-start | bytes 221192 | tf_op jit(solution)/shard_map/ppermute | solution.py:34
  8.4 0.7 collective-permute-start.9
  10.5 0.8 collective-permute-done.5
  11.3 2.8 %collective-permute-start.6 = (bf16[64,1152]{1,0:T(8,128)(2,1)S(1)}, bf16[64,1152]{1,0:T(8,128)(2,1)S(1)}, u32[]{:S(2)}, u32[]{:S(2)}) collective-permute-start(bf16[64,1152]{1,0:T(8,128)(2,1)S(1)} %pad_maximum_fusion.6), channel_id=1, source_target_pairs={{0,136},{1,137},{2,138},{3,139},{4,140},{5,141},{6,142},{7,143},{8... | collective-permute-start | bytes 442376 | tf_op jit(solution)/shard_map/ppermute | solution.py:34
  14.1 0.3 collective-permute-start.10
  14.5 5.0 %collective-permute-start.1 = (bf16[128,1152]{1,0:T(8,128)(2,1)S(1)}, bf16[128,1152]{1,0:T(8,128)(2,1)S(1)}, u32[]{:S(2)}, u32[]{:S(2)}) collective-permute-start(bf16[128,1152]{1,0:T(8,128)(2,1)S(1)} %pad_maximum_fusion.2), channel_id=1, source_target_pairs={{0,7},{1,2},{2,1},{3,4},{4,3},{5,6},{6,5},{7,0},{8,15},{9,10},{10,... | collective-permute-start | bytes 884744 | tf_op jit(solution)/shard_map/ppermute | solution.py:34
  19.6 1.1 collective-permute-start.7
  20.7 0.3 collective-permute-start.11
  21.0 3.2 %collective-permute-done.1 = bf16[128,1152]{1,0:T(8,128)(2,1)S(1)} collective-permute-done((bf16[128,1152]{1,0:T(8,128)(2,1)S(1)}, bf16[128,1152]{1,0:T(8,128)(2,1)S(1)}, u32[]{:S(2)}, u32[]{:S(2)}) %collective-permute-start.1) | collective-permute-done | bytes 294944 | tf_op jit(solution)/shard_map/ppermute | solution.py:34
  24.3 2.1 %collective-permute-done.7 = bf16[128,1152]{1,0:T(8,128)(2,1)S(1)} collective-permute-done((bf16[128,1152]{1,0:T(8,128)(2,1)S(1)}, bf16[128,1152]{1,0:T(8,128)(2,1)S(1)}, u32[]{:S(2)}, u32[]{:S(2)}) %collective-permute-start.7) | collective-permute-done | bytes 294944 | tf_op jit(solution)/shard_map/ppermute | solution.py:34
  26.5 3.1 %collective-permute-start.8 = (bf16[256,1152]{1,0:T(8,128)(2,1)S(1)}, bf16[256,1152]{1,0:T(8,128)(2,1)S(1)}, u32[]{:S(2)}, u32[]{:S(2)}) collective-permute-start(bf16[256,1152]{1,0:T(8,128)(2,1)S(1)} %pad_maximum_fusion), channel_id=1, source_target_pairs={{0,48},{1,49},{2,50},{3,51},{4,52},{5,53},{6,54},{7,55},{8,56},{9,... | collective-permute-start | bytes 1769480 | tf_op jit(solution)/shard_map/ppermute | solution.py:34
  29.6 0.8 collective-permute-start.12
  30.4 0.5 collective-permute-done.2
  30.9 5.5 %collective-permute-start.3 = (bf16[128,1152]{1,0:T(8,128)(2,1)S(1)}, bf16[128,1152]{1,0:T(8,128)(2,1)S(1)}, u32[]{:S(2)}, u32[]{:S(2)}) collective-permute-start(bf16[128,1152]{1,0:T(8,128)(2,1)S(1)} %collective-permute-done.2), channel_id=1, source_target_pairs={{0,7},{1,2},{2,1},{3,4},{4,3},{5,6},{6,5},{7,0},{8,15},{9,10},{10,... | collective-permute-start | bytes 884744 | tf_op jit(solution)/shard_map/ppermute | solution.py:34
  36.5 4.6 %collective-permute-done.3 = bf16[128,1152]{1,0:T(8,128)(2,1)S(1)} collective-permute-done((bf16[128,1152]{1,0:T(8,128)(2,1)S(1)}, bf16[128,1152]{1,0:T(8,128)(2,1)S(1)}, u32[]{:S(2)}, u32[]{:S(2)}) %collective-permute-start.3) | collective-permute-done | bytes 294944 | tf_op jit(solution)/shard_map/ppermute | solution.py:34
  41.2 0.3 collective-permute-start.4
  41.8 2.6 %collective-permute-done.4 = bf16[512,1152]{1,0:T(8,128)(2,1)S(1)} collective-permute-done((bf16[512,1152]{1,0:T(8,128)(2,1)S(1)}, bf16[512,1152]{1,0:T(8,128)(2,1)S(1)}, u32[]{:S(2)}, u32[]{:S(2)}) %collective-permute-start.4) | collective-permute-done | bytes 1179680 | tf_op jit(solution)/shard_map/ppermute | solution.py:34
  44.3 0.2 constant_dynamic-update-slice_fusion.5
  44.5 4.1 %multiply_convert_fusion = bf16[1024,1024]{1,0:T(8,128)(2,1)S(1)} fusion(bf16[1024,1152]{1,0:T(8,128)(2,1)S(1)} %constant_dynamic-update-slice_fusion.5, bf16[1024,1152]{1,0:T(8,128)(2,1)S(1)} %constant_dynamic-update-slice_fusion.11, s32[1024]{0:T(1024)S(1)} %iota_add_fusion, f32[]{:T(128)} %bitcast.9, f32[]{:T(128)} %bitcast.8, ...), kind=kOutput, calls=%fused_computation | convolution fusion | flops 2428502016 | bytes 6821896 | tf_op jit(solution)/shard_map/dot_general | solution.py:103
  48.6 3.1 %fusion.31 = f32[1024,1152]{1,0:T(8,128)S(1)} fusion(bf16[1024,1024]{1,0:T(8,128)(2,1)S(1)} %multiply_convert_fusion, bf16[1024,1152]{1,0:T(8,128)(2,1)S(1)} %constant_dynamic-update-slice_fusion.5), kind=kOutput, calls=%fused_computation.94 | convolution fusion | flops 2415919104 | bytes 9175040 | tf_op jit(solution)/shard_map/dot_general | solution.py:117
  51.8 4.7 %collective-permute-start.13 = (f16[256,1152]{1,0:T(8,128)(2,1)S(1)}, f16[256,1152]{1,0:T(8,128)(2,1)S(1)}, u32[]{:S(2)}, u32[]{:S(2)}) collective-permute-start(f16[256,1152]{1,0:T(8,128)(2,1)S(1)} %fusion.1), channel_id=1, source_target_pairs={{0,48},{1,49},{2,50},{3,51},{4,52},{5,53},{6,54},{7,55},{8,56},{9,... | collective-permute-start | bytes 1769480 | tf_op jit(solution)/shard_map/ppermute | solution.py:34
  56.5 7.9 %collective-permute-done.13 = f16[256,1152]{1,0:T(8,128)(2,1)S(1)} collective-permute-done((f16[256,1152]{1,0:T(8,128)(2,1)S(1)}, f16[256,1152]{1,0:T(8,128)(2,1)S(1)}, u32[]{:S(2)}, u32[]{:S(2)}) %collective-permute-start.13) | collective-permute-done | bytes 589856 | tf_op jit(solution)/shard_map/ppermute | solution.py:34
  64.3 0.2 slice_add_fusion.2
  64.7 6.7 %collective-permute-done.14 = f16[128,1152]{1,0:T(8,128)(2,1)S(1)} collective-permute-done((f16[128,1152]{1,0:T(8,128)(2,1)S(1)}, f16[128,1152]{1,0:T(8,128)(2,1)S(1)}, u32[]{:S(2)}, u32[]{:S(2)}) %collective-permute-start.14) | collective-permute-done | bytes 294944 | tf_op jit(solution)/shard_map/ppermute | solution.py:34
  71.6 1.8 %collective-permute-start.15 = (f16[64,1152]{1,0:T(8,128)(2,1)S(1)}, f16[64,1152]{1,0:T(8,128)(2,1)S(1)}, u32[]{:S(2)}, u32[]{:S(2)}) collective-permute-start(f16[64,1152]{1,0:T(8,128)(2,1)S(1)} %fusion.25), channel_id=1, source_target_pairs={{0,136},{1,137},{2,138},{3,139},{4,140},{5,141},{6,142},{7,143},{8... | collective-permute-start | bytes 442376 | tf_op jit(solution)/shard_map/ppermute | solution.py:34
  73.4 2.9 %fusion.32 = f32[1024,1152]{1,0:T(8,128)S(1)} fusion(bf16[1024,1024]{1,0:T(8,128)(2,1)S(1)} %multiply_convert_fusion, bf16[1024,1152]{1,0:T(8,128)(2,1)S(1)} %constant_dynamic-update-slice_fusion.11), kind=kOutput, calls=%fused_computation.95 | convolution fusion | flops 2415919104 | bytes 9175040 | tf_op jit(solution)/shard_map/dot_general | solution.py:116
  76.3 0.2 slice.129
  76.5 1.6 %collective-permute-start.17 = (f16[256,1152]{1,0:T(8,128)(2,1)S(1)}, f16[256,1152]{1,0:T(8,128)(2,1)S(1)}, u32[]{:S(2)}, u32[]{:S(2)}) collective-permute-start(f16[256,1152]{1,0:T(8,128)(2,1)S(1)} %get-tuple-element.5), channel_id=1, source_target_pairs={{0,136},{1,137},{2,138},{3,139},{4,140},{5,141},{6,142},{7,143},{8... | collective-permute-start | bytes 1769480 | tf_op jit(solution)/shard_map/ppermute | solution.py:34
  78.3 9.8 %collective-permute-done.17 = f16[256,1152]{1,0:T(8,128)(2,1)S(1)} collective-permute-done((f16[256,1152]{1,0:T(8,128)(2,1)S(1)}, f16[256,1152]{1,0:T(8,128)(2,1)S(1)}, u32[]{:S(2)}, u32[]{:S(2)}) %collective-permute-start.17) | collective-permute-done | bytes 589856 | tf_op jit(solution)/shard_map/ppermute | solution.py:34
  88.1 0.2 slice_add_fusion.1
  88.5 6.7 %collective-permute-done.18 = f16[128,1152]{1,0:T(8,128)(2,1)S(1)} collective-permute-done((f16[128,1152]{1,0:T(8,128)(2,1)S(1)}, f16[128,1152]{1,0:T(8,128)(2,1)S(1)}, u32[]{:S(2)}, u32[]{:S(2)}) %collective-permute-start.18) | collective-permute-done | bytes 294944 | tf_op jit(solution)/shard_map/ppermute | solution.py:34
  95.3 3.0 %collective-permute-start.19 = (f16[64,1152]{1,0:T(8,128)(2,1)S(1)}, f16[64,1152]{1,0:T(8,128)(2,1)S(1)}, u32[]{:S(2)}, u32[]{:S(2)}) collective-permute-start(f16[64,1152]{1,0:T(8,128)(2,1)S(1)} %fusion.24), channel_id=1, source_target_pairs={{0,48},{1,49},{2,50},{3,51},{4,52},{5,53},{6,54},{7,55},{8,56},{9,... | collective-permute-start | bytes 442376 | tf_op jit(solution)/shard_map/ppermute | solution.py:34
  98.3 0.2 slice_add_fusion
  98.6 3.3 %collective-permute-start.22 = (f16[128,1152]{1,0:T(8,128)(2,1)S(1)}, f16[128,1152]{1,0:T(8,128)(2,1)S(1)}, u32[]{:S(2)}, u32[]{:S(2)}) collective-permute-start(f16[128,1152]{1,0:T(8,128)(2,1)S(1)} %fusion.2), channel_id=1, source_target_pairs={{0,7},{1,2},{2,1},{3,4},{4,3},{5,6},{6,5},{7,0},{8,15},{9,10},{10,... | collective-permute-start | bytes 884744 | tf_op jit(solution)/shard_map/ppermute | solution.py:34
  102.0 6.3 %collective-permute-done.22 = f16[128,1152]{1,0:T(8,128)(2,1)S(1)} collective-permute-done((f16[128,1152]{1,0:T(8,128)(2,1)S(1)}, f16[128,1152]{1,0:T(8,128)(2,1)S(1)}, u32[]{:S(2)}, u32[]{:S(2)}) %collective-permute-start.22) | collective-permute-done | bytes 294944 | tf_op jit(solution)/shard_map/ppermute | solution.py:34
  108.6 9.4 %collective-permute-done.23 = f16[128,1152]{1,0:T(8,128)(2,1)S(1)} collective-permute-done((f16[128,1152]{1,0:T(8,128)(2,1)S(1)}, f16[128,1152]{1,0:T(8,128)(2,1)S(1)}, u32[]{:S(2)}, u32[]{:S(2)}) %collective-permute-start.23) | collective-permute-done | bytes 294944 | tf_op jit(solution)/shard_map/ppermute | solution.py:34
  118.1 3.9 %collective-permute-start.24 = (f16[128,1152]{1,0:T(8,128)(2,1)S(1)}, f16[128,1152]{1,0:T(8,128)(2,1)S(1)}, u32[]{:S(2)}, u32[]{:S(2)}) collective-permute-start(f16[128,1152]{1,0:T(8,128)(2,1)S(1)} %fusion.6), channel_id=1, source_target_pairs={{0,7},{1,2},{2,1},{3,4},{4,3},{5,6},{6,5},{7,0},{8,15},{9,10},{10,... | collective-permute-start | bytes 884744 | tf_op jit(solution)/shard_map/ppermute | solution.py:34
  122.0 0.2 fusion.19
  122.3 5.5 %collective-permute-done.24 = f16[128,1152]{1,0:T(8,128)(2,1)S(1)} collective-permute-done((f16[128,1152]{1,0:T(8,128)(2,1)S(1)}, f16[128,1152]{1,0:T(8,128)(2,1)S(1)}, u32[]{:S(2)}, u32[]{:S(2)}) %collective-permute-start.24) | collective-permute-done | bytes 294944 | tf_op jit(solution)/shard_map/ppermute | solution.py:34
  127.9 0.8 fusion.21
  128.8 4.3 %collective-permute-done.25 = f16[64,1152]{1,0:T(8,128)(2,1)S(1)} collective-permute-done((f16[64,1152]{1,0:T(8,128)(2,1)S(1)}, f16[64,1152]{1,0:T(8,128)(2,1)S(1)}, u32[]{:S(2)}, u32[]{:S(2)}) %collective-permute-start.25) | collective-permute-done | bytes 147488 | tf_op jit(solution)/shard_map/ppermute | solution.py:34
  133.1 0.2 fusion.15
  133.3 0.8 fusion.17
  (68 shorter events, 2.4 us)
Async XLA Ops:
  2.7 11.7 %collective-permute-start = (bf16[64,1152]{1,0:T(8,128)(2,1)S(1)}, bf16[64,1152]{1,0:T(8,128)(2,1)S(1)}, u32[]{:S(2)}, u32[]{:S(2)}) collective-permute-start(bf16[64,1152]{1,0:T(8,128)(2,1)S(1)} %get-tuple-element.3), channel_id=1, source_target_pairs={{0,1},{1,0},{2,3},{3,2},{4,5},{5,4},{6,7},{7,6},{8,9},{9,8},{10,11... | collective-permute-start | bytes 442376 | tf_op jit(solution)/shard_map/ppermute | solution.py:34
  6.8 4.4 %collective-permute-start.5 = (bf16[32,1152]{1,0:T(8,128)(2,1)S(1)}, bf16[32,1152]{1,0:T(8,128)(2,1)S(1)}, u32[]{:S(2)}, u32[]{:S(2)}) collective-permute-start(bf16[32,1152]{1,0:T(8,128)(2,1)S(1)} %get-tuple-element.14), channel_id=1, source_target_pairs={{0,8},{1,9},{2,10},{3,11},{4,12},{5,13},{6,14},{7,15},{8,0},{9,1},... | collective-permute-start | bytes 221192 | tf_op jit(solution)/shard_map/ppermute | solution.py:34
  8.4 5.7 %collective-permute-start.9 = (bf16[32,1152]{1,0:T(8,128)(2,1)S(1)}, bf16[32,1152]{1,0:T(8,128)(2,1)S(1)}, u32[]{:S(2)}, u32[]{:S(2)}) collective-permute-start(bf16[32,1152]{1,0:T(8,128)(2,1)S(1)} %get-tuple-element.12), channel_id=1, source_target_pairs={{0,16},{1,17},{2,18},{3,19},{4,20},{5,21},{6,22},{7,23},{8,24},{9,... | collective-permute-start | bytes 221192 | tf_op jit(solution)/shard_map/ppermute | solution.py:34
  11.3 8.3 %collective-permute-start.6 = (bf16[64,1152]{1,0:T(8,128)(2,1)S(1)}, bf16[64,1152]{1,0:T(8,128)(2,1)S(1)}, u32[]{:S(2)}, u32[]{:S(2)}) collective-permute-start(bf16[64,1152]{1,0:T(8,128)(2,1)S(1)} %pad_maximum_fusion.6), channel_id=1, source_target_pairs={{0,136},{1,137},{2,138},{3,139},{4,140},{5,141},{6,142},{7,143},{8... | collective-permute-start | bytes 442376 | tf_op jit(solution)/shard_map/ppermute | solution.py:34
  14.1 6.5 %collective-permute-start.10 = (bf16[64,1152]{1,0:T(8,128)(2,1)S(1)}, bf16[64,1152]{1,0:T(8,128)(2,1)S(1)}, u32[]{:S(2)}, u32[]{:S(2)}) collective-permute-start(bf16[64,1152]{1,0:T(8,128)(2,1)S(1)} %pad_maximum_fusion.7), channel_id=1, source_target_pairs={{0,48},{1,49},{2,50},{3,51},{4,52},{5,53},{6,54},{7,55},{8,56},{9,... | collective-permute-start | bytes 442376 | tf_op jit(solution)/shard_map/ppermute | solution.py:34
  14.5 9.7 %collective-permute-start.1 = (bf16[128,1152]{1,0:T(8,128)(2,1)S(1)}, bf16[128,1152]{1,0:T(8,128)(2,1)S(1)}, u32[]{:S(2)}, u32[]{:S(2)}) collective-permute-start(bf16[128,1152]{1,0:T(8,128)(2,1)S(1)} %pad_maximum_fusion.2), channel_id=1, source_target_pairs={{0,7},{1,2},{2,1},{3,4},{4,3},{5,6},{6,5},{7,0},{8,15},{9,10},{10,... | collective-permute-start | bytes 884744 | tf_op jit(solution)/shard_map/ppermute | solution.py:34
  19.6 6.8 %collective-permute-start.7 = (bf16[128,1152]{1,0:T(8,128)(2,1)S(1)}, bf16[128,1152]{1,0:T(8,128)(2,1)S(1)}, u32[]{:S(2)}, u32[]{:S(2)}) collective-permute-start(bf16[128,1152]{1,0:T(8,128)(2,1)S(1)} %pad_maximum_fusion.3), channel_id=1, source_target_pairs={{0,16},{1,17},{2,18},{3,19},{4,20},{5,21},{6,22},{7,23},{8,24},{9,... | collective-permute-start | bytes 884744 | tf_op jit(solution)/shard_map/ppermute | solution.py:34
  20.7 8.9 %collective-permute-start.11 = (bf16[128,1152]{1,0:T(8,128)(2,1)S(1)}, bf16[128,1152]{1,0:T(8,128)(2,1)S(1)}, u32[]{:S(2)}, u32[]{:S(2)}) collective-permute-start(bf16[128,1152]{1,0:T(8,128)(2,1)S(1)} %pad_maximum_fusion.4), channel_id=1, source_target_pairs={{0,8},{1,9},{2,10},{3,11},{4,12},{5,13},{6,14},{7,15},{8,0},{9,1},... | collective-permute-start | bytes 884744 | tf_op jit(solution)/shard_map/ppermute | solution.py:34
  24.2 6.7 %collective-permute-start.2 = (bf16[128,1152]{1,0:T(8,128)(2,1)S(1)}, bf16[128,1152]{1,0:T(8,128)(2,1)S(1)}, u32[]{:S(2)}, u32[]{:S(2)}) collective-permute-start(bf16[128,1152]{1,0:T(8,128)(2,1)S(1)} %collective-permute-done.1), channel_id=1, source_target_pairs={{0,1},{1,0},{2,3},{3,2},{4,5},{5,4},{6,7},{7,6},{8,9},{9,8},{10,11... | collective-permute-start | bytes 884744 | tf_op jit(solution)/shard_map/ppermute | solution.py:34
  26.5 15.0 %collective-permute-start.8 = (bf16[256,1152]{1,0:T(8,128)(2,1)S(1)}, bf16[256,1152]{1,0:T(8,128)(2,1)S(1)}, u32[]{:S(2)}, u32[]{:S(2)}) collective-permute-start(bf16[256,1152]{1,0:T(8,128)(2,1)S(1)} %pad_maximum_fusion), channel_id=1, source_target_pairs={{0,48},{1,49},{2,50},{3,51},{4,52},{5,53},{6,54},{7,55},{8,56},{9,... | collective-permute-start | bytes 1769480 | tf_op jit(solution)/shard_map/ppermute | solution.py:34
  29.6 12.1 %collective-permute-start.12 = (bf16[256,1152]{1,0:T(8,128)(2,1)S(1)}, bf16[256,1152]{1,0:T(8,128)(2,1)S(1)}, u32[]{:S(2)}, u32[]{:S(2)}) collective-permute-start(bf16[256,1152]{1,0:T(8,128)(2,1)S(1)} %pad_maximum_fusion.1), channel_id=1, source_target_pairs={{0,136},{1,137},{2,138},{3,139},{4,140},{5,141},{6,142},{7,143},{8... | collective-permute-start | bytes 1769480 | tf_op jit(solution)/shard_map/ppermute | solution.py:34
  30.9 10.2 %collective-permute-start.3 = (bf16[128,1152]{1,0:T(8,128)(2,1)S(1)}, bf16[128,1152]{1,0:T(8,128)(2,1)S(1)}, u32[]{:S(2)}, u32[]{:S(2)}) collective-permute-start(bf16[128,1152]{1,0:T(8,128)(2,1)S(1)} %collective-permute-done.2), channel_id=1, source_target_pairs={{0,7},{1,2},{2,1},{3,4},{4,3},{5,6},{6,5},{7,0},{8,15},{9,10},{10,... | collective-permute-start | bytes 884744 | tf_op jit(solution)/shard_map/ppermute | solution.py:34
  41.2 3.1 %collective-permute-start.4 = (bf16[512,1152]{1,0:T(8,128)(2,1)S(1)}, bf16[512,1152]{1,0:T(8,128)(2,1)S(1)}, u32[]{:S(2)}, u32[]{:S(2)}) collective-permute-start(bf16[512,1152]{1,0:T(8,128)(2,1)S(1)} %get-tuple-element.6), channel_id=1, source_target_pairs={{0,64},{1,65},{2,66},{3,67},{4,68},{5,69},{6,70},{7,71},{8,72},{9,... | collective-permute-start | bytes 3538952 | tf_op jit(solution)/shard_map/ppermute | solution.py:34
  51.8 12.6 %collective-permute-start.13 = (f16[256,1152]{1,0:T(8,128)(2,1)S(1)}, f16[256,1152]{1,0:T(8,128)(2,1)S(1)}, u32[]{:S(2)}, u32[]{:S(2)}) collective-permute-start(f16[256,1152]{1,0:T(8,128)(2,1)S(1)} %fusion.1), channel_id=1, source_target_pairs={{0,48},{1,49},{2,50},{3,51},{4,52},{5,53},{6,54},{7,55},{8,56},{9,... | collective-permute-start | bytes 1769480 | tf_op jit(solution)/shard_map/ppermute | solution.py:34
  64.6 6.8 %collective-permute-start.14 = (f16[128,1152]{1,0:T(8,128)(2,1)S(1)}, f16[128,1152]{1,0:T(8,128)(2,1)S(1)}, u32[]{:S(2)}, u32[]{:S(2)}) collective-permute-start(f16[128,1152]{1,0:T(8,128)(2,1)S(1)} %fusion.8), channel_id=1, source_target_pairs={{0,16},{1,17},{2,18},{3,19},{4,20},{5,21},{6,22},{7,23},{8,24},{9,... | collective-permute-start | bytes 884744 | tf_op jit(solution)/shard_map/ppermute | solution.py:34
  71.6 6.6 %collective-permute-start.15 = (f16[64,1152]{1,0:T(8,128)(2,1)S(1)}, f16[64,1152]{1,0:T(8,128)(2,1)S(1)}, u32[]{:S(2)}, u32[]{:S(2)}) collective-permute-start(f16[64,1152]{1,0:T(8,128)(2,1)S(1)} %fusion.25), channel_id=1, source_target_pairs={{0,136},{1,137},{2,138},{3,139},{4,140},{5,141},{6,142},{7,143},{8... | collective-permute-start | bytes 442376 | tf_op jit(solution)/shard_map/ppermute | solution.py:34
  76.4 21.9 %collective-permute-start.21 = (f32[512,1152]{1,0:T(8,128)S(1)}, f32[512,1152]{1,0:T(8,128)S(1)}, u32[]{:S(2)}, u32[]{:S(2)}) collective-permute-start(f32[512,1152]{1,0:T(8,128)S(1)} %slice.129), channel_id=1, source_target_pairs={{0,64},{1,65},{2,66},{3,67},{4,68},{5,69},{6,70},{7,71},{8,72},{9,... | collective-permute-start | bytes 7077896 | tf_op jit(solution)/shard_map/ppermute | solution.py:34
  76.5 11.6 %collective-permute-start.17 = (f16[256,1152]{1,0:T(8,128)(2,1)S(1)}, f16[256,1152]{1,0:T(8,128)(2,1)S(1)}, u32[]{:S(2)}, u32[]{:S(2)}) collective-permute-start(f16[256,1152]{1,0:T(8,128)(2,1)S(1)} %get-tuple-element.5), channel_id=1, source_target_pairs={{0,136},{1,137},{2,138},{3,139},{4,140},{5,141},{6,142},{7,143},{8... | collective-permute-start | bytes 1769480 | tf_op jit(solution)/shard_map/ppermute | solution.py:34
  78.2 10.3 %collective-permute-start.16 = (f16[32,1152]{1,0:T(8,128)(2,1)S(1)}, f16[32,1152]{1,0:T(8,128)(2,1)S(1)}, u32[]{:S(2)}, u32[]{:S(2)}) collective-permute-start(f16[32,1152]{1,0:T(8,128)(2,1)S(1)} %fusion.27), channel_id=1, source_target_pairs={{0,8},{1,9},{2,10},{3,11},{4,12},{5,13},{6,14},{7,15},{8,0},{9,1},... | collective-permute-start | bytes 221192 | tf_op jit(solution)/shard_map/ppermute | solution.py:34
  88.3 6.8 %collective-permute-start.18 = (f16[128,1152]{1,0:T(8,128)(2,1)S(1)}, f16[128,1152]{1,0:T(8,128)(2,1)S(1)}, u32[]{:S(2)}, u32[]{:S(2)}) collective-permute-start(f16[128,1152]{1,0:T(8,128)(2,1)S(1)} %fusion.7), channel_id=1, source_target_pairs={{0,8},{1,9},{2,10},{3,11},{4,12},{5,13},{6,14},{7,15},{8,0},{9,1},... | collective-permute-start | bytes 884744 | tf_op jit(solution)/shard_map/ppermute | solution.py:34
  95.3 6.7 %collective-permute-start.19 = (f16[64,1152]{1,0:T(8,128)(2,1)S(1)}, f16[64,1152]{1,0:T(8,128)(2,1)S(1)}, u32[]{:S(2)}, u32[]{:S(2)}) collective-permute-start(f16[64,1152]{1,0:T(8,128)(2,1)S(1)} %fusion.24), channel_id=1, source_target_pairs={{0,48},{1,49},{2,50},{3,51},{4,52},{5,53},{6,54},{7,55},{8,56},{9,... | collective-permute-start | bytes 442376 | tf_op jit(solution)/shard_map/ppermute | solution.py:34
  98.5 23.5 %copy-start = (bf16[64,1152]{1,0:T(8,128)(2,1)S(1)}, bf16[64,1152]{1,0:T(8,128)(2,1)}, u32[]{:S(2)}) copy-start(bf16[64,1152]{1,0:T(8,128)(2,1)} %param.4) | copy-start | bytes 442372
  98.6 9.6 %collective-permute-start.22 = (f16[128,1152]{1,0:T(8,128)(2,1)S(1)}, f16[128,1152]{1,0:T(8,128)(2,1)S(1)}, u32[]{:S(2)}, u32[]{:S(2)}) collective-permute-start(f16[128,1152]{1,0:T(8,128)(2,1)S(1)} %fusion.2), channel_id=1, source_target_pairs={{0,7},{1,2},{2,1},{3,4},{4,3},{5,6},{6,5},{7,0},{8,15},{9,10},{10,... | collective-permute-start | bytes 884744 | tf_op jit(solution)/shard_map/ppermute | solution.py:34
  108.4 9.7 %collective-permute-start.23 = (f16[128,1152]{1,0:T(8,128)(2,1)S(1)}, f16[128,1152]{1,0:T(8,128)(2,1)S(1)}, u32[]{:S(2)}, u32[]{:S(2)}) collective-permute-start(f16[128,1152]{1,0:T(8,128)(2,1)S(1)} %fusion.4), channel_id=1, source_target_pairs={{0,1},{1,0},{2,3},{3,2},{4,5},{5,4},{6,7},{7,6},{8,9},{9,8},{10,11... | collective-permute-start | bytes 884744 | tf_op jit(solution)/shard_map/ppermute | solution.py:34
  108.5 24.6 %copy-start.1 = (bf16[64,1152]{1,0:T(8,128)(2,1)S(1)}, bf16[64,1152]{1,0:T(8,128)(2,1)}, u32[]{:S(2)}) copy-start(bf16[64,1152]{1,0:T(8,128)(2,1)} %param.5) | copy-start | bytes 442372
  108.5 13.5 %collective-permute-start.20 = (f16[32,1152]{1,0:T(8,128)(2,1)S(1)}, f16[32,1152]{1,0:T(8,128)(2,1)S(1)}, u32[]{:S(2)}, u32[]{:S(2)}) collective-permute-start(f16[32,1152]{1,0:T(8,128)(2,1)S(1)} %fusion.26), channel_id=1, source_target_pairs={{0,16},{1,17},{2,18},{3,19},{4,20},{5,21},{6,22},{7,23},{8,24},{9,... | collective-permute-start | bytes 221192 | tf_op jit(solution)/shard_map/ppermute | solution.py:34
  118.1 9.6 %collective-permute-start.24 = (f16[128,1152]{1,0:T(8,128)(2,1)S(1)}, f16[128,1152]{1,0:T(8,128)(2,1)S(1)}, u32[]{:S(2)}, u32[]{:S(2)}) collective-permute-start(f16[128,1152]{1,0:T(8,128)(2,1)S(1)} %fusion.6), channel_id=1, source_target_pairs={{0,7},{1,2},{2,1},{3,4},{4,3},{5,6},{6,5},{7,0},{8,15},{9,10},{10,... | collective-permute-start | bytes 884744 | tf_op jit(solution)/shard_map/ppermute | solution.py:34
  127.8 5.2 %collective-permute-start.25 = (f16[64,1152]{1,0:T(8,128)(2,1)S(1)}, f16[64,1152]{1,0:T(8,128)(2,1)S(1)}, u32[]{:S(2)}, u32[]{:S(2)}) collective-permute-start(f16[64,1152]{1,0:T(8,128)(2,1)S(1)} %fusion.23), channel_id=1, source_target_pairs={{0,1},{1,0},{2,3},{3,2},{4,5},{5,4},{6,7},{7,6},{8,9},{9,8},{10,11... | collective-permute-start | bytes 442376 | tf_op jit(solution)/shard_map/ppermute | solution.py:34

commit v2 on v1

v2 whole, which is shorter than its diff:
```python
import jax
import jax.numpy as jnp
import numpy as np
from jax import lax
from jax.sharding import PartitionSpec as P

epsilon = 1e-06

SHAPE = (2, 2, 4, 2, 8)
AXES = ("group", "blk")
SHRINK = 0.25


def neighbour_pairs(axis, phase):
    perm = []
    for i, (xh, core, y, xl, z) in enumerate(np.ndindex(*SHAPE)):
        at = {"x": 2 * xh + xl, "y": y, "z": z}
        n = {"x": 4, "y": 4, "z": 8}[axis]
        p = at[axis]
        if (phase + core) % 2 == 0:
            at[axis] = p ^ 1
        else:
            at[axis] = (p + 1) % n if p % 2 else (p - 1) % n
        there = (at["x"] // 2, core, at["y"], at["x"] % 2, at["z"])
        perm.append((i, int(np.ravel_multi_index(there, SHAPE))))
    return perm


PX, PY, PZ = ([neighbour_pairs(axis, 0), neighbour_pairs(axis, 1)] for axis in "xyz")
PC = [(i, i ^ 64) for i in range(256)]


def swap(array, perm):
    return lax.ppermute(array, AXES, perm)


def join(*arrays):
    return jnp.concatenate(arrays, axis=0)


def normalize(embedding):
    values = embedding.astype(jnp.float32)
    inverse = lax.rsqrt(jnp.sum(values * values, axis=-1, keepdims=True) + epsilon)
    return (values * inverse, inverse)


def unit_grad(unit_vec, inverse, grad_sum):
    return (grad_sum - unit_vec * jnp.sum(unit_vec * grad_sum, axis=-1, keepdims=True)) * inverse


def step(*arrays):
    return lax.optimization_barrier(arrays)


def gather(images, texts):
    half = images.shape[0] // 2
    a, b, text_parts = images[:half], images[half:], [texts]
    for k, (pa, pb) in enumerate(zip(PX + PY, PY + PX)):
        text = join(*text_parts) if k < 2 else text_parts[-1]
        got_text, got_a, got_b = step(swap(text, PZ[k % 2]), swap(a, pa), swap(b, pb))
        a, b = join(a, got_a), join(b, got_b)
        text_parts.append(got_text)
    return a, b, join(*text_parts)


def shrunk(part):
    return (part * SHRINK).astype(jnp.float16)


def grown(part):
    return part.astype(jnp.float32) * (1 / SHRINK)


def scatter(a, b, text):
    n = text.shape[0] // 4
    texts = [text[i * n : (i + 1) * n] for i in range(4)]
    half_text = n // 2
    for k, (pa, pb) in reversed(list(enumerate(zip(PX + PY, PY + PX)))):
        n = a.shape[0] // 2
        out_text = texts[k] if k else texts[0][half_text:]
        got_a, got_b, got_text = step(
            swap(shrunk(a[n:]), pa), swap(shrunk(b[n:]), pb), swap(shrunk(out_text), PZ[k % 2])
        )
        a, b = a[:n] + grown(got_a), b[:n] + grown(got_b)
        if k:
            texts[k - 1] = texts[k - 1] + grown(got_text)
        else:
            texts[0] = texts[0][:half_text] + grown(got_text)
    return a, b, texts[0]


def logits_of(texts, images, factor, offset):
    product = lax.dot_general(
        texts, images, (((1,), (1,)), ((), ())), preferred_element_type=jnp.float32
    )
    return factor * product + offset


def body(images, texts, logit_scale, bias):
    image_unit, image_inv = normalize(images)
    text_unit, text_inv = normalize(texts)
    image_low = image_unit.astype(jnp.bfloat16)
    text_low = text_unit.astype(jnp.bfloat16)
    factor = logit_scale[0]
    offset = bias[0]
    rows = images.shape[0]
    half = rows // 2
    images_a, images_b, texts_core = gather(image_low, text_low)
    texts_other = swap(texts_core, PC)
    image_all = join(images_a, images_b)
    n = image_all.shape[0]
    row = lax.broadcasted_iota(jnp.int32, (n // 2, n), 0)
    col = lax.broadcasted_iota(jnp.int32, (n // 2, n), 1)
    image_id = jnp.where(
        col < half, col, jnp.where((col >= n // 2) & (col < n // 2 + half), col - n // 2 + half, n)
    )
    positive = (row == image_id).astype(jnp.float32)
    weights_core = (
        factor * (jax.nn.sigmoid(logits_of(texts_core, image_all, factor, offset)) - positive)
    ).astype(jnp.bfloat16)
    texts_other, weights_core = lax.optimization_barrier((texts_other, weights_core))
    weights_other = (
        factor * jax.nn.sigmoid(logits_of(texts_other, image_all, factor, offset))
    ).astype(jnp.bfloat16)
    text_sum_other = jnp.dot(weights_other, image_all, preferred_element_type=jnp.float32)
    weights_other, text_sum_other = lax.optimization_barrier((weights_other, text_sum_other))
    got_text = swap(text_sum_other, PC)
    weights = join(weights_core, weights_other)
    image_sum = lax.dot_general(
        weights,
        join(texts_core, texts_other),
        (((0,), (0,)), ((), ())),
        preferred_element_type=jnp.float32,
    )
    weights_core, image_sum = lax.optimization_barrier((weights_core, image_sum))
    text_sum_core = jnp.dot(weights_core, image_all, preferred_element_type=jnp.float32)
    a, b, text_own = scatter(image_sum[: n // 2], image_sum[n // 2 :], text_sum_core + got_text)
    return (
        unit_grad(image_unit, image_inv, join(a, b)),
        unit_grad(text_unit, text_inv, text_own),
    )


def solution(mesh):
    return jax.shard_map(
        body,
        mesh=mesh,
        in_specs=(P(("group", "blk"), None), P(("group", "blk"), None), P(), P()),
        out_specs=(P(("group", "blk"), None), P(("group", "blk"), None)),
        check_vma=False,
    )
```

time: 134 us -> 99.2 us (0.74)
  waiting for transfers between devices: 70.3 us -> 43.7 us
  starting transfers between devices: 42.5 us -> 34.6 us
    ppermute x26, waiting for transfers between devices: 70.3 us -> 43.7 us  [swap(): return lax.ppermute(array, AXES, perm)]
    ppermute x26, starting transfers between devices: 42.5 us -> 34.6 us  [swap(): return lax.ppermute(array, AXES, perm)]
    dot_general x3 -> x5, matrix products: 10 us -> 9.85 us  [the longest x2 3.78 us: logits_of(): lax.dot_general(texts, images, (((1,), (1,)), ((), ())), preferred_elemen...]
  transfers between devices with their start and end apart: 26 -> 26, of which waited for: 14 -> 21; matrix products, arithmetic and copies ran while one was open for 6% -> 10% of each run, Pallas kernels for 0% -> 0%
where the time goes in v2:
time: 99.2 us; the launch traced here: 98.9 us
  waiting for transfers between devices  43.7 us (44%)
  starting transfers between devices  34.6 us (35%)
  matrix products  9.85 us (10%)
  other arithmetic  7.76 us (8%)
  between operations  2.26 us (2%)
    ppermute x26, waiting for transfers between devices, swap(): return lax.ppermute(array, AXES, perm)  43.7 us
    ppermute x26, starting transfers between devices, swap(): return lax.ppermute(array, AXES, perm)  34.6 us
    dot_general x2, matrix products, logits_of(): lax.dot_general(texts, images, (((1,), (1,)), ((), ())), preferred_elemen...  3.78 us
    dot_general x1, matrix products, body(): lax.dot_general(weights, join(texts_core, texts_other), (((0,), (0,)), ((...  3 us
    reduce_sum x2, other arithmetic, normalize(): jnp.sum(values * values, axis=-1, keepdims=True) + epsilon  2.08 us
  transfers between devices with their start and end apart: 26, of which 21 were waited for; matrix products, arithmetic and copies ran while one was open for 10% of the time, Pallas kernels for 0%

profile of v2, /device:TPU:24, one launch (start us, length us, event | category | flops | bytes accessed | tf_op | source)
XLA Modules:
  0.0 98.9 jit_solution(17361509405564408999)
XLA Ops:
  0.6 1.0 %fusion.20 = f32[64]{0:T(128)S(1)} fusion(bf16[64,1152]{1,0:T(8,128)(2,1)} %param.5), kind=kLoop, calls=%fused_computation.42 | loop fusion | flops 221120 | bytes 147712 | tf_op jit(solution)/shard_map/reduce_sum | solution.py:43
  1.7 1.0 %constant_dynamic-update-slice_fusion.20 = (bf16[1024,1152]{1,0:T(8,128)(2,1)S(1)}, bf16[64,1152]{1,0:T(8,128)(2,1)S(1)}) fusion(f32[64]{0:T(128)S(1)} %add_rsqrt_fusion.1, bf16[64,1152]{1,0:T(8,128)(2,1)} %param.5), kind=kLoop, calls=%fused_computation.88 | loop fusion | flops 221183 | bytes 442624
  2.7 2.0 %collective-permute-start = (bf16[64,1152]{1,0:T(8,128)(2,1)S(1)}, bf16[64,1152]{1,0:T(8,128)(2,1)S(1)}, u32[]{:S(2)}, u32[]{:S(2)}) collective-permute-start(bf16[64,1152]{1,0:T(8,128)(2,1)S(1)} %get-tuple-element.63), channel_id=1, source_target_pairs={{0,1},{1,0},{2,3},{3,2},{4,5},{5,4},{6,7},{7,6},{8,9},{9,8},{10,11... | collective-permute-start | bytes 442376 | tf_op jit(solution)/shard_map/ppermute | solution.py:34
  4.7 1.0 %fusion.24 = f32[64]{0:T(128)S(1)} fusion(bf16[64,1152]{1,0:T(8,128)(2,1)} %param.4), kind=kLoop, calls=%fused_computation.46 | loop fusion | flops 221120 | bytes 147712 | tf_op jit(solution)/shard_map/reduce_sum | solution.py:43
  5.8 1.0 %fusion.13 = bf16[64,1152]{1,0:T(8,128)(2,1)S(1)} fusion(bf16[64,1152]{1,0:T(8,128)(2,1)} %param.4, f32[64]{0:T(128)S(1)} %add_rsqrt_fusion), kind=kLoop, calls=%fused_computation.33 | loop fusion | flops 221184 | bytes 295168 | tf_op jit(solution)/shard_map/convert_element_type | solution.py:102
  6.8 1.6 %collective-permute-start.1 = (bf16[32,1152]{1,0:T(8,128)(2,1)S(1)}, bf16[32,1152]{1,0:T(8,128)(2,1)S(1)}, u32[]{:S(2)}, u32[]{:S(2)}) collective-permute-start(bf16[32,1152]{1,0:T(8,128)(2,1)S(1)} %get-tuple-element.78), channel_id=1, source_target_pairs={{0,8},{1,9},{2,10},{3,11},{4,12},{5,13},{6,14},{7,15},{8,0},{9,1},... | collective-permute-start | bytes 221192 | tf_op jit(solution)/shard_map/ppermute | solution.py:34
  8.4 0.7 collective-permute-start.2
  9.1 2.1 %collective-permute-done.1 = bf16[32,1152]{1,0:T(8,128)(2,1)S(1)} collective-permute-done((bf16[32,1152]{1,0:T(8,128)(2,1)S(1)}, bf16[32,1152]{1,0:T(8,128)(2,1)S(1)}, u32[]{:S(2)}, u32[]{:S(2)}) %collective-permute-start.1) | collective-permute-done | bytes 73760 | tf_op jit(solution)/shard_map/ppermute | solution.py:34
  11.2 1.5 %collective-permute-done.2 = bf16[32,1152]{1,0:T(8,128)(2,1)S(1)} collective-permute-done((bf16[32,1152]{1,0:T(8,128)(2,1)S(1)}, bf16[32,1152]{1,0:T(8,128)(2,1)S(1)}, u32[]{:S(2)}, u32[]{:S(2)}) %collective-permute-start.2) | collective-permute-done | bytes 73760 | tf_op jit(solution)/shard_map/ppermute | solution.py:34
  12.8 5.0 %collective-permute-start.3 = (bf16[128,1152]{1,0:T(8,128)(2,1)S(1)}, bf16[128,1152]{1,0:T(8,128)(2,1)S(1)}, u32[]{:S(2)}, u32[]{:S(2)}) collective-permute-start(bf16[128,1152]{1,0:T(8,128)(2,1)S(1)} %pad_maximum_fusion.2), channel_id=1, source_target_pairs={{0,7},{1,2},{2,1},{3,4},{4,3},{5,6},{6,5},{7,0},{8,15},{9,10},{10,... | collective-permute-start | bytes 884744 | tf_op jit(solution)/shard_map/ppermute | solution.py:34
  17.8 2.2 %collective-permute-start.4 = (bf16[64,1152]{1,0:T(8,128)(2,1)S(1)}, bf16[64,1152]{1,0:T(8,128)(2,1)S(1)}, u32[]{:S(2)}, u32[]{:S(2)}) collective-permute-start(bf16[64,1152]{1,0:T(8,128)(2,1)S(1)} %pad_maximum_fusion.6), channel_id=1, source_target_pairs={{0,136},{1,137},{2,138},{3,139},{4,140},{5,141},{6,142},{7,143},{8... | collective-permute-start | bytes 442376 | tf_op jit(solution)/shard_map/ppermute | solution.py:34
  21.6 2.6 %collective-permute-done.4 = bf16[64,1152]{1,0:T(8,128)(2,1)S(1)} collective-permute-done((bf16[64,1152]{1,0:T(8,128)(2,1)S(1)}, bf16[64,1152]{1,0:T(8,128)(2,1)S(1)}, u32[]{:S(2)}, u32[]{:S(2)}) %collective-permute-start.4) | collective-permute-done | bytes 147488 | tf_op jit(solution)/shard_map/ppermute | solution.py:34
  24.3 2.2 %collective-permute-done.5 = bf16[64,1152]{1,0:T(8,128)(2,1)S(1)} collective-permute-done((bf16[64,1152]{1,0:T(8,128)(2,1)S(1)}, bf16[64,1152]{1,0:T(8,128)(2,1)S(1)}, u32[]{:S(2)}, u32[]{:S(2)}) %collective-permute-start.5) | collective-permute-done | bytes 147488 | tf_op jit(solution)/shard_map/ppermute | solution.py:34
  26.6 0.7 collective-permute-start.8
  27.4 5.8 %collective-permute-done.6 = bf16[128,1152]{1,0:T(8,128)(2,1)S(1)} collective-permute-done((bf16[128,1152]{1,0:T(8,128)(2,1)S(1)}, bf16[128,1152]{1,0:T(8,128)(2,1)S(1)}, u32[]{:S(2)}, u32[]{:S(2)}) %collective-permute-start.6) | collective-permute-done | bytes 294944 | tf_op jit(solution)/shard_map/ppermute | solution.py:34
  33.6 0.6 collective-permute-start.10
  34.2 1.3 %collective-permute-start.11 = (bf16[256,1152]{1,0:T(8,128)(2,1)S(1)}, bf16[256,1152]{1,0:T(8,128)(2,1)S(1)}, u32[]{:S(2)}, u32[]{:S(2)}) collective-permute-start(bf16[256,1152]{1,0:T(8,128)(2,1)S(1)} %pad_maximum_fusion.1), channel_id=1, source_target_pairs={{0,136},{1,137},{2,138},{3,139},{4,140},{5,141},{6,142},{7,143},{8... | collective-permute-start | bytes 1769480 | tf_op jit(solution)/shard_map/ppermute | solution.py:34
  35.5 2.0 %collective-permute-start.9 = (bf16[128,1152]{1,0:T(8,128)(2,1)S(1)}, bf16[128,1152]{1,0:T(8,128)(2,1)S(1)}, u32[]{:S(2)}, u32[]{:S(2)}) collective-permute-start(bf16[128,1152]{1,0:T(8,128)(2,1)S(1)} %collective-permute-done.6), channel_id=1, source_target_pairs={{0,7},{1,2},{2,1},{3,4},{4,3},{5,6},{6,5},{7,0},{8,15},{9,10},{10,... | collective-permute-start | bytes 884744 | tf_op jit(solution)/shard_map/ppermute | solution.py:34
  37.7 5.8 %collective-permute-done.9 = bf16[128,1152]{1,0:T(8,128)(2,1)S(1)} collective-permute-done((bf16[128,1152]{1,0:T(8,128)(2,1)S(1)}, bf16[128,1152]{1,0:T(8,128)(2,1)S(1)}, u32[]{:S(2)}, u32[]{:S(2)}) %collective-permute-start.9) | collective-permute-done | bytes 294944 | tf_op jit(solution)/shard_map/ppermute | solution.py:34
  43.6 1.2 %collective-permute-done.10 = bf16[256,1152]{1,0:T(8,128)(2,1)S(1)} collective-permute-done((bf16[256,1152]{1,0:T(8,128)(2,1)S(1)}, bf16[256,1152]{1,0:T(8,128)(2,1)S(1)}, u32[]{:S(2)}, u32[]{:S(2)}) %collective-permute-start.10) | collective-permute-done | bytes 589856 | tf_op jit(solution)/shard_map/ppermute | solution.py:34
  44.7 0.6 collective-permute-done.11
  46.0 2.0 %multiply_convert_fusion.1 = bf16[512,1024]{1,0:T(8,128)(2,1)S(1)} fusion(bf16[512,1152]{1,0:T(8,128)(2,1)S(1)} %get-tuple-element.69, bf16[1024,1152]{1,0:T(8,128)(2,1)S(1)} %constant_dynamic-update-slice_fusion.5, s32[1024]{0:T(1024)S(1)} %iota_add_fusion, f32[]{:T(128)} %bitcast.13, f32[]{:T(128)} %bitcast.12, pred[1024]{0:T(1024)(128)(4,1)S(1)} %get-tuple-element.81, ...), kind=kOutput, calls=%fused_computation.6 | convolution fusion | flops 1214251008 | bytes 4593672 | tf_op jit(solution)/shard_map/dot_general | solution.py:93
  48.0 0.6 collective-permute-done.12
  48.5 1.8 %multiply_convert_fusion = bf16[512,1024]{1,0:T(8,128)(2,1)S(1)} fusion(bf16[512,1152]{1,0:T(8,128)(2,1)S(1)} %collective-permute-done.12, bf16[1024,1152]{1,0:T(8,128)(2,1)S(1)} %constant_dynamic-update-slice_fusion.5, f32[]{:T(128)} %bitcast.14, f32[]{:T(128)} %bitcast.11), kind=kOutput, calls=%fused_computation.5 | convolution fusion | flops 1211629568 | bytes 4587528 | tf_op jit(solution)/shard_map/dot_general | solution.py:93
  50.4 1.5 %fusion.33 = f32[512,1152]{1,0:T(8,128)S(1)} fusion(bf16[512,1024]{1,0:T(8,128)(2,1)S(1)} %multiply_convert_fusion, bf16[1024,1152]{1,0:T(8,128)(2,1)S(1)} %constant_dynamic-update-slice_fusion.5), kind=kOutput, calls=%fused_computation.97 | convolution fusion | flops 1207959552 | bytes 5767168 | tf_op jit(solution)/shard_map/dot_general | solution.py:125
  52.3 3.0 %fusion = f32[1024,1152]{1,0:T(8,128)S(1)} fusion(bf16[1024,1152]{1,0:T(8,128)(2,1)S(1)} %constant_dynamic-update-slice_fusion.15, bf16[512,1024]{1,0:T(8,128)(2,1)S(1)} %multiply_convert_fusion, bf16[512,1024]{1,0:T(8,128)(2,1)S(1)} %multiply_convert_fusion.1), kind=kOutput, calls=%fused_computation.1 | convolution fusion | flops 2420113408 | bytes 9175040 | tf_op jit(solution)/shard_map/dot_general | solution.py:129
  55.5 2.8 %collective-permute-start.13 = (f16[256,1152]{1,0:T(8,128)(2,1)S(1)}, f16[256,1152]{1,0:T(8,128)(2,1)S(1)}, u32[]{:S(2)}, u32[]{:S(2)}) collective-permute-start(f16[256,1152]{1,0:T(8,128)(2,1)S(1)} %get-tuple-element.67), channel_id=1, source_target_pairs={{0,48},{1,49},{2,50},{3,51},{4,52},{5,53},{6,54},{7,55},{8,56},{9,... | collective-permute-start | bytes 1769480 | tf_op jit(solution)/shard_map/ppermute | solution.py:34
  58.4 1.5 %collective-permute-start.14 = (f16[256,1152]{1,0:T(8,128)(2,1)S(1)}, f16[256,1152]{1,0:T(8,128)(2,1)S(1)}, u32[]{:S(2)}, u32[]{:S(2)}) collective-permute-start(f16[256,1152]{1,0:T(8,128)(2,1)S(1)} %get-tuple-element.66), channel_id=1, source_target_pairs={{0,136},{1,137},{2,138},{3,139},{4,140},{5,141},{6,142},{7,143},{8... | collective-permute-start | bytes 1769480 | tf_op jit(solution)/shard_map/ppermute | solution.py:34
  59.9 1.5 %convolution_add_fusion = f32[512,1152]{1,0:T(8,128)S(1)} fusion(f32[512,1152]{1,0:T(8,128)S(1)} %collective-permute-done.15, bf16[512,1024]{1,0:T(8,128)(2,1)S(1)} %multiply_convert_fusion.1, bf16[1024,1152]{1,0:T(8,128)(2,1)S(1)} %constant_dynamic-update-slice_fusion.5), kind=kOutput, calls=%fused_computation | convolution fusion | flops 1208549376 | bytes 8126464 | tf_op jit(solution)/shard_map/dot_general | solution.py:136
  61.5 1.7 %collective-permute-start.16 = (f16[128,1152]{1,0:T(8,128)(2,1)S(1)}, f16[128,1152]{1,0:T(8,128)(2,1)S(1)}, u32[]{:S(2)}, u32[]{:S(2)}) collective-permute-start(f16[128,1152]{1,0:T(8,128)(2,1)S(1)} %fusion.10), channel_id=1, source_target_pairs={{0,7},{1,2},{2,1},{3,4},{4,3},{5,6},{6,5},{7,0},{8,15},{9,10},{10,... | collective-permute-start | bytes 884744 | tf_op jit(solution)/shard_map/ppermute | solution.py:34
  63.1 3.6 %collective-permute-done.13 = f16[256,1152]{1,0:T(8,128)(2,1)S(1)} collective-permute-done((f16[256,1152]{1,0:T(8,128)(2,1)S(1)}, f16[256,1152]{1,0:T(8,128)(2,1)S(1)}, u32[]{:S(2)}, u32[]{:S(2)}) %collective-permute-start.13) | collective-permute-done | bytes 589856 | tf_op jit(solution)/shard_map/ppermute | solution.py:34
  66.7 2.7 %collective-permute-done.14 = f16[256,1152]{1,0:T(8,128)(2,1)S(1)} collective-permute-done((f16[256,1152]{1,0:T(8,128)(2,1)S(1)}, f16[256,1152]{1,0:T(8,128)(2,1)S(1)}, u32[]{:S(2)}, u32[]{:S(2)}) %collective-permute-start.14) | collective-permute-done | bytes 589856 | tf_op jit(solution)/shard_map/ppermute | solution.py:34
  69.8 1.2 %collective-permute-start.17 = (f16[128,1152]{1,0:T(8,128)(2,1)S(1)}, f16[128,1152]{1,0:T(8,128)(2,1)S(1)}, u32[]{:S(2)}, u32[]{:S(2)}) collective-permute-start(f16[128,1152]{1,0:T(8,128)(2,1)S(1)} %fusion.9), channel_id=1, source_target_pairs={{0,16},{1,17},{2,18},{3,19},{4,20},{5,21},{6,22},{7,23},{8,24},{9,... | collective-permute-start | bytes 884744 | tf_op jit(solution)/shard_map/ppermute | solution.py:34
  71.5 3.1 %collective-permute-start.19 = (f16[128,1152]{1,0:T(8,128)(2,1)S(1)}, f16[128,1152]{1,0:T(8,128)(2,1)S(1)}, u32[]{:S(2)}, u32[]{:S(2)}) collective-permute-start(f16[128,1152]{1,0:T(8,128)(2,1)S(1)} %fusion.7), channel_id=1, source_target_pairs={{0,1},{1,0},{2,3},{3,2},{4,5},{5,4},{6,7},{7,6},{8,9},{9,8},{10,11... | collective-permute-start | bytes 884744 | tf_op jit(solution)/shard_map/ppermute | solution.py:34
  74.6 2.1 %collective-permute-done.17 = f16[128,1152]{1,0:T(8,128)(2,1)S(1)} collective-permute-done((f16[128,1152]{1,0:T(8,128)(2,1)S(1)}, f16[128,1152]{1,0:T(8,128)(2,1)S(1)}, u32[]{:S(2)}, u32[]{:S(2)}) %collective-permute-start.17) | collective-permute-done | bytes 294944 | tf_op jit(solution)/shard_map/ppermute | solution.py:34
  76.6 1.5 %collective-permute-done.18 = f16[128,1152]{1,0:T(8,128)(2,1)S(1)} collective-permute-done((f16[128,1152]{1,0:T(8,128)(2,1)S(1)}, f16[128,1152]{1,0:T(8,128)(2,1)S(1)}, u32[]{:S(2)}, u32[]{:S(2)}) %collective-permute-start.18) | collective-permute-done | bytes 294944 | tf_op jit(solution)/shard_map/ppermute | solution.py:34
  78.1 1.2 %collective-permute-done.19 = f16[128,1152]{1,0:T(8,128)(2,1)S(1)} collective-permute-done((f16[128,1152]{1,0:T(8,128)(2,1)S(1)}, f16[128,1152]{1,0:T(8,128)(2,1)S(1)}, u32[]{:S(2)}, u32[]{:S(2)}) %collective-permute-start.19) | collective-permute-done | bytes 294944 | tf_op jit(solution)/shard_map/ppermute | solution.py:34
  79.5 1.3 %collective-permute-start.20 = (f16[64,1152]{1,0:T(8,128)(2,1)S(1)}, f16[64,1152]{1,0:T(8,128)(2,1)S(1)}, u32[]{:S(2)}, u32[]{:S(2)}) collective-permute-start(f16[64,1152]{1,0:T(8,128)(2,1)S(1)} %fusion.27), channel_id=1, source_target_pairs={{0,136},{1,137},{2,138},{3,139},{4,140},{5,141},{6,142},{7,143},{8... | collective-permute-start | bytes 442376 | tf_op jit(solution)/shard_map/ppermute | solution.py:34
  80.9 1.3 %collective-permute-start.22 = (f16[128,1152]{1,0:T(8,128)(2,1)S(1)}, f16[128,1152]{1,0:T(8,128)(2,1)S(1)}, u32[]{:S(2)}, u32[]{:S(2)}) collective-permute-start(f16[128,1152]{1,0:T(8,128)(2,1)S(1)} %fusion.5), channel_id=1, source_target_pairs={{0,7},{1,2},{2,1},{3,4},{4,3},{5,6},{6,5},{7,0},{8,15},{9,10},{10,... | collective-permute-start | bytes 884744 | tf_op jit(solution)/shard_map/ppermute | solution.py:34
  82.2 0.8 collective-permute-start.21
  83.0 2.9 %collective-permute-done.20 = f16[64,1152]{1,0:T(8,128)(2,1)S(1)} collective-permute-done((f16[64,1152]{1,0:T(8,128)(2,1)S(1)}, f16[64,1152]{1,0:T(8,128)(2,1)S(1)}, u32[]{:S(2)}, u32[]{:S(2)}) %collective-permute-start.20) | collective-permute-done | bytes 147488 | tf_op jit(solution)/shard_map/ppermute | solution.py:34
  85.9 2.7 %collective-permute-done.21 = f16[64,1152]{1,0:T(8,128)(2,1)S(1)} collective-permute-done((f16[64,1152]{1,0:T(8,128)(2,1)S(1)}, f16[64,1152]{1,0:T(8,128)(2,1)S(1)}, u32[]{:S(2)}, u32[]{:S(2)}) %collective-permute-start.21) | collective-permute-done | bytes 147488 | tf_op jit(solution)/shard_map/ppermute | solution.py:34
  89.1 1.5 %collective-permute-start.23 = (f16[32,1152]{1,0:T(8,128)(2,1)S(1)}, f16[32,1152]{1,0:T(8,128)(2,1)S(1)}, u32[]{:S(2)}, u32[]{:S(2)}) collective-permute-start(f16[32,1152]{1,0:T(8,128)(2,1)S(1)} %fusion.29), channel_id=1, source_target_pairs={{0,8},{1,9},{2,10},{3,11},{4,12},{5,13},{6,14},{7,15},{8,0},{9,1},... | collective-permute-start | bytes 221192 | tf_op jit(solution)/shard_map/ppermute | solution.py:34
  90.7 1.6 %collective-permute-start.25 = (f16[64,1152]{1,0:T(8,128)(2,1)S(1)}, f16[64,1152]{1,0:T(8,128)(2,1)S(1)}, u32[]{:S(2)}, u32[]{:S(2)}) collective-permute-start(f16[64,1152]{1,0:T(8,128)(2,1)S(1)} %fusion.25), channel_id=1, source_target_pairs={{0,1},{1,0},{2,3},{3,2},{4,5},{5,4},{6,7},{7,6},{8,9},{9,8},{10,11... | collective-permute-start | bytes 442376 | tf_op jit(solution)/shard_map/ppermute | solution.py:34
  92.9 0.6 collective-permute-done.23
  93.5 3.3 %collective-permute-done.24 = f16[32,1152]{1,0:T(8,128)(2,1)S(1)} collective-permute-done((f16[32,1152]{1,0:T(8,128)(2,1)S(1)}, f16[32,1152]{1,0:T(8,128)(2,1)S(1)}, u32[]{:S(2)}, u32[]{:S(2)}) %collective-permute-start.24) | collective-permute-done | bytes 73760 | tf_op jit(solution)/shard_map/ppermute | solution.py:34
  97.0 0.8 fusion.23
  98.1 0.8 fusion.19
  (66 shorter events, 5.1 us)
Async XLA Ops:
  2.7 10.0 %collective-permute-start = (bf16[64,1152]{1,0:T(8,128)(2,1)S(1)}, bf16[64,1152]{1,0:T(8,128)(2,1)S(1)}, u32[]{:S(2)}, u32[]{:S(2)}) collective-permute-start(bf16[64,1152]{1,0:T(8,128)(2,1)S(1)} %get-tuple-element.63), channel_id=1, source_target_pairs={{0,1},{1,0},{2,3},{3,2},{4,5},{5,4},{6,7},{7,6},{8,9},{9,8},{10,11... | collective-permute-start | bytes 442376 | tf_op jit(solution)/shard_map/ppermute | solution.py:34
  6.8 4.4 %collective-permute-start.1 = (bf16[32,1152]{1,0:T(8,128)(2,1)S(1)}, bf16[32,1152]{1,0:T(8,128)(2,1)S(1)}, u32[]{:S(2)}, u32[]{:S(2)}) collective-permute-start(bf16[32,1152]{1,0:T(8,128)(2,1)S(1)} %get-tuple-element.78), channel_id=1, source_target_pairs={{0,8},{1,9},{2,10},{3,11},{4,12},{5,13},{6,14},{7,15},{8,0},{9,1},... | collective-permute-start | bytes 221192 | tf_op jit(solution)/shard_map/ppermute | solution.py:34
  8.4 4.4 %collective-permute-start.2 = (bf16[32,1152]{1,0:T(8,128)(2,1)S(1)}, bf16[32,1152]{1,0:T(8,128)(2,1)S(1)}, u32[]{:S(2)}, u32[]{:S(2)}) collective-permute-start(bf16[32,1152]{1,0:T(8,128)(2,1)S(1)} %get-tuple-element.77), channel_id=1, source_target_pairs={{0,16},{1,17},{2,18},{3,19},{4,20},{5,21},{6,22},{7,23},{8,24},{9,... | collective-permute-start | bytes 221192 | tf_op jit(solution)/shard_map/ppermute | solution.py:34
  12.8 13.7 %collective-permute-start.3 = (bf16[128,1152]{1,0:T(8,128)(2,1)S(1)}, bf16[128,1152]{1,0:T(8,128)(2,1)S(1)}, u32[]{:S(2)}, u32[]{:S(2)}) collective-permute-start(bf16[128,1152]{1,0:T(8,128)(2,1)S(1)} %pad_maximum_fusion.2), channel_id=1, source_target_pairs={{0,7},{1,2},{2,1},{3,4},{4,3},{5,6},{6,5},{7,0},{8,15},{9,10},{10,... | collective-permute-start | bytes 884744 | tf_op jit(solution)/shard_map/ppermute | solution.py:34
  17.8 6.4 %collective-permute-start.4 = (bf16[64,1152]{1,0:T(8,128)(2,1)S(1)}, bf16[64,1152]{1,0:T(8,128)(2,1)S(1)}, u32[]{:S(2)}, u32[]{:S(2)}) collective-permute-start(bf16[64,1152]{1,0:T(8,128)(2,1)S(1)} %pad_maximum_fusion.6), channel_id=1, source_target_pairs={{0,136},{1,137},{2,138},{3,139},{4,140},{5,141},{6,142},{7,143},{8... | collective-permute-start | bytes 442376 | tf_op jit(solution)/shard_map/ppermute | solution.py:34
  20.0 6.4 %collective-permute-start.5 = (bf16[64,1152]{1,0:T(8,128)(2,1)S(1)}, bf16[64,1152]{1,0:T(8,128)(2,1)S(1)}, u32[]{:S(2)}, u32[]{:S(2)}) collective-permute-start(bf16[64,1152]{1,0:T(8,128)(2,1)S(1)} %pad_maximum_fusion.7), channel_id=1, source_target_pairs={{0,48},{1,49},{2,50},{3,51},{4,52},{5,53},{6,54},{7,55},{8,56},{9,... | collective-permute-start | bytes 442376 | tf_op jit(solution)/shard_map/ppermute | solution.py:34
  26.5 6.7 %collective-permute-start.6 = (bf16[128,1152]{1,0:T(8,128)(2,1)S(1)}, bf16[128,1152]{1,0:T(8,128)(2,1)S(1)}, u32[]{:S(2)}, u32[]{:S(2)}) collective-permute-start(bf16[128,1152]{1,0:T(8,128)(2,1)S(1)} %collective-permute-done.3), channel_id=1, source_target_pairs={{0,1},{1,0},{2,3},{3,2},{4,5},{5,4},{6,7},{7,6},{8,9},{9,8},{10,11... | collective-permute-start | bytes 884744 | tf_op jit(solution)/shard_map/ppermute | solution.py:34
  26.5 6.9 %collective-permute-start.7 = (bf16[128,1152]{1,0:T(8,128)(2,1)S(1)}, bf16[128,1152]{1,0:T(8,128)(2,1)S(1)}, u32[]{:S(2)}, u32[]{:S(2)}) collective-permute-start(bf16[128,1152]{1,0:T(8,128)(2,1)S(1)} %pad_maximum_fusion.3), channel_id=1, source_target_pairs={{0,16},{1,17},{2,18},{3,19},{4,20},{5,21},{6,22},{7,23},{8,24},{9,... | collective-permute-start | bytes 884744 | tf_op jit(solution)/shard_map/ppermute | solution.py:34
  26.6 6.9 %collective-permute-start.8 = (bf16[128,1152]{1,0:T(8,128)(2,1)S(1)}, bf16[128,1152]{1,0:T(8,128)(2,1)S(1)}, u32[]{:S(2)}, u32[]{:S(2)}) collective-permute-start(bf16[128,1152]{1,0:T(8,128)(2,1)S(1)} %pad_maximum_fusion.4), channel_id=1, source_target_pairs={{0,8},{1,9},{2,10},{3,11},{4,12},{5,13},{6,14},{7,15},{8,0},{9,1},... | collective-permute-start | bytes 884744 | tf_op jit(solution)/shard_map/ppermute | solution.py:34
  33.6 11.2 %collective-permute-start.10 = (bf16[256,1152]{1,0:T(8,128)(2,1)S(1)}, bf16[256,1152]{1,0:T(8,128)(2,1)S(1)}, u32[]{:S(2)}, u32[]{:S(2)}) collective-permute-start(bf16[256,1152]{1,0:T(8,128)(2,1)S(1)} %pad_maximum_fusion), channel_id=1, source_target_pairs={{0,48},{1,49},{2,50},{3,51},{4,52},{5,53},{6,54},{7,55},{8,56},{9,... | collective-permute-start | bytes 1769480 | tf_op jit(solution)/shard_map/ppermute | solution.py:34
  34.2 11.2 %collective-permute-start.11 = (bf16[256,1152]{1,0:T(8,128)(2,1)S(1)}, bf16[256,1152]{1,0:T(8,128)(2,1)S(1)}, u32[]{:S(2)}, u32[]{:S(2)}) collective-permute-start(bf16[256,1152]{1,0:T(8,128)(2,1)S(1)} %pad_maximum_fusion.1), channel_id=1, source_target_pairs={{0,136},{1,137},{2,138},{3,139},{4,140},{5,141},{6,142},{7,143},{8... | collective-permute-start | bytes 1769480 | tf_op jit(solution)/shard_map/ppermute | solution.py:34
  35.5 8.0 %collective-permute-start.9 = (bf16[128,1152]{1,0:T(8,128)(2,1)S(1)}, bf16[128,1152]{1,0:T(8,128)(2,1)S(1)}, u32[]{:S(2)}, u32[]{:S(2)}) collective-permute-start(bf16[128,1152]{1,0:T(8,128)(2,1)S(1)} %collective-permute-done.6), channel_id=1, source_target_pairs={{0,7},{1,2},{2,1},{3,4},{4,3},{5,6},{6,5},{7,0},{8,15},{9,10},{10,... | collective-permute-start | bytes 884744 | tf_op jit(solution)/shard_map/ppermute | solution.py:34
  45.4 3.1 %collective-permute-start.12 = (bf16[512,1152]{1,0:T(8,128)(2,1)S(1)}, bf16[512,1152]{1,0:T(8,128)(2,1)S(1)}, u32[]{:S(2)}, u32[]{:S(2)}) collective-permute-start(bf16[512,1152]{1,0:T(8,128)(2,1)S(1)} %get-tuple-element.69), channel_id=1, source_target_pairs={{0,64},{1,65},{2,66},{3,67},{4,68},{5,69},{6,70},{7,71},{8,72},{9,... | collective-permute-start | bytes 3538952 | tf_op jit(solution)/shard_map/ppermute | solution.py:34
  51.9 8.0 %collective-permute-start.15 = (f32[512,1152]{1,0:T(8,128)S(1)}, f32[512,1152]{1,0:T(8,128)S(1)}, u32[]{:S(2)}, u32[]{:S(2)}) collective-permute-start(f32[512,1152]{1,0:T(8,128)S(1)} %fusion.33), channel_id=1, source_target_pairs={{0,64},{1,65},{2,66},{3,67},{4,68},{5,69},{6,70},{7,71},{8,72},{9,... | collective-permute-start | bytes 7077896 | tf_op jit(solution)/shard_map/ppermute | solution.py:34
  55.5 11.2 %collective-permute-start.13 = (f16[256,1152]{1,0:T(8,128)(2,1)S(1)}, f16[256,1152]{1,0:T(8,128)(2,1)S(1)}, u32[]{:S(2)}, u32[]{:S(2)}) collective-permute-start(f16[256,1152]{1,0:T(8,128)(2,1)S(1)} %get-tuple-element.67), channel_id=1, source_target_pairs={{0,48},{1,49},{2,50},{3,51},{4,52},{5,53},{6,54},{7,55},{8,56},{9,... | collective-permute-start | bytes 1769480 | tf_op jit(solution)/shard_map/ppermute | solution.py:34
  58.4 11.1 %collective-permute-start.14 = (f16[256,1152]{1,0:T(8,128)(2,1)S(1)}, f16[256,1152]{1,0:T(8,128)(2,1)S(1)}, u32[]{:S(2)}, u32[]{:S(2)}) collective-permute-start(f16[256,1152]{1,0:T(8,128)(2,1)S(1)} %get-tuple-element.66), channel_id=1, source_target_pairs={{0,136},{1,137},{2,138},{3,139},{4,140},{5,141},{6,142},{7,143},{8... | collective-permute-start | bytes 1769480 | tf_op jit(solution)/shard_map/ppermute | solution.py:34
  61.5 8.0 %collective-permute-start.16 = (f16[128,1152]{1,0:T(8,128)(2,1)S(1)}, f16[128,1152]{1,0:T(8,128)(2,1)S(1)}, u32[]{:S(2)}, u32[]{:S(2)}) collective-permute-start(f16[128,1152]{1,0:T(8,128)(2,1)S(1)} %fusion.10), channel_id=1, source_target_pairs={{0,7},{1,2},{2,1},{3,4},{4,3},{5,6},{6,5},{7,0},{8,15},{9,10},{10,... | collective-permute-start | bytes 884744 | tf_op jit(solution)/shard_map/ppermute | solution.py:34
  69.8 6.8 %collective-permute-start.17 = (f16[128,1152]{1,0:T(8,128)(2,1)S(1)}, f16[128,1152]{1,0:T(8,128)(2,1)S(1)}, u32[]{:S(2)}, u32[]{:S(2)}) collective-permute-start(f16[128,1152]{1,0:T(8,128)(2,1)S(1)} %fusion.9), channel_id=1, source_target_pairs={{0,16},{1,17},{2,18},{3,19},{4,20},{5,21},{6,22},{7,23},{8,24},{9,... | collective-permute-start | bytes 884744 | tf_op jit(solution)/shard_map/ppermute | solution.py:34
  71.0 7.0 %collective-permute-start.18 = (f16[128,1152]{1,0:T(8,128)(2,1)S(1)}, f16[128,1152]{1,0:T(8,128)(2,1)S(1)}, u32[]{:S(2)}, u32[]{:S(2)}) collective-permute-start(f16[128,1152]{1,0:T(8,128)(2,1)S(1)} %fusion.8), channel_id=1, source_target_pairs={{0,8},{1,9},{2,10},{3,11},{4,12},{5,13},{6,14},{7,15},{8,0},{9,1},... | collective-permute-start | bytes 884744 | tf_op jit(solution)/shard_map/ppermute | solution.py:34
  71.5 7.8 %collective-permute-start.19 = (f16[128,1152]{1,0:T(8,128)(2,1)S(1)}, f16[128,1152]{1,0:T(8,128)(2,1)S(1)}, u32[]{:S(2)}, u32[]{:S(2)}) collective-permute-start(f16[128,1152]{1,0:T(8,128)(2,1)S(1)} %fusion.7), channel_id=1, source_target_pairs={{0,1},{1,0},{2,3},{3,2},{4,5},{5,4},{6,7},{7,6},{8,9},{9,8},{10,11... | collective-permute-start | bytes 884744 | tf_op jit(solution)/shard_map/ppermute | solution.py:34
  79.5 6.4 %collective-permute-start.20 = (f16[64,1152]{1,0:T(8,128)(2,1)S(1)}, f16[64,1152]{1,0:T(8,128)(2,1)S(1)}, u32[]{:S(2)}, u32[]{:S(2)}) collective-permute-start(f16[64,1152]{1,0:T(8,128)(2,1)S(1)} %fusion.27), channel_id=1, source_target_pairs={{0,136},{1,137},{2,138},{3,139},{4,140},{5,141},{6,142},{7,143},{8... | collective-permute-start | bytes 442376 | tf_op jit(solution)/shard_map/ppermute | solution.py:34
  80.9 8.0 %collective-permute-start.22 = (f16[128,1152]{1,0:T(8,128)(2,1)S(1)}, f16[128,1152]{1,0:T(8,128)(2,1)S(1)}, u32[]{:S(2)}, u32[]{:S(2)}) collective-permute-start(f16[128,1152]{1,0:T(8,128)(2,1)S(1)} %fusion.5), channel_id=1, source_target_pairs={{0,7},{1,2},{2,1},{3,4},{4,3},{5,6},{6,5},{7,0},{8,15},{9,10},{10,... | collective-permute-start | bytes 884744 | tf_op jit(solution)/shard_map/ppermute | solution.py:34
  82.2 6.4 %collective-permute-start.21 = (f16[64,1152]{1,0:T(8,128)(2,1)S(1)}, f16[64,1152]{1,0:T(8,128)(2,1)S(1)}, u32[]{:S(2)}, u32[]{:S(2)}) collective-permute-start(f16[64,1152]{1,0:T(8,128)(2,1)S(1)} %fusion.26), channel_id=1, source_target_pairs={{0,48},{1,49},{2,50},{3,51},{4,52},{5,53},{6,54},{7,55},{8,56},{9,... | collective-permute-start | bytes 442376 | tf_op jit(solution)/shard_map/ppermute | solution.py:34
  89.0 7.8 %copy-start = (bf16[64,1152]{1,0:T(8,128)(2,1)S(1)}, bf16[64,1152]{1,0:T(8,128)(2,1)}, u32[]{:S(2)}) copy-start(bf16[64,1152]{1,0:T(8,128)(2,1)} %param.4) | copy-start | bytes 442372
  89.0 8.9 %copy-start.1 = (bf16[64,1152]{1,0:T(8,128)(2,1)S(1)}, bf16[64,1152]{1,0:T(8,128)(2,1)}, u32[]{:S(2)}) copy-start(bf16[64,1152]{1,0:T(8,128)(2,1)} %param.5) | copy-start | bytes 442372
  89.1 4.4 %collective-permute-start.23 = (f16[32,1152]{1,0:T(8,128)(2,1)S(1)}, f16[32,1152]{1,0:T(8,128)(2,1)S(1)}, u32[]{:S(2)}, u32[]{:S(2)}) collective-permute-start(f16[32,1152]{1,0:T(8,128)(2,1)S(1)} %fusion.29), channel_id=1, source_target_pairs={{0,8},{1,9},{2,10},{3,11},{4,12},{5,13},{6,14},{7,15},{8,0},{9,1},... | collective-permute-start | bytes 221192 | tf_op jit(solution)/shard_map/ppermute | solution.py:34
  90.7 6.1 %collective-permute-start.25 = (f16[64,1152]{1,0:T(8,128)(2,1)S(1)}, f16[64,1152]{1,0:T(8,128)(2,1)S(1)}, u32[]{:S(2)}, u32[]{:S(2)}) collective-permute-start(f16[64,1152]{1,0:T(8,128)(2,1)S(1)} %fusion.25), channel_id=1, source_target_pairs={{0,1},{1,0},{2,3},{3,2},{4,5},{5,4},{6,7},{7,6},{8,9},{9,8},{10,11... | collective-permute-start | bytes 442376 | tf_op jit(solution)/shard_map/ppermute | solution.py:34
  92.3 4.4 %collective-permute-start.24 = (f16[32,1152]{1,0:T(8,128)(2,1)S(1)}, f16[32,1152]{1,0:T(8,128)(2,1)S(1)}, u32[]{:S(2)}, u32[]{:S(2)}) collective-permute-start(f16[32,1152]{1,0:T(8,128)(2,1)S(1)} %fusion.28), channel_id=1, source_target_pairs={{0,16},{1,17},{2,18},{3,19},{4,20},{5,21},{6,22},{7,23},{8,24},{9,... | collective-permute-start | bytes 221192 | tf_op jit(solution)/shard_map/ppermute | solution.py:34

commit v3 on v1

v3 whole, which is shorter than its diff:
```python
import jax
import jax.numpy as jnp
import numpy as np
from jax import lax
from jax.experimental import pallas as pl
from jax.experimental.pallas import tpu as pltpu
from jax.sharding import PartitionSpec as P

epsilon = 1e-06

SHAPE = (2, 2, 4, 2, 8)
AXES = ("group", "blk")
SHRINK = 0.25
SMALL = pltpu.CompilerParams(vmem_limit_bytes=4 * 2**20)


def neighbour_pairs(axis, phase):
    perm = []
    for i, (xh, core, y, xl, z) in enumerate(np.ndindex(*SHAPE)):
        at = {"x": 2 * xh + xl, "y": y, "z": z}
        n = {"x": 4, "y": 4, "z": 8}[axis]
        p = at[axis]
        if (phase + core) % 2 == 0:
            at[axis] = p ^ 1
        else:
            at[axis] = (p + 1) % n if p % 2 else (p - 1) % n
        there = (at["x"] // 2, core, at["y"], at["x"] % 2, at["z"])
        perm.append((i, int(np.ravel_multi_index(there, SHAPE))))
    return perm


PX, PY, PZ = ([neighbour_pairs(axis, 0), neighbour_pairs(axis, 1)] for axis in "xyz")
PC = [(i, i ^ 64) for i in range(256)]


def swap(array, perm):
    return lax.ppermute(array, AXES, perm)


def join(*arrays):
    return jnp.concatenate(arrays, axis=0)


def step(*arrays):
    return lax.optimization_barrier(arrays)


def unit_of(embedding):
    values = embedding.astype(jnp.float32)
    inverse = lax.rsqrt(jnp.sum(values * values, axis=-1, keepdims=True) + epsilon)
    return values * inverse, inverse


def low_kernel(rows, low):
    low[...] = unit_of(rows[...])[0].astype(jnp.bfloat16)


def low_rows(rows):
    out = jax.ShapeDtypeStruct(rows.shape, jnp.bfloat16)
    return pl.pallas_call(low_kernel, out_shape=out, compiler_params=SMALL)(rows)


def shrunk(part):
    return (part * SHRINK).astype(jnp.float16)


def grown(part):
    return part.astype(jnp.float32) * (1 / SHRINK)


def grads_kernel(images, texts, image_sum, text_sum, image_out, text_out):
    for rows, summed, out in ((images, image_sum, image_out), (texts, text_sum, text_out)):
        unit, inverse = unit_of(rows[...])
        total = summed[...]
        along = jnp.sum(unit * total, axis=-1, keepdims=True)
        out[...] = (total - unit * along) * inverse


def grads(images, texts, *sums):
    out = jax.ShapeDtypeStruct(images.shape, jnp.float32)
    return pl.pallas_call(grads_kernel, out_shape=(out, out), compiler_params=SMALL)(
        images, texts, *sums
    )


def weights_of(texts, images, factor, offset, own=None):
    product = lax.dot_general(
        texts, images, (((1,), (1,)), ((), ())), preferred_element_type=jnp.float32
    )
    value = jax.nn.sigmoid(factor * product + offset)
    if own is not None:
        row = lax.broadcasted_iota(jnp.int32, value.shape, 0)
        col = lax.broadcasted_iota(jnp.int32, value.shape, 1)
        half, cols = own // 2, value.shape[1] // 2
        image = jnp.where(col < cols, col, col - cols + half)
        mine = (jnp.where(col < cols, col, col - cols) < half) & (row == image)
        value = value - mine.astype(jnp.float32)
    return (factor * value).astype(jnp.bfloat16)


def dot(a, b):
    return jnp.dot(a, b, preferred_element_type=jnp.float32)


def dot_t(a, b):
    return lax.dot_general(a, b, (((0,), (0,)), ((), ())), preferred_element_type=jnp.float32)


def body(images, texts, logit_scale, bias):
    factor = logit_scale[0]
    offset = bias[0]
    n = images.shape[0]
    text_low, image_low = low_rows(texts), low_rows(images)

    h = n // 2
    a, b = image_low[:h], image_low[h:]
    parts = [text_low]
    for k, (pa, pb) in enumerate(zip(PX + PY, PY + PX)):
        t = join(*parts) if k < 2 else parts[-1]
        if k == 2:
            own_a = join(*parts)
            other_a = swap(own_a, PC)
        if k == 3:
            first = join(a, b)
            own_0 = join(own_a, parts[3])
        if k < 3:
            got_t, got_a, got_b = step(swap(t, PZ[k % 2]), swap(a, pa), swap(b, pb))
        else:
            got_a, got_b, got_t = step(swap(a, pa), swap(b, pb), swap(t, PZ[k % 2]))
        parts.append(got_t)
        if k < 3:
            a, b = join(a, got_a), join(b, got_b)

    first_own_0 = weights_of(own_0, first, factor, offset, n)
    first_other_a = weights_of(other_a, first, factor, offset)
    text_own_0 = dot(first_own_0, first)
    text_other_a = dot(first_other_a, first)
    sum_first = dot_t(first_own_0, own_0) + dot_t(first_other_a, other_a)

    h, m, q = 4 * n, 2 * n, 6 * n
    second = join(got_a, got_b)
    own_1 = parts[4]
    other_b = swap(join(parts[3], own_1), PC)
    own = join(own_0, own_1)
    second_own = weights_of(own, second, factor, offset)
    sum_second = dot_t(second_own, own)
    sum_second, second_own, other_b, other_a, text_other_a = lax.optimization_barrier(
        (sum_second, second_own, other_b, other_a, text_other_a)
    )
    other = join(other_a, other_b)
    second_other = weights_of(other, second, factor, offset)
    sum_second = shrunk(sum_second + dot_t(second_other, other))

    first_other_1 = weights_of(other_b[m:], first, factor, offset)
    late_other = shrunk(dot(first_other_1, first) + dot(second_other[q:], second))
    sum_second, late_other, second_own, second_other, first_other_1, sum_first, other_b = (
        lax.optimization_barrier(
            (sum_second, late_other, second_own, second_other, first_other_1, sum_first, other_b)
        )
    )
    got_late = swap(late_other, PC)
    got_a = swap(sum_second[:h], PY[1])
    got_b = swap(sum_second[h:], PX[1])
    first_own_1 = weights_of(own_1, first, factor, offset)
    late = dot(first_own_1, first) + dot(second_own[q:], second) + grown(got_late)
    late, first_own_1, first_other_1, text_own_0, text_other_a, second_own, second_other, sum_first, other_b = (
        lax.optimization_barrier(
            (
                shrunk(late),
                first_own_1,
                first_other_1,
                text_own_0,
                text_other_a,
                second_own,
                second_other,
                sum_first,
                other_b,
            )
        )
    )
    got_t = swap(late, PZ[1])

    first_other_0 = weights_of(other_b[:m], first, factor, offset)
    early_other = join(text_other_a, dot(first_other_0, first)) + dot(second_other[:q], second)
    got_early = swap(shrunk(early_other), PC)
    early = text_own_0 + dot(second_own[:q], second) + grown(got_early)
    sum_first = sum_first + dot_t(
        join(first_own_1, first_other_0, first_other_1), join(own_1, other_b)
    )

    ts = [early[i * m : (i + 1) * m] for i in range(3)]
    a, b = sum_first[:h], sum_first[h:]
    got_t, got_a, got_b = step(got_t, got_a, got_b)
    for k in (2, 1, 0):
        a, b = a + grown(got_a), b + grown(got_b)
        ts[k] = ts[k] + grown(got_t)
        q = a.shape[0] // 2
        out = ts[k] if k else ts[0][n:]
        got_a, got_b, got_t = step(
            swap(shrunk(a[q:]), (PX + PY)[k]),
            swap(shrunk(b[q:]), (PY + PX)[k]),
            swap(shrunk(out), PZ[k % 2]),
        )
        a, b = a[:q], b[:q]
    image_sum = join(a + grown(got_a), b + grown(got_b))
    return grads(images, texts, image_sum, ts[0][:n] + grown(got_t))


def solution(mesh):
    return jax.shard_map(
        body,
        mesh=mesh,
        in_specs=(P(("group", "blk"), None), P(("group", "blk"), None), P(), P()),
        out_specs=(P(("group", "blk"), None), P(("group", "blk"), None)),
        check_vma=False,
    )
```

time: 134 us -> 94.4 us (0.70)
  waiting for transfers between devices: 70.3 us -> 37.1 us
  starting transfers between devices: 42.5 us -> 35.2 us
  other arithmetic: 8 us -> 1.78 us
  matrix products: 10 us -> 13.5 us
  local copies, waits for them, and re-layouts: 0.86 us -> 2.55 us
    ppermute x26 -> x28, waiting for transfers between devices: 70.3 us -> 37.1 us  [swap(): return lax.ppermute(array, AXES, perm)]
    ppermute x26 -> x28, starting transfers between devices: 42.5 us -> 35.2 us  [swap(): return lax.ppermute(array, AXES, perm)]
    dot_general x3 -> x21, matrix products: 10 us -> 13.5 us  [the longest x7 5.24 us: weights_of(): lax.dot_general(texts, images, (((1,), (1,)), ((), ())), preferred_elemen...]
    reduce_sum x4 -> x0, other arithmetic: 2.49 us -> none  [the longest x2 2.08 us: normalize(): jnp.sum(values * values, axis=-1, keepdims=True) + epsilon]
    unnamed x16 -> x21, local copies, waits for them, and re-layouts: 0.39 us -> 2.14 us
    mul x2 -> x0, other arithmetic: 1.69 us -> none  [unit_grad(): (grad_sum - unit_vec * jnp.sum(unit_vec * grad_sum, axis=-1, keepdims=Tru...]
  transfers between devices with their start and end apart: 26 -> 28, of which waited for: 14 -> 19; matrix products, arithmetic and copies ran while one was open for 6% -> 13% of each run, Pallas kernels for 0% -> 0%
where the time goes in v3:
time: 94.4 us; the launch traced here: 93.9 us
  waiting for transfers between devices  37.1 us (39%)
  starting transfers between devices  35.2 us (37%)
  matrix products  13.5 us (14%)
  local copies, waits for them, and re-layouts  2.55 us (3%)
  between operations  2.43 us (3%)
  other arithmetic  1.78 us (2%)
  Pallas kernels  1.28 us (1%)
    ppermute x28, waiting for transfers between devices, swap(): return lax.ppermute(array, AXES, perm)  37.1 us
    ppermute x28, starting transfers between devices, swap(): return lax.ppermute(array, AXES, perm)  35.2 us
    dot_general x7, matrix products, weights_of(): lax.dot_general(texts, images, (((1,), (1,)), ((), ())), preferred_elemen...  5.24 us
    dot_general x9, matrix products, dot(): return jnp.dot(a, b, preferred_element_type=jnp.float32)  4.3 us
    dot_general x5, matrix products, dot_t(): lax.dot_general(a, b, (((0,), (0,)), ((), ())), preferred_element_type=jn...  3.99 us
    unnamed x21, local copies, waits for them, and re-layouts  2.14 us
  transfers between devices with their start and end apart: 28, of which 19 were waited for; matrix products, arithmetic and copies ran while one was open for 13% of the time, Pallas kernels for 0%

profile of v3, /device:TPU:24, one launch (start us, length us, event | category | flops | bytes accessed | tf_op | source)
XLA Modules:
  0.0 93.9 jit_solution(438753913391018153)
XLA Ops:
  0.6 0.9 copy-done.2
  1.7 2.0 %collective-permute-start = (bf16[64,1152]{1,0:T(8,128)(2,1)S(1)}, bf16[64,1152]{1,0:T(8,128)(2,1)S(1)}, u32[]{:S(2)}, u32[]{:S(2)}) collective-permute-start(bf16[64,1152]{1,0:T(8,128)(2,1)S(1)} %shard_map.60), channel_id=1, source_target_pairs={{0,1},{1,0},{2,3},{3,2},{4,5},{5,4},{6,7},{7,6},{8,9},{9,8},{10,11... | collective-permute-start | bytes 442376 | tf_op jit(solution)/shard_map/ppermute | solution.py:37
  3.7 0.9 copy-done
  4.7 1.6 %collective-permute-start.1 = (bf16[32,1152]{1,0:T(8,128)(2,1)S(1)}, bf16[32,1152]{1,0:T(8,128)(2,1)S(1)}, u32[]{:S(2)}, u32[]{:S(2)}) collective-permute-start(bf16[32,1152]{1,0:T(8,128)(2,1)S(1)} %get-tuple-element.98), channel_id=1, source_target_pairs={{0,8},{1,9},{2,10},{3,11},{4,12},{5,13},{6,14},{7,15},{8,0},{9,1},... | collective-permute-start | bytes 221192 | tf_op jit(solution)/shard_map/ppermute | solution.py:37
  6.3 0.7 collective-permute-start.2
  8.4 0.8 collective-permute-done.1
  9.2 1.5 %collective-permute-done.2 = bf16[32,1152]{1,0:T(8,128)(2,1)S(1)} collective-permute-done((bf16[32,1152]{1,0:T(8,128)(2,1)S(1)}, bf16[32,1152]{1,0:T(8,128)(2,1)S(1)}, u32[]{:S(2)}, u32[]{:S(2)}) %collective-permute-start.2) | collective-permute-done | bytes 73760 | tf_op jit(solution)/shard_map/ppermute | solution.py:37
  10.7 5.0 %collective-permute-start.3 = (bf16[128,1152]{1,0:T(8,128)(2,1)S(1)}, bf16[128,1152]{1,0:T(8,128)(2,1)S(1)}, u32[]{:S(2)}, u32[]{:S(2)}) collective-permute-start(bf16[128,1152]{1,0:T(8,128)(2,1)S(1)} %pad_maximum_fusion.5), channel_id=1, source_target_pairs={{0,7},{1,2},{2,1},{3,4},{4,3},{5,6},{6,5},{7,0},{8,15},{9,10},{10,... | collective-permute-start | bytes 884744 | tf_op jit(solution)/shard_map/ppermute | solution.py:37
  15.7 2.2 %collective-permute-start.4 = (bf16[64,1152]{1,0:T(8,128)(2,1)S(1)}, bf16[64,1152]{1,0:T(8,128)(2,1)S(1)}, u32[]{:S(2)}, u32[]{:S(2)}) collective-permute-start(bf16[64,1152]{1,0:T(8,128)(2,1)S(1)} %pad_maximum_fusion.11), channel_id=1, source_target_pairs={{0,136},{1,137},{2,138},{3,139},{4,140},{5,141},{6,142},{7,143},{8... | collective-permute-start | bytes 442376 | tf_op jit(solution)/shard_map/ppermute | solution.py:37
  18.3 3.9 %collective-permute-done.4 = bf16[64,1152]{1,0:T(8,128)(2,1)S(1)} collective-permute-done((bf16[64,1152]{1,0:T(8,128)(2,1)S(1)}, bf16[64,1152]{1,0:T(8,128)(2,1)S(1)}, u32[]{:S(2)}, u32[]{:S(2)}) %collective-permute-start.4) | collective-permute-done | bytes 147488 | tf_op jit(solution)/shard_map/ppermute | solution.py:37
  22.2 2.2 %collective-permute-done.5 = bf16[64,1152]{1,0:T(8,128)(2,1)S(1)} collective-permute-done((bf16[64,1152]{1,0:T(8,128)(2,1)S(1)}, bf16[64,1152]{1,0:T(8,128)(2,1)S(1)}, u32[]{:S(2)}, u32[]{:S(2)}) %collective-permute-start.5) | collective-permute-done | bytes 147488 | tf_op jit(solution)/shard_map/ppermute | solution.py:37
  24.6 0.7 collective-permute-start.8
  25.3 5.8 %collective-permute-done.6 = bf16[128,1152]{1,0:T(8,128)(2,1)S(1)} collective-permute-done((bf16[128,1152]{1,0:T(8,128)(2,1)S(1)}, bf16[128,1152]{1,0:T(8,128)(2,1)S(1)}, u32[]{:S(2)}, u32[]{:S(2)}) %collective-permute-start.6) | collective-permute-done | bytes 294944 | tf_op jit(solution)/shard_map/ppermute | solution.py:37
  32.2 1.2 %collective-permute-start.10 = (bf16[256,1152]{1,0:T(8,128)(2,1)S(1)}, bf16[256,1152]{1,0:T(8,128)(2,1)S(1)}, u32[]{:S(2)}, u32[]{:S(2)}) collective-permute-start(bf16[256,1152]{1,0:T(8,128)(2,1)S(1)} %pad_maximum_fusion.2), channel_id=1, source_target_pairs={{0,136},{1,137},{2,138},{3,139},{4,140},{5,141},{6,142},{7,143},{8... | collective-permute-start | bytes 1769480 | tf_op jit(solution)/shard_map/ppermute | solution.py:37
  33.4 2.0 %collective-permute-start.11 = (bf16[128,1152]{1,0:T(8,128)(2,1)S(1)}, bf16[128,1152]{1,0:T(8,128)(2,1)S(1)}, u32[]{:S(2)}, u32[]{:S(2)}) collective-permute-start(bf16[128,1152]{1,0:T(8,128)(2,1)S(1)} %collective-permute-done.6), channel_id=1, source_target_pairs={{0,7},{1,2},{2,1},{3,4},{4,3},{5,6},{6,5},{7,0},{8,15},{9,10},{10,... | collective-permute-start | bytes 884744 | tf_op jit(solution)/shard_map/ppermute | solution.py:37
  35.6 0.9 fusion.29
  36.5 0.9 fusion.82
  37.4 0.7 fusion.96
  39.7 1.6 %collective-permute-done.11 = bf16[128,1152]{1,0:T(8,128)(2,1)S(1)} collective-permute-done((bf16[128,1152]{1,0:T(8,128)(2,1)S(1)}, bf16[128,1152]{1,0:T(8,128)(2,1)S(1)}, u32[]{:S(2)}, u32[]{:S(2)}) %collective-permute-start.11) | collective-permute-done | bytes 294944 | tf_op jit(solution)/shard_map/ppermute | solution.py:37
  41.3 1.4 %collective-permute-done.9 = bf16[256,1152]{1,0:T(8,128)(2,1)S(1)} collective-permute-done((bf16[256,1152]{1,0:T(8,128)(2,1)S(1)}, bf16[256,1152]{1,0:T(8,128)(2,1)S(1)}, u32[]{:S(2)}, u32[]{:S(2)}) %collective-permute-start.9) | collective-permute-done | bytes 589856 | tf_op jit(solution)/shard_map/ppermute | solution.py:37
  43.9 1.0 %fusion.21 = bf16[512,512]{1,0:T(8,128)(2,1)S(1)} fusion(bf16[512,1152]{1,0:T(8,128)(2,1)S(1)} %constant_dynamic-update-slice_fusion.8, bf16[512,1152]{1,0:T(8,128)(2,1)S(1)} %constant_dynamic-update-slice_fusion.13, f32[]{:T(128)} %bitcast.42, f32[]{:T(128)} %bitcast.38), kind=kOutput, calls=%fused_computation.30 | convolution fusion | flops 605814784 | bytes 2883592 | tf_op jit(solution)/shard_map/dot_general | solution.py:87
  45.5 0.9 fusion.93
  46.5 1.0 %fusion.20 = bf16[512,512]{1,0:T(8,128)(2,1)S(1)} fusion(bf16[512,1152]{1,0:T(8,128)(2,1)S(1)} %constant_dynamic-update-slice_fusion.15, bf16[512,1152]{1,0:T(8,128)(2,1)S(1)} %constant_dynamic-update-slice_fusion.13, f32[]{:T(128)} %bitcast.45, f32[]{:T(128)} %bitcast.35), kind=kOutput, calls=%fused_computation.29 | convolution fusion | flops 605814784 | bytes 2883592 | tf_op jit(solution)/shard_map/dot_general | solution.py:87
  47.5 0.9 fusion.95
  50.7 2.8 %collective-permute-start.16 = (f16[256,1152]{1,0:T(8,128)(2,1)S(1)}, f16[256,1152]{1,0:T(8,128)(2,1)S(1)}, u32[]{:S(2)}, u32[]{:S(2)}) collective-permute-start(f16[256,1152]{1,0:T(8,128)(2,1)S(1)} %get-tuple-element.95), channel_id=1, source_target_pairs={{0,48},{1,49},{2,50},{3,51},{4,52},{5,53},{6,54},{7,55},{8,56},{9,... | collective-permute-start | bytes 1769480 | tf_op jit(solution)/shard_map/ppermute | solution.py:37
  53.6 1.5 %collective-permute-start.17 = (f16[256,1152]{1,0:T(8,128)(2,1)S(1)}, f16[256,1152]{1,0:T(8,128)(2,1)S(1)}, u32[]{:S(2)}, u32[]{:S(2)}) collective-permute-start(f16[256,1152]{1,0:T(8,128)(2,1)S(1)} %get-tuple-element.94), channel_id=1, source_target_pairs={{0,136},{1,137},{2,138},{3,139},{4,140},{5,141},{6,142},{7,143},{8... | collective-permute-start | bytes 1769480 | tf_op jit(solution)/shard_map/ppermute | solution.py:37
  55.8 1.7 %collective-permute-start.15 = (f16[128,1152]{1,0:T(8,128)(2,1)S(1)}, f16[128,1152]{1,0:T(8,128)(2,1)S(1)}, u32[]{:S(2)}, u32[]{:S(2)}) collective-permute-start(f16[128,1152]{1,0:T(8,128)(2,1)S(1)} %fusion.6), channel_id=1, source_target_pairs={{0,7},{1,2},{2,1},{3,4},{4,3},{5,6},{6,5},{7,0},{8,15},{9,10},{10,... | collective-permute-start | bytes 884744 | tf_op jit(solution)/shard_map/ppermute | solution.py:37
  58.4 0.7 fusion.2
  59.2 0.9 convolution_add_fusion
  60.0 3.8 %collective-permute-done.15 = f16[128,1152]{1,0:T(8,128)(2,1)S(1)} collective-permute-done((f16[128,1152]{1,0:T(8,128)(2,1)S(1)}, f16[128,1152]{1,0:T(8,128)(2,1)S(1)}, u32[]{:S(2)}, u32[]{:S(2)}) %collective-permute-start.15) | collective-permute-done | bytes 294944 | tf_op jit(solution)/shard_map/ppermute | solution.py:37
  63.8 0.8 collective-permute-done.17
  65.0 1.2 %collective-permute-start.18 = (f16[128,1152]{1,0:T(8,128)(2,1)S(1)}, f16[128,1152]{1,0:T(8,128)(2,1)S(1)}, u32[]{:S(2)}, u32[]{:S(2)}) collective-permute-start(f16[128,1152]{1,0:T(8,128)(2,1)S(1)} %fusion.69), channel_id=1, source_target_pairs={{0,16},{1,17},{2,18},{3,19},{4,20},{5,21},{6,22},{7,23},{8,24},{9,... | collective-permute-start | bytes 884744 | tf_op jit(solution)/shard_map/ppermute | solution.py:37
  66.4 0.7 fusion.1
  67.2 3.3 %collective-permute-start.21 = (f16[128,1152]{1,0:T(8,128)(2,1)S(1)}, f16[128,1152]{1,0:T(8,128)(2,1)S(1)}, u32[]{:S(2)}, u32[]{:S(2)}) collective-permute-start(f16[128,1152]{1,0:T(8,128)(2,1)S(1)} %fusion.67), channel_id=1, source_target_pairs={{0,1},{1,0},{2,3},{3,2},{4,5},{5,4},{6,7},{7,6},{8,9},{9,8},{10,11... | collective-permute-start | bytes 884744 | tf_op jit(solution)/shard_map/ppermute | solution.py:37
  70.5 1.3 %collective-permute-done.18 = f16[128,1152]{1,0:T(8,128)(2,1)S(1)} collective-permute-done((f16[128,1152]{1,0:T(8,128)(2,1)S(1)}, f16[128,1152]{1,0:T(8,128)(2,1)S(1)}, u32[]{:S(2)}, u32[]{:S(2)}) %collective-permute-start.18) | collective-permute-done | bytes 294944 | tf_op jit(solution)/shard_map/ppermute | solution.py:37
  71.8 1.2 %collective-permute-done.19 = f16[128,1152]{1,0:T(8,128)(2,1)S(1)} collective-permute-done((f16[128,1152]{1,0:T(8,128)(2,1)S(1)}, f16[128,1152]{1,0:T(8,128)(2,1)S(1)}, u32[]{:S(2)}, u32[]{:S(2)}) %collective-permute-start.19) | collective-permute-done | bytes 294944 | tf_op jit(solution)/shard_map/ppermute | solution.py:37
  73.1 2.2 %collective-permute-done.21 = f16[128,1152]{1,0:T(8,128)(2,1)S(1)} collective-permute-done((f16[128,1152]{1,0:T(8,128)(2,1)S(1)}, f16[128,1152]{1,0:T(8,128)(2,1)S(1)}, u32[]{:S(2)}, u32[]{:S(2)}) %collective-permute-start.21) | collective-permute-done | bytes 294944 | tf_op jit(solution)/shard_map/ppermute | solution.py:37
  75.4 1.3 %collective-permute-start.22 = (f16[64,1152]{1,0:T(8,128)(2,1)S(1)}, f16[64,1152]{1,0:T(8,128)(2,1)S(1)}, u32[]{:S(2)}, u32[]{:S(2)}) collective-permute-start(f16[64,1152]{1,0:T(8,128)(2,1)S(1)} %fusion.79), channel_id=1, source_target_pairs={{0,136},{1,137},{2,138},{3,139},{4,140},{5,141},{6,142},{7,143},{8... | collective-permute-start | bytes 442376 | tf_op jit(solution)/shard_map/ppermute | solution.py:37
  76.9 0.8 collective-permute-start.24
  77.7 0.8 collective-permute-start.23
  78.5 3.4 %collective-permute-done.22 = f16[64,1152]{1,0:T(8,128)(2,1)S(1)} collective-permute-done((f16[64,1152]{1,0:T(8,128)(2,1)S(1)}, f16[64,1152]{1,0:T(8,128)(2,1)S(1)}, u32[]{:S(2)}, u32[]{:S(2)}) %collective-permute-start.22) | collective-permute-done | bytes 147488 | tf_op jit(solution)/shard_map/ppermute | solution.py:37
  81.9 2.3 %collective-permute-done.23 = f16[64,1152]{1,0:T(8,128)(2,1)S(1)} collective-permute-done((f16[64,1152]{1,0:T(8,128)(2,1)S(1)}, f16[64,1152]{1,0:T(8,128)(2,1)S(1)}, u32[]{:S(2)}, u32[]{:S(2)}) %collective-permute-start.23) | collective-permute-done | bytes 147488 | tf_op jit(solution)/shard_map/ppermute | solution.py:37
  84.1 0.7 collective-permute-done.24
  85.0 1.5 %collective-permute-start.25 = (f16[32,1152]{1,0:T(8,128)(2,1)S(1)}, f16[32,1152]{1,0:T(8,128)(2,1)S(1)}, u32[]{:S(2)}, u32[]{:S(2)}) collective-permute-start(f16[32,1152]{1,0:T(8,128)(2,1)S(1)} %fusion.84), channel_id=1, source_target_pairs={{0,8},{1,9},{2,10},{3,11},{4,12},{5,13},{6,14},{7,15},{8,0},{9,1},... | collective-permute-start | bytes 221192 | tf_op jit(solution)/shard_map/ppermute | solution.py:37
  86.6 1.6 %collective-permute-start.27 = (f16[64,1152]{1,0:T(8,128)(2,1)S(1)}, f16[64,1152]{1,0:T(8,128)(2,1)S(1)}, u32[]{:S(2)}, u32[]{:S(2)}) collective-permute-start(f16[64,1152]{1,0:T(8,128)(2,1)S(1)} %fusion.77), channel_id=1, source_target_pairs={{0,1},{1,0},{2,3},{3,2},{4,5},{5,4},{6,7},{7,6},{8,9},{9,8},{10,11... | collective-permute-start | bytes 442376 | tf_op jit(solution)/shard_map/ppermute | solution.py:37
  88.3 1.2 %collective-permute-start.26 = (f16[32,1152]{1,0:T(8,128)(2,1)S(1)}, f16[32,1152]{1,0:T(8,128)(2,1)S(1)}, u32[]{:S(2)}, u32[]{:S(2)}) collective-permute-start(f16[32,1152]{1,0:T(8,128)(2,1)S(1)} %fusion.83), channel_id=1, source_target_pairs={{0,16},{1,17},{2,18},{3,19},{4,20},{5,21},{6,22},{7,23},{8,24},{9,... | collective-permute-start | bytes 221192 | tf_op jit(solution)/shard_map/ppermute | solution.py:37
  89.5 3.2 %collective-permute-done.26 = f16[32,1152]{1,0:T(8,128)(2,1)S(1)} collective-permute-done((f16[32,1152]{1,0:T(8,128)(2,1)S(1)}, f16[32,1152]{1,0:T(8,128)(2,1)S(1)}, u32[]{:S(2)}, u32[]{:S(2)}) %collective-permute-start.26) | collective-permute-done | bytes 73760 | tf_op jit(solution)/shard_map/ppermute | solution.py:37
  92.9 1.0 %shard_map.61 = (f32[64,1152]{1,0:T(8,128)}, f32[64,1152]{1,0:T(8,128)}) custom-call(bf16[64,1152]{1,0:T(8,128)(2,1)S(1)} %copy-done.1, bf16[64,1152]{1,0:T(8,128)(2,1)S(1)} %copy-done.3, f32[64,1152]{1,0:T(8,128)S(1)} %pad_maximum_fusion.8.image_sum, f32[64,1152]{1,0:T(8,128)S(1)} %slice_add_fusion.7.text_sum), custom_call_target="tpu_custom_call" | custom-call | tf_op jit(solution)/shard_map/pallas_call | solution.py:81
  (89 shorter events, 10.9 us)
Async XLA Ops:
  0.6 0.9 copy-start.2
  1.7 9.0 %collective-permute-start = (bf16[64,1152]{1,0:T(8,128)(2,1)S(1)}, bf16[64,1152]{1,0:T(8,128)(2,1)S(1)}, u32[]{:S(2)}, u32[]{:S(2)}) collective-permute-start(bf16[64,1152]{1,0:T(8,128)(2,1)S(1)} %shard_map.60), channel_id=1, source_target_pairs={{0,1},{1,0},{2,3},{3,2},{4,5},{5,4},{6,7},{7,6},{8,9},{9,8},{10,11... | collective-permute-start | bytes 442376 | tf_op jit(solution)/shard_map/ppermute | solution.py:37
  3.7 0.9 copy-start
  4.7 4.4 %collective-permute-start.1 = (bf16[32,1152]{1,0:T(8,128)(2,1)S(1)}, bf16[32,1152]{1,0:T(8,128)(2,1)S(1)}, u32[]{:S(2)}, u32[]{:S(2)}) collective-permute-start(bf16[32,1152]{1,0:T(8,128)(2,1)S(1)} %get-tuple-element.98), channel_id=1, source_target_pairs={{0,8},{1,9},{2,10},{3,11},{4,12},{5,13},{6,14},{7,15},{8,0},{9,1},... | collective-permute-start | bytes 221192 | tf_op jit(solution)/shard_map/ppermute | solution.py:37
  6.3 4.4 %collective-permute-start.2 = (bf16[32,1152]{1,0:T(8,128)(2,1)S(1)}, bf16[32,1152]{1,0:T(8,128)(2,1)S(1)}, u32[]{:S(2)}, u32[]{:S(2)}) collective-permute-start(bf16[32,1152]{1,0:T(8,128)(2,1)S(1)} %get-tuple-element.97), channel_id=1, source_target_pairs={{0,16},{1,17},{2,18},{3,19},{4,20},{5,21},{6,22},{7,23},{8,24},{9,... | collective-permute-start | bytes 221192 | tf_op jit(solution)/shard_map/ppermute | solution.py:37
  10.7 13.7 %collective-permute-start.3 = (bf16[128,1152]{1,0:T(8,128)(2,1)S(1)}, bf16[128,1152]{1,0:T(8,128)(2,1)S(1)}, u32[]{:S(2)}, u32[]{:S(2)}) collective-permute-start(bf16[128,1152]{1,0:T(8,128)(2,1)S(1)} %pad_maximum_fusion.5), channel_id=1, source_target_pairs={{0,7},{1,2},{2,1},{3,4},{4,3},{5,6},{6,5},{7,0},{8,15},{9,10},{10,... | collective-permute-start | bytes 884744 | tf_op jit(solution)/shard_map/ppermute | solution.py:37
  15.7 6.4 %collective-permute-start.4 = (bf16[64,1152]{1,0:T(8,128)(2,1)S(1)}, bf16[64,1152]{1,0:T(8,128)(2,1)S(1)}, u32[]{:S(2)}, u32[]{:S(2)}) collective-permute-start(bf16[64,1152]{1,0:T(8,128)(2,1)S(1)} %pad_maximum_fusion.11), channel_id=1, source_target_pairs={{0,136},{1,137},{2,138},{3,139},{4,140},{5,141},{6,142},{7,143},{8... | collective-permute-start | bytes 442376 | tf_op jit(solution)/shard_map/ppermute | solution.py:37
  17.9 6.4 %collective-permute-start.5 = (bf16[64,1152]{1,0:T(8,128)(2,1)S(1)}, bf16[64,1152]{1,0:T(8,128)(2,1)S(1)}, u32[]{:S(2)}, u32[]{:S(2)}) collective-permute-start(bf16[64,1152]{1,0:T(8,128)(2,1)S(1)} %pad_maximum_fusion.12), channel_id=1, source_target_pairs={{0,48},{1,49},{2,50},{3,51},{4,52},{5,53},{6,54},{7,55},{8,56},{9,... | collective-permute-start | bytes 442376 | tf_op jit(solution)/shard_map/ppermute | solution.py:37
  24.4 6.7 %collective-permute-start.6 = (bf16[128,1152]{1,0:T(8,128)(2,1)S(1)}, bf16[128,1152]{1,0:T(8,128)(2,1)S(1)}, u32[]{:S(2)}, u32[]{:S(2)}) collective-permute-start(bf16[128,1152]{1,0:T(8,128)(2,1)S(1)} %collective-permute-done.3), channel_id=1, source_target_pairs={{0,1},{1,0},{2,3},{3,2},{4,5},{5,4},{6,7},{7,6},{8,9},{9,8},{10,11... | collective-permute-start | bytes 884744 | tf_op jit(solution)/shard_map/ppermute | solution.py:37
  24.5 6.9 %collective-permute-start.7 = (bf16[128,1152]{1,0:T(8,128)(2,1)S(1)}, bf16[128,1152]{1,0:T(8,128)(2,1)S(1)}, u32[]{:S(2)}, u32[]{:S(2)}) collective-permute-start(bf16[128,1152]{1,0:T(8,128)(2,1)S(1)} %pad_maximum_fusion.6), channel_id=1, source_target_pairs={{0,16},{1,17},{2,18},{3,19},{4,20},{5,21},{6,22},{7,23},{8,24},{9,... | collective-permute-start | bytes 884744 | tf_op jit(solution)/shard_map/ppermute | solution.py:37
  24.6 6.9 %collective-permute-start.8 = (bf16[128,1152]{1,0:T(8,128)(2,1)S(1)}, bf16[128,1152]{1,0:T(8,128)(2,1)S(1)}, u32[]{:S(2)}, u32[]{:S(2)}) collective-permute-start(bf16[128,1152]{1,0:T(8,128)(2,1)S(1)} %pad_maximum_fusion.7), channel_id=1, source_target_pairs={{0,8},{1,9},{2,10},{3,11},{4,12},{5,13},{6,14},{7,15},{8,0},{9,1},... | collective-permute-start | bytes 884744 | tf_op jit(solution)/shard_map/ppermute | solution.py:37
  25.3 12.8 %collective-permute-start.13 = (bf16[256,1152]{1,0:T(8,128)(2,1)S(1)}, bf16[256,1152]{1,0:T(8,128)(2,1)S(1)}, u32[]{:S(2)}, u32[]{:S(2)}) collective-permute-start(bf16[256,1152]{1,0:T(8,128)(2,1)S(1)} %pad_maximum_fusion.4), channel_id=1, source_target_pairs={{0,64},{1,65},{2,66},{3,67},{4,68},{5,69},{6,70},{7,71},{8,72},{9,... | collective-permute-start | bytes 1769480 | tf_op jit(solution)/shard_map/ppermute | solution.py:37
  31.5 11.2 %collective-permute-start.9 = (bf16[256,1152]{1,0:T(8,128)(2,1)S(1)}, bf16[256,1152]{1,0:T(8,128)(2,1)S(1)}, u32[]{:S(2)}, u32[]{:S(2)}) collective-permute-start(bf16[256,1152]{1,0:T(8,128)(2,1)S(1)} %pad_maximum_fusion.1), channel_id=1, source_target_pairs={{0,48},{1,49},{2,50},{3,51},{4,52},{5,53},{6,54},{7,55},{8,56},{9,... | collective-permute-start | bytes 1769480 | tf_op jit(solution)/shard_map/ppermute | solution.py:37
  32.2 11.2 %collective-permute-start.10 = (bf16[256,1152]{1,0:T(8,128)(2,1)S(1)}, bf16[256,1152]{1,0:T(8,128)(2,1)S(1)}, u32[]{:S(2)}, u32[]{:S(2)}) collective-permute-start(bf16[256,1152]{1,0:T(8,128)(2,1)S(1)} %pad_maximum_fusion.2), channel_id=1, source_target_pairs={{0,136},{1,137},{2,138},{3,139},{4,140},{5,141},{6,142},{7,143},{8... | collective-permute-start | bytes 1769480 | tf_op jit(solution)/shard_map/ppermute | solution.py:37
  33.4 7.9 %collective-permute-start.11 = (bf16[128,1152]{1,0:T(8,128)(2,1)S(1)}, bf16[128,1152]{1,0:T(8,128)(2,1)S(1)}, u32[]{:S(2)}, u32[]{:S(2)}) collective-permute-start(bf16[128,1152]{1,0:T(8,128)(2,1)S(1)} %collective-permute-done.6), channel_id=1, source_target_pairs={{0,7},{1,2},{2,1},{3,4},{4,3},{5,6},{6,5},{7,0},{8,15},{9,10},{10,... | collective-permute-start | bytes 884744 | tf_op jit(solution)/shard_map/ppermute | solution.py:37
  43.5 2.8 %collective-permute-start.12 = (bf16[256,1152]{1,0:T(8,128)(2,1)S(1)}, bf16[256,1152]{1,0:T(8,128)(2,1)S(1)}, u32[]{:S(2)}, u32[]{:S(2)}) collective-permute-start(bf16[256,1152]{1,0:T(8,128)(2,1)S(1)} %pad_maximum_fusion.3), channel_id=1, source_target_pairs={{0,64},{1,65},{2,66},{3,67},{4,68},{5,69},{6,70},{7,71},{8,72},{9,... | collective-permute-start | bytes 1769480 | tf_op jit(solution)/shard_map/ppermute | solution.py:37
  50.0 5.5 %collective-permute-start.14 = (f16[128,1152]{1,0:T(8,128)(2,1)S(1)}, f16[128,1152]{1,0:T(8,128)(2,1)S(1)}, u32[]{:S(2)}, u32[]{:S(2)}) collective-permute-start(f16[128,1152]{1,0:T(8,128)(2,1)S(1)} %fusion.7), channel_id=1, source_target_pairs={{0,64},{1,65},{2,66},{3,67},{4,68},{5,69},{6,70},{7,71},{8,72},{9,... | collective-permute-start | bytes 884744 | tf_op jit(solution)/shard_map/ppermute | solution.py:37
  50.7 13.1 %collective-permute-start.16 = (f16[256,1152]{1,0:T(8,128)(2,1)S(1)}, f16[256,1152]{1,0:T(8,128)(2,1)S(1)}, u32[]{:S(2)}, u32[]{:S(2)}) collective-permute-start(f16[256,1152]{1,0:T(8,128)(2,1)S(1)} %get-tuple-element.95), channel_id=1, source_target_pairs={{0,48},{1,49},{2,50},{3,51},{4,52},{5,53},{6,54},{7,55},{8,56},{9,... | collective-permute-start | bytes 1769480 | tf_op jit(solution)/shard_map/ppermute | solution.py:37
  53.6 11.1 %collective-permute-start.17 = (f16[256,1152]{1,0:T(8,128)(2,1)S(1)}, f16[256,1152]{1,0:T(8,128)(2,1)S(1)}, u32[]{:S(2)}, u32[]{:S(2)}) collective-permute-start(f16[256,1152]{1,0:T(8,128)(2,1)S(1)} %get-tuple-element.94), channel_id=1, source_target_pairs={{0,136},{1,137},{2,138},{3,139},{4,140},{5,141},{6,142},{7,143},{8... | collective-permute-start | bytes 1769480 | tf_op jit(solution)/shard_map/ppermute | solution.py:37
  55.8 8.0 %collective-permute-start.15 = (f16[128,1152]{1,0:T(8,128)(2,1)S(1)}, f16[128,1152]{1,0:T(8,128)(2,1)S(1)}, u32[]{:S(2)}, u32[]{:S(2)}) collective-permute-start(f16[128,1152]{1,0:T(8,128)(2,1)S(1)} %fusion.6), channel_id=1, source_target_pairs={{0,7},{1,2},{2,1},{3,4},{4,3},{5,6},{6,5},{7,0},{8,15},{9,10},{10,... | collective-permute-start | bytes 884744 | tf_op jit(solution)/shard_map/ppermute | solution.py:37
  59.1 7.3 %collective-permute-start.20 = (f16[384,1152]{1,0:T(8,128)(2,1)S(1)}, f16[384,1152]{1,0:T(8,128)(2,1)S(1)}, u32[]{:S(2)}, u32[]{:S(2)}) collective-permute-start(f16[384,1152]{1,0:T(8,128)(2,1)S(1)} %fusion.2), channel_id=1, source_target_pairs={{0,64},{1,65},{2,66},{3,67},{4,68},{5,69},{6,70},{7,71},{8,72},{9,... | collective-permute-start | bytes 2654216 | tf_op jit(solution)/shard_map/ppermute | solution.py:37
  65.0 6.8 %collective-permute-start.18 = (f16[128,1152]{1,0:T(8,128)(2,1)S(1)}, f16[128,1152]{1,0:T(8,128)(2,1)S(1)}, u32[]{:S(2)}, u32[]{:S(2)}) collective-permute-start(f16[128,1152]{1,0:T(8,128)(2,1)S(1)} %fusion.69), channel_id=1, source_target_pairs={{0,16},{1,17},{2,18},{3,19},{4,20},{5,21},{6,22},{7,23},{8,24},{9,... | collective-permute-start | bytes 884744 | tf_op jit(solution)/shard_map/ppermute | solution.py:37
  66.3 6.8 %collective-permute-start.19 = (f16[128,1152]{1,0:T(8,128)(2,1)S(1)}, f16[128,1152]{1,0:T(8,128)(2,1)S(1)}, u32[]{:S(2)}, u32[]{:S(2)}) collective-permute-start(f16[128,1152]{1,0:T(8,128)(2,1)S(1)} %fusion.68), channel_id=1, source_target_pairs={{0,8},{1,9},{2,10},{3,11},{4,12},{5,13},{6,14},{7,15},{8,0},{9,1},... | collective-permute-start | bytes 884744 | tf_op jit(solution)/shard_map/ppermute | solution.py:37
  67.2 8.0 %collective-permute-start.21 = (f16[128,1152]{1,0:T(8,128)(2,1)S(1)}, f16[128,1152]{1,0:T(8,128)(2,1)S(1)}, u32[]{:S(2)}, u32[]{:S(2)}) collective-permute-start(f16[128,1152]{1,0:T(8,128)(2,1)S(1)} %fusion.67), channel_id=1, source_target_pairs={{0,1},{1,0},{2,3},{3,2},{4,5},{5,4},{6,7},{7,6},{8,9},{9,8},{10,11... | collective-permute-start | bytes 884744 | tf_op jit(solution)/shard_map/ppermute | solution.py:37
  75.4 6.4 %collective-permute-start.22 = (f16[64,1152]{1,0:T(8,128)(2,1)S(1)}, f16[64,1152]{1,0:T(8,128)(2,1)S(1)}, u32[]{:S(2)}, u32[]{:S(2)}) collective-permute-start(f16[64,1152]{1,0:T(8,128)(2,1)S(1)} %fusion.79), channel_id=1, source_target_pairs={{0,136},{1,137},{2,138},{3,139},{4,140},{5,141},{6,142},{7,143},{8... | collective-permute-start | bytes 442376 | tf_op jit(solution)/shard_map/ppermute | solution.py:37
  76.9 8.0 %collective-permute-start.24 = (f16[128,1152]{1,0:T(8,128)(2,1)S(1)}, f16[128,1152]{1,0:T(8,128)(2,1)S(1)}, u32[]{:S(2)}, u32[]{:S(2)}) collective-permute-start(f16[128,1152]{1,0:T(8,128)(2,1)S(1)} %fusion.65), channel_id=1, source_target_pairs={{0,7},{1,2},{2,1},{3,4},{4,3},{5,6},{6,5},{7,0},{8,15},{9,10},{10,... | collective-permute-start | bytes 884744 | tf_op jit(solution)/shard_map/ppermute | solution.py:37
  77.7 6.4 %collective-permute-start.23 = (f16[64,1152]{1,0:T(8,128)(2,1)S(1)}, f16[64,1152]{1,0:T(8,128)(2,1)S(1)}, u32[]{:S(2)}, u32[]{:S(2)}) collective-permute-start(f16[64,1152]{1,0:T(8,128)(2,1)S(1)} %fusion.78), channel_id=1, source_target_pairs={{0,48},{1,49},{2,50},{3,51},{4,52},{5,53},{6,54},{7,55},{8,56},{9,... | collective-permute-start | bytes 442376 | tf_op jit(solution)/shard_map/ppermute | solution.py:37
  85.0 4.5 %collective-permute-start.25 = (f16[32,1152]{1,0:T(8,128)(2,1)S(1)}, f16[32,1152]{1,0:T(8,128)(2,1)S(1)}, u32[]{:S(2)}, u32[]{:S(2)}) collective-permute-start(f16[32,1152]{1,0:T(8,128)(2,1)S(1)} %fusion.84), channel_id=1, source_target_pairs={{0,8},{1,9},{2,10},{3,11},{4,12},{5,13},{6,14},{7,15},{8,0},{9,1},... | collective-permute-start | bytes 221192 | tf_op jit(solution)/shard_map/ppermute | solution.py:37
  86.6 6.3 %copy-start.1 = (bf16[64,1152]{1,0:T(8,128)(2,1)S(1)}, bf16[64,1152]{1,0:T(8,128)(2,1)}, u32[]{:S(2)}) copy-start(bf16[64,1152]{1,0:T(8,128)(2,1)} %images.1) | copy-start | bytes 442372
  86.6 6.3 %copy-start.3 = (bf16[64,1152]{1,0:T(8,128)(2,1)S(1)}, bf16[64,1152]{1,0:T(8,128)(2,1)}, u32[]{:S(2)}) copy-start(bf16[64,1152]{1,0:T(8,128)(2,1)} %texts.1) | copy-start | bytes 442372
  86.6 6.1 %collective-permute-start.27 = (f16[64,1152]{1,0:T(8,128)(2,1)S(1)}, f16[64,1152]{1,0:T(8,128)(2,1)S(1)}, u32[]{:S(2)}, u32[]{:S(2)}) collective-permute-start(f16[64,1152]{1,0:T(8,128)(2,1)S(1)} %fusion.77), channel_id=1, source_target_pairs={{0,1},{1,0},{2,3},{3,2},{4,5},{5,4},{6,7},{7,6},{8,9},{9,8},{10,11... | collective-permute-start | bytes 442376 | tf_op jit(solution)/shard_map/ppermute | solution.py:37
  88.3 4.4 %collective-permute-start.26 = (f16[32,1152]{1,0:T(8,128)(2,1)S(1)}, f16[32,1152]{1,0:T(8,128)(2,1)S(1)}, u32[]{:S(2)}, u32[]{:S(2)}) collective-permute-start(f16[32,1152]{1,0:T(8,128)(2,1)S(1)} %fusion.83), channel_id=1, source_target_pairs={{0,16},{1,17},{2,18},{3,19},{4,20},{5,21},{6,22},{7,23},{8,24},{9,... | collective-permute-start | bytes 221192 | tf_op jit(solution)/shard_map/ppermute | solution.py:37

commit v4 on v3

v4 whole, which is shorter than its diff:
```python
import jax
import jax.numpy as jnp
import numpy as np
from jax import lax
from jax.experimental import pallas as pl
from jax.experimental.pallas import tpu as pltpu
from jax.sharding import PartitionSpec as P

epsilon = 1e-06

SHAPE = (2, 2, 4, 2, 8)
AXES = ("group", "blk")
SHRINK = 0.25
SMALL = pltpu.CompilerParams(vmem_limit_bytes=4 * 2**20)


def pairs(axis, phase):
    partner = []
    for xh, core, y, xl, z in np.ndindex(*SHAPE):
        at = {"x": 2 * xh + xl, "y": y, "z": z}
        n = {"x": 4, "y": 4, "z": 8}[axis]
        p = at[axis]
        if (phase + core) % 2 == 0:
            at[axis] = p ^ 1
        else:
            at[axis] = (p + 1) % n if p % 2 else (p - 1) % n
        there = (at["x"] // 2, core, at["y"], at["x"] % 2, at["z"])
        partner.append(int(np.ravel_multi_index(there, SHAPE)))
    return partner


X0, X1, Y0, Y1 = pairs("x", 1), pairs("x", 0), pairs("y", 1), pairs("y", 0)
XY = [X0[i] for i in Y0]
Z0, Z1 = pairs("z", 0), pairs("z", 1)
ZFAR = [i ^ 4 for i in range(256)]
CORE = [i ^ 64 for i in range(256)]


def swap(array, partner):
    return lax.ppermute(array, AXES, list(enumerate(partner)))


def join(*arrays):
    return jnp.concatenate(arrays, axis=0)


def step(*arrays):
    return lax.optimization_barrier(arrays)


def unit_of(embedding):
    values = embedding.astype(jnp.float32)
    inverse = lax.rsqrt(jnp.sum(values * values, axis=-1, keepdims=True) + epsilon)
    return values * inverse, inverse


def low_kernel(texts, images, text_low, image_low):
    for rows, low in ((texts, text_low), (images, image_low)):
        low[...] = unit_of(rows[...])[0].astype(jnp.bfloat16)


def low_rows(texts, images):
    out = jax.ShapeDtypeStruct(texts.shape, jnp.bfloat16)
    return pl.pallas_call(low_kernel, out_shape=(out, out), compiler_params=SMALL)(texts, images)


def shrunk(part):
    return (part * SHRINK).astype(jnp.float16)


def grown(part):
    return part.astype(jnp.float32) * (1 / SHRINK)


def grads_kernel(images, texts, image_sum, text_sum, image_out, text_out):
    for rows, summed, out in ((images, image_sum, image_out), (texts, text_sum, text_out)):
        unit, inverse = unit_of(rows[...])
        total = summed[...]
        along = jnp.sum(unit * total, axis=-1, keepdims=True)
        out[...] = (total - unit * along) * inverse


def grads(images, texts, *sums):
    out = jax.ShapeDtypeStruct(images.shape, jnp.float32)
    return pl.pallas_call(grads_kernel, out_shape=(out, out), compiler_params=SMALL)(
        images, texts, *sums
    )


def weights_of(texts, images, factor, offset, own=None):
    product = lax.dot_general(
        texts, images, (((1,), (1,)), ((), ())), preferred_element_type=jnp.float32
    )
    value = jax.nn.sigmoid(factor * product + offset)
    if own is not None:
        row = lax.broadcasted_iota(jnp.int32, value.shape, 0)
        col = lax.broadcasted_iota(jnp.int32, value.shape, 1)
        value = value - ((row == col) & (row < own)).astype(jnp.float32)
    return (factor * value).astype(jnp.bfloat16)


def dot(a, b):
    return jnp.dot(a, b, preferred_element_type=jnp.float32)


def dot_t(a, b):
    return lax.dot_general(a, b, (((0,), (0,)), ((), ())), preferred_element_type=jnp.float32)


def body(images, texts, logit_scale, bias):
    factor = logit_scale[0]
    offset = bias[0]
    n = images.shape[0]
    text_low, image_low = low_rows(texts, images)

    t1, x1, y1, xy1 = step(
        swap(text_low, ZFAR), swap(image_low, X0), swap(image_low, Y0), swap(image_low, XY)
    )
    t, a, b = join(text_low, t1), join(image_low, x1), join(y1, xy1)
    got_t, got_a, got_b = step(swap(t, Z0), swap(a, X1), swap(b, Y1))
    own_a, a, b = join(t, got_t), join(a, got_a), join(b, got_b)
    first = join(a, b)
    got_a, got_b, own_b = step(swap(a, Y1), swap(b, X1), swap(own_a, Z1))

    first_own_a = weights_of(own_a, first, factor, offset, n)
    text_own_a = dot(first_own_a, first)
    sum_first = dot_t(first_own_a, own_a)

    h = 4 * n
    second = join(got_a, got_b)
    own = join(own_a, own_b)
    other = swap(own, CORE)
    second_own = weights_of(own, second, factor, offset)
    sum_second = dot_t(second_own, own)
    first_own_b = weights_of(own_b, first, factor, offset)
    text_own_b = dot(first_own_b, first)
    sum_second, second_own, text_own_b, other = lax.optimization_barrier(
        (sum_second, second_own, text_own_b, other)
    )
    second_other = weights_of(other, second, factor, offset)
    sum_second = shrunk(sum_second + dot_t(second_other, other))

    first_other_b = weights_of(other[h:], first, factor, offset)
    late_other = shrunk(dot(first_other_b, first) + dot(second_other[h:], second))
    sum_second, late_other, second_own, second_other, first_other_b, sum_first, other = (
        lax.optimization_barrier(
            (sum_second, late_other, second_own, second_other, first_other_b, sum_first, other)
        )
    )
    got_late = swap(late_other, CORE)
    got_a, got_b = swap(sum_second[:h], Y1), swap(sum_second[h:], X1)
    late = shrunk(text_own_b + dot(second_own[h:], second) + grown(got_late))
    late, first_own_b, first_other_b, text_own_a, other, second_own, second_other = (
        lax.optimization_barrier(
            (late, first_own_b, first_other_b, text_own_a, other, second_own, second_other)
        )
    )
    got_t = swap(late, Z1)

    first_other_a = weights_of(other[:h], first, factor, offset)
    text_other_a = dot(first_other_a, first)
    got_early = swap(shrunk(text_other_a + dot(second_other[:h], second)), CORE)
    t = text_own_a + dot(second_own[:h], second) + grown(got_early)
    sum_first = sum_first + dot_t(
        join(first_own_b, first_other_a, first_other_b), join(own_b, other)
    )

    got_a, got_b, got_t = step(got_a, got_b, got_t)
    a, b, t = sum_first[:h] + grown(got_a), sum_first[h:] + grown(got_b), t + grown(got_t)
    m = 2 * n
    got_a, got_b, got_t = step(
        swap(shrunk(a[m:]), X1), swap(shrunk(b[m:]), Y1), swap(shrunk(t[m:]), Z0)
    )
    a, b, t = a[:m] + grown(got_a), b[:m] + grown(got_b), t[:m] + grown(got_t)
    got_x, got_y, got_xy, got_t = step(
        swap(shrunk(a[n:]), X0),
        swap(shrunk(b[:n]), Y0),
        swap(shrunk(b[n:]), XY),
        swap(shrunk(t[n:]), ZFAR),
    )
    image_sum = a[:n] + grown(got_x) + grown(got_y) + grown(got_xy)
    return grads(images, texts, image_sum, t[:n] + grown(got_t))


def solution(mesh):
    return jax.shard_map(
        body,
        mesh=mesh,
        in_specs=(P(("group", "blk"), None), P(("group", "blk"), None), P(), P()),
        out_specs=(P(("group", "blk"), None), P(("group", "blk"), None)),
        check_vma=False,
    )
```

time: 94.4 us -> 93 us (0.985)
  waiting for transfers between devices: 37.1 us -> 29.2 us
  starting transfers between devices: 35.2 us -> 43.1 us
  matrix products: 13.5 us -> 12.2 us
    ppermute x28 -> x23, waiting for transfers between devices: 37.1 us -> 29.2 us  [swap(): return lax.ppermute(array, AXES, list(enumerate(partner)))]
    ppermute x28 -> x23, starting transfers between devices: 35.2 us -> 43.1 us  [swap(): return lax.ppermute(array, AXES, list(enumerate(partner)))]
    dot_general x7 -> x6, matrix products: 5.24 us -> 4.51 us  [weights_of(): lax.dot_general(texts, images, (((1,), (1,)), ((), ())), preferred_elemen...]
    dot_general x5 -> x4, matrix products: 3.99 us -> 3.5 us  [dot_t(): lax.dot_general(a, b, (((0,), (0,)), ((), ())), preferred_element_type=jn...]
    dot_general x9 -> x8, matrix products: 4.3 us -> 4.17 us  [dot(): return jnp.dot(a, b, preferred_element_type=jnp.float32)]
    unnamed x21 -> x16, local copies, waits for them, and re-layouts: 2.14 us -> 2.03 us
  transfers between devices with their start and end apart: 28 -> 23, of which waited for: 19 -> 14; matrix products, arithmetic and copies ran while one was open for 13% -> 11% of each run, Pallas kernels for 0% -> 0%
where the time goes in v4:
time: 93 us; the launch traced here: 92 us
  starting transfers between devices  43.1 us (46%)
  waiting for transfers between devices  29.2 us (31%)
  matrix products  12.2 us (13%)
  local copies, waits for them, and re-layouts  2.47 us (3%)
  between operations  2.31 us (2%)
  other arithmetic  1.62 us (2%)
  Pallas kernels  1.18 us (1%)
    ppermute x23, starting transfers between devices, swap(): return lax.ppermute(array, AXES, list(enumerate(partner)))  43.1 us
    ppermute x23, waiting for transfers between devices, swap(): return lax.ppermute(array, AXES, list(enumerate(partner)))  29.2 us
    dot_general x6, matrix products, weights_of(): lax.dot_general(texts, images, (((1,), (1,)), ((), ())), preferred_elemen...  4.51 us
    dot_general x8, matrix products, dot(): return jnp.dot(a, b, preferred_element_type=jnp.float32)  4.17 us
    dot_general x4, matrix products, dot_t(): lax.dot_general(a, b, (((0,), (0,)), ((), ())), preferred_element_type=jn...  3.5 us
    unnamed x16, local copies, waits for them, and re-layouts  2.03 us
  transfers between devices with their start and end apart: 23, of which 14 were waited for; matrix products, arithmetic and copies ran while one was open for 11% of the time, Pallas kernels for 0%

profile of v4, /device:TPU:24, one launch (start us, length us, event | category | flops | bytes accessed | tf_op | source)
XLA Modules:
  0.0 92.0 jit_solution(954249743980625300)
XLA Ops:
  0.6 0.9 copy-done
  1.5 0.9 copy-done.2
  2.6 2.8 %collective-permute-start.1 = (bf16[64,1152]{1,0:T(8,128)(2,1)S(1)}, bf16[64,1152]{1,0:T(8,128)(2,1)S(1)}, u32[]{:S(2)}, u32[]{:S(2)}) collective-permute-start(bf16[64,1152]{1,0:T(8,128)(2,1)S(1)} %get-tuple-element.43), channel_id=1, source_target_pairs={{0,136},{1,137},{2,138},{3,139},{4,140},{5,141},{6,142},{7,143},{8... | collective-permute-start | bytes 442376 | tf_op jit(solution)/shard_map/ppermute | solution.py:40
  5.7 2.9 %collective-permute-start.3 = (bf16[64,1152]{1,0:T(8,128)(2,1)S(1)}, bf16[64,1152]{1,0:T(8,128)(2,1)S(1)}, u32[]{:S(2)}, u32[]{:S(2)}) collective-permute-start(bf16[64,1152]{1,0:T(8,128)(2,1)S(1)} %get-tuple-element.43), channel_id=1, source_target_pairs={{0,184},{1,185},{2,186},{3,187},{4,188},{5,189},{6,190},{7,191},{8... | collective-permute-start | bytes 442376 | tf_op jit(solution)/shard_map/ppermute | solution.py:40
  8.6 7.2 %collective-permute-start = (bf16[64,1152]{1,0:T(8,128)(2,1)S(1)}, bf16[64,1152]{1,0:T(8,128)(2,1)S(1)}, u32[]{:S(2)}, u32[]{:S(2)}) collective-permute-start(bf16[64,1152]{1,0:T(8,128)(2,1)S(1)} %get-tuple-element.42), channel_id=1, source_target_pairs={{0,4},{1,5},{2,6},{3,7},{4,0},{5,1},{6,2},{7,3},{8,12},{9,13},{10,... | collective-permute-start | bytes 442376 | tf_op jit(solution)/shard_map/ppermute | solution.py:40
  17.1 2.9 %collective-permute-done = bf16[64,1152]{1,0:T(8,128)(2,1)S(1)} collective-permute-done((bf16[64,1152]{1,0:T(8,128)(2,1)S(1)}, bf16[64,1152]{1,0:T(8,128)(2,1)S(1)}, u32[]{:S(2)}, u32[]{:S(2)}) %collective-permute-start) | collective-permute-done | bytes 147488 | tf_op jit(solution)/shard_map/ppermute | solution.py:40
  20.0 1.2 %collective-permute-start.4 = (bf16[128,1152]{1,0:T(8,128)(2,1)S(1)}, bf16[128,1152]{1,0:T(8,128)(2,1)S(1)}, u32[]{:S(2)}, u32[]{:S(2)}) collective-permute-start(bf16[128,1152]{1,0:T(8,128)(2,1)S(1)} %pad_maximum_fusion.2), channel_id=1, source_target_pairs={{0,1},{1,0},{2,3},{3,2},{4,5},{5,4},{6,7},{7,6},{8,9},{9,8},{10,11... | collective-permute-start | bytes 884744 | tf_op jit(solution)/shard_map/ppermute | solution.py:40
  21.4 1.5 %collective-permute-start.6 = (bf16[128,1152]{1,0:T(8,128)(2,1)S(1)}, bf16[128,1152]{1,0:T(8,128)(2,1)S(1)}, u32[]{:S(2)}, u32[]{:S(2)}) collective-permute-start(bf16[128,1152]{1,0:T(8,128)(2,1)S(1)} %pad_maximum_fusion.4), channel_id=1, source_target_pairs={{0,16},{1,17},{2,18},{3,19},{4,20},{5,21},{6,22},{7,23},{8,24},{9,... | collective-permute-start | bytes 884744 | tf_op jit(solution)/shard_map/ppermute | solution.py:40
  22.9 4.0 %collective-permute-done.4 = bf16[128,1152]{1,0:T(8,128)(2,1)S(1)} collective-permute-done((bf16[128,1152]{1,0:T(8,128)(2,1)S(1)}, bf16[128,1152]{1,0:T(8,128)(2,1)S(1)}, u32[]{:S(2)}, u32[]{:S(2)}) %collective-permute-start.4) | collective-permute-done | bytes 294944 | tf_op jit(solution)/shard_map/ppermute | solution.py:40
  26.9 1.2 %collective-permute-done.5 = bf16[128,1152]{1,0:T(8,128)(2,1)S(1)} collective-permute-done((bf16[128,1152]{1,0:T(8,128)(2,1)S(1)}, bf16[128,1152]{1,0:T(8,128)(2,1)S(1)}, u32[]{:S(2)}, u32[]{:S(2)}) %collective-permute-start.5) | collective-permute-done | bytes 294944 | tf_op jit(solution)/shard_map/ppermute | solution.py:40
  28.2 1.5 %collective-permute-start.7 = (bf16[256,1152]{1,0:T(8,128)(2,1)S(1)}, bf16[256,1152]{1,0:T(8,128)(2,1)S(1)}, u32[]{:S(2)}, u32[]{:S(2)}) collective-permute-start(bf16[256,1152]{1,0:T(8,128)(2,1)S(1)} %pad_maximum_fusion), channel_id=1, source_target_pairs={{0,16},{1,17},{2,18},{3,19},{4,20},{5,21},{6,22},{7,23},{8,24},{9,... | collective-permute-start | bytes 1769480 | tf_op jit(solution)/shard_map/ppermute | solution.py:40
  29.7 0.7 collective-permute-start.8
  30.5 4.2 %collective-permute-start.9 = (bf16[256,1152]{1,0:T(8,128)(2,1)S(1)}, bf16[256,1152]{1,0:T(8,128)(2,1)S(1)}, u32[]{:S(2)}, u32[]{:S(2)}) collective-permute-start(bf16[256,1152]{1,0:T(8,128)(2,1)S(1)} %get-tuple-element.88), channel_id=1, source_target_pairs={{0,7},{1,2},{2,1},{3,4},{4,3},{5,6},{6,5},{7,0},{8,15},{9,10},{10,... | collective-permute-start | bytes 1769480 | tf_op jit(solution)/shard_map/ppermute | solution.py:40
  34.8 0.6 fusion.48
  35.5 0.5 fusion.82
  36.0 0.5 fusion.81
  36.5 1.7 %collective-permute-done.7 = bf16[256,1152]{1,0:T(8,128)(2,1)S(1)} collective-permute-done((bf16[256,1152]{1,0:T(8,128)(2,1)S(1)}, bf16[256,1152]{1,0:T(8,128)(2,1)S(1)}, u32[]{:S(2)}, u32[]{:S(2)}) %collective-permute-start.7) | collective-permute-done | bytes 589856 | tf_op jit(solution)/shard_map/ppermute | solution.py:40
  38.2 1.5 %collective-permute-done.8 = bf16[256,1152]{1,0:T(8,128)(2,1)S(1)} collective-permute-done((bf16[256,1152]{1,0:T(8,128)(2,1)S(1)}, bf16[256,1152]{1,0:T(8,128)(2,1)S(1)}, u32[]{:S(2)}, u32[]{:S(2)}) %collective-permute-start.8) | collective-permute-done | bytes 589856 | tf_op jit(solution)/shard_map/ppermute | solution.py:40
  39.7 2.9 %collective-permute-done.9 = bf16[256,1152]{1,0:T(8,128)(2,1)S(1)} collective-permute-done((bf16[256,1152]{1,0:T(8,128)(2,1)S(1)}, bf16[256,1152]{1,0:T(8,128)(2,1)S(1)}, u32[]{:S(2)}, u32[]{:S(2)}) %collective-permute-start.9) | collective-permute-done | bytes 589856 | tf_op jit(solution)/shard_map/ppermute | solution.py:40
  43.0 0.6 fusion.51
  43.7 0.5 fusion.79
  44.2 1.0 %fusion.22 = bf16[512,512]{1,0:T(8,128)(2,1)S(1)} fusion(bf16[512,1152]{1,0:T(8,128)(2,1)S(1)} %constant_dynamic-update-slice_fusion.3, bf16[512,1152]{1,0:T(8,128)(2,1)S(1)} %constant_dynamic-update-slice_fusion.7, f32[]{:T(128)} %bitcast.36, f32[]{:T(128)} %bitcast.32), kind=kOutput, calls=%fused_computation.29 | convolution fusion | flops 605814784 | bytes 2883592 | tf_op jit(solution)/shard_map/dot_general | solution.py:91
  45.2 0.9 fusion.78
  46.1 1.0 %fusion.21 = bf16[512,512]{1,0:T(8,128)(2,1)S(1)} fusion(bf16[512,1152]{1,0:T(8,128)(2,1)S(1)} %collective-permute-done.10, bf16[512,1152]{1,0:T(8,128)(2,1)S(1)} %constant_dynamic-update-slice_fusion.7, f32[]{:T(128)} %bitcast.38, f32[]{:T(128)} %bitcast.30), kind=kOutput, calls=%fused_computation.28 | convolution fusion | flops 605814784 | bytes 2883592 | tf_op jit(solution)/shard_map/dot_general | solution.py:91
  47.1 0.9 fusion.80
  48.8 0.6 fusion.50
  49.4 0.5 fusion.4
  50.0 0.6 collective-permute-start.11
  50.8 1.6 %collective-permute-start.12 = (f16[256,1152]{1,0:T(8,128)(2,1)S(1)}, f16[256,1152]{1,0:T(8,128)(2,1)S(1)}, u32[]{:S(2)}, u32[]{:S(2)}) collective-permute-start(f16[256,1152]{1,0:T(8,128)(2,1)S(1)} %get-tuple-element.85), channel_id=1, source_target_pairs={{0,16},{1,17},{2,18},{3,19},{4,20},{5,21},{6,22},{7,23},{8,24},{9,... | collective-permute-start | bytes 1769480 | tf_op jit(solution)/shard_map/ppermute | solution.py:40
  52.4 1.3 %collective-permute-start.13 = (f16[256,1152]{1,0:T(8,128)(2,1)S(1)}, f16[256,1152]{1,0:T(8,128)(2,1)S(1)}, u32[]{:S(2)}, u32[]{:S(2)}) collective-permute-start(f16[256,1152]{1,0:T(8,128)(2,1)S(1)} %get-tuple-element.84), channel_id=1, source_target_pairs={{0,8},{1,9},{2,10},{3,11},{4,12},{5,13},{6,14},{7,15},{8,0},{9,1},... | collective-permute-start | bytes 1769480 | tf_op jit(solution)/shard_map/ppermute | solution.py:40
  54.4 3.3 %collective-permute-start.14 = (f16[256,1152]{1,0:T(8,128)(2,1)S(1)}, f16[256,1152]{1,0:T(8,128)(2,1)S(1)}, u32[]{:S(2)}, u32[]{:S(2)}) collective-permute-start(f16[256,1152]{1,0:T(8,128)(2,1)S(1)} %multiply_convert_fusion.1), channel_id=1, source_target_pairs={{0,7},{1,2},{2,1},{3,4},{4,3},{5,6},{6,5},{7,0},{8,15},{9,10},{10,... | collective-permute-start | bytes 1769480 | tf_op jit(solution)/shard_map/ppermute | solution.py:40
  58.2 0.6 fusion.49
  58.9 0.5 fusion.5
  59.5 1.2 %convolution_add_fusion = f32[512,1152]{1,0:T(8,128)S(1)} fusion(f32[512,1152]{1,0:T(8,128)S(1)} %fusion.81, bf16[512,1152]{1,0:T(8,128)(2,1)S(1)} %collective-permute-done.10, bf16[256,1152]{1,0:T(8,128)(2,1)S(1)} %collective-permute-done.9, bf16[256,512]{1,0:T(8,128)(2,1)S(1)} %fusion.50, bf16[256,512]{1,0:T(8,128)(2,1)S(1)} %fusion.49, ...), kind=kOutput, calls=%fused_computation | convolution fusion | flops 912457728 | bytes 7274496 | tf_op jit(solution)/shard_map/dot_general | solution.py:107
  60.7 1.5 %collective-permute-done.13 = f16[256,1152]{1,0:T(8,128)(2,1)S(1)} collective-permute-done((f16[256,1152]{1,0:T(8,128)(2,1)S(1)}, f16[256,1152]{1,0:T(8,128)(2,1)S(1)}, u32[]{:S(2)}, u32[]{:S(2)}) %collective-permute-start.13) | collective-permute-done | bytes 589856 | tf_op jit(solution)/shard_map/ppermute | solution.py:40
  62.2 3.4 %collective-permute-done.14 = f16[256,1152]{1,0:T(8,128)(2,1)S(1)} collective-permute-done((f16[256,1152]{1,0:T(8,128)(2,1)S(1)}, f16[256,1152]{1,0:T(8,128)(2,1)S(1)}, u32[]{:S(2)}, u32[]{:S(2)}) %collective-permute-start.14) | collective-permute-done | bytes 589856 | tf_op jit(solution)/shard_map/ppermute | solution.py:40
  65.9 0.8 collective-permute-start.15
  66.8 0.8 collective-permute-start.16
  67.7 0.6 fusion.2
  68.4 4.3 %collective-permute-done.15 = f16[128,1152]{1,0:T(8,128)(2,1)S(1)} collective-permute-done((f16[128,1152]{1,0:T(8,128)(2,1)S(1)}, f16[128,1152]{1,0:T(8,128)(2,1)S(1)}, u32[]{:S(2)}, u32[]{:S(2)}) %collective-permute-start.15) | collective-permute-done | bytes 294944 | tf_op jit(solution)/shard_map/ppermute | solution.py:40
  72.7 1.1 %collective-permute-done.16 = f16[128,1152]{1,0:T(8,128)(2,1)S(1)} collective-permute-done((f16[128,1152]{1,0:T(8,128)(2,1)S(1)}, f16[128,1152]{1,0:T(8,128)(2,1)S(1)}, u32[]{:S(2)}, u32[]{:S(2)}) %collective-permute-start.16) | collective-permute-done | bytes 294944 | tf_op jit(solution)/shard_map/ppermute | solution.py:40
  73.9 1.3 %collective-permute-done.18 = f16[128,1152]{1,0:T(8,128)(2,1)S(1)} collective-permute-done((f16[128,1152]{1,0:T(8,128)(2,1)S(1)}, f16[128,1152]{1,0:T(8,128)(2,1)S(1)}, u32[]{:S(2)}, u32[]{:S(2)}) %collective-permute-start.18) | collective-permute-done | bytes 294944 | tf_op jit(solution)/shard_map/ppermute | solution.py:40
  75.3 2.8 %collective-permute-start.19 = (f16[64,1152]{1,0:T(8,128)(2,1)S(1)}, f16[64,1152]{1,0:T(8,128)(2,1)S(1)}, u32[]{:S(2)}, u32[]{:S(2)}) collective-permute-start(f16[64,1152]{1,0:T(8,128)(2,1)S(1)} %fusion.66), channel_id=1, source_target_pairs={{0,136},{1,137},{2,138},{3,139},{4,140},{5,141},{6,142},{7,143},{8... | collective-permute-start | bytes 442376 | tf_op jit(solution)/shard_map/ppermute | solution.py:40
  78.3 1.1 %collective-permute-start.20 = (f16[64,1152]{1,0:T(8,128)(2,1)S(1)}, f16[64,1152]{1,0:T(8,128)(2,1)S(1)}, u32[]{:S(2)}, u32[]{:S(2)}) collective-permute-start(f16[64,1152]{1,0:T(8,128)(2,1)S(1)} %get-tuple-element.87), channel_id=1, source_target_pairs={{0,48},{1,49},{2,50},{3,51},{4,52},{5,53},{6,54},{7,55},{8,56},{9,... | collective-permute-start | bytes 442376 | tf_op jit(solution)/shard_map/ppermute | solution.py:40
  79.5 2.1 %collective-permute-start.21 = (f16[64,1152]{1,0:T(8,128)(2,1)S(1)}, f16[64,1152]{1,0:T(8,128)(2,1)S(1)}, u32[]{:S(2)}, u32[]{:S(2)}) collective-permute-start(f16[64,1152]{1,0:T(8,128)(2,1)S(1)} %get-tuple-element.86), channel_id=1, source_target_pairs={{0,184},{1,185},{2,186},{3,187},{4,188},{5,189},{6,190},{7,191},{8... | collective-permute-start | bytes 442376 | tf_op jit(solution)/shard_map/ppermute | solution.py:40
  81.6 5.8 %collective-permute-start.22 = (f16[64,1152]{1,0:T(8,128)(2,1)S(1)}, f16[64,1152]{1,0:T(8,128)(2,1)S(1)}, u32[]{:S(2)}, u32[]{:S(2)}) collective-permute-start(f16[64,1152]{1,0:T(8,128)(2,1)S(1)} %fusion.63), channel_id=1, source_target_pairs={{0,4},{1,5},{2,6},{3,7},{4,0},{5,1},{6,2},{7,3},{8,12},{9,13},{10,... | collective-permute-start | bytes 442376 | tf_op jit(solution)/shard_map/ppermute | solution.py:40
  88.0 2.9 %collective-permute-done.22 = f16[64,1152]{1,0:T(8,128)(2,1)S(1)} collective-permute-done((f16[64,1152]{1,0:T(8,128)(2,1)S(1)}, f16[64,1152]{1,0:T(8,128)(2,1)S(1)}, u32[]{:S(2)}, u32[]{:S(2)}) %collective-permute-start.22) | collective-permute-done | bytes 147488 | tf_op jit(solution)/shard_map/ppermute | solution.py:40
  91.0 1.0 %shard_map.60 = (f32[64,1152]{1,0:T(8,128)}, f32[64,1152]{1,0:T(8,128)}) custom-call(bf16[64,1152]{1,0:T(8,128)(2,1)S(1)} %copy-done.1, bf16[64,1152]{1,0:T(8,128)(2,1)S(1)} %copy-done.3, f32[64,1152]{1,0:T(8,128)S(1)} %get-tuple-element.95.image_sum, f32[64,1152]{1,0:T(8,128)S(1)} %get-tuple-element.94.text_sum), custom_call_target="tpu_custom_call" | custom-call | tf_op jit(solution)/shard_map/pallas_call | solution.py:85
  (58 shorter events, 5.4 us)
Async XLA Ops:
  0.6 0.9 copy-start
  1.5 0.9 copy-start.2
  2.6 17.4 %collective-permute-start.1 = (bf16[64,1152]{1,0:T(8,128)(2,1)S(1)}, bf16[64,1152]{1,0:T(8,128)(2,1)S(1)}, u32[]{:S(2)}, u32[]{:S(2)}) collective-permute-start(bf16[64,1152]{1,0:T(8,128)(2,1)S(1)} %get-tuple-element.43), channel_id=1, source_target_pairs={{0,136},{1,137},{2,138},{3,139},{4,140},{5,141},{6,142},{7,143},{8... | collective-permute-start | bytes 442376 | tf_op jit(solution)/shard_map/ppermute | solution.py:40
  5.4 14.6 %collective-permute-start.2 = (bf16[64,1152]{1,0:T(8,128)(2,1)S(1)}, bf16[64,1152]{1,0:T(8,128)(2,1)S(1)}, u32[]{:S(2)}, u32[]{:S(2)}) collective-permute-start(bf16[64,1152]{1,0:T(8,128)(2,1)S(1)} %get-tuple-element.43), channel_id=1, source_target_pairs={{0,48},{1,49},{2,50},{3,51},{4,52},{5,53},{6,54},{7,55},{8,56},{9,... | collective-permute-start | bytes 442376 | tf_op jit(solution)/shard_map/ppermute | solution.py:40
  5.7 14.3 %collective-permute-start.3 = (bf16[64,1152]{1,0:T(8,128)(2,1)S(1)}, bf16[64,1152]{1,0:T(8,128)(2,1)S(1)}, u32[]{:S(2)}, u32[]{:S(2)}) collective-permute-start(bf16[64,1152]{1,0:T(8,128)(2,1)S(1)} %get-tuple-element.43), channel_id=1, source_target_pairs={{0,184},{1,185},{2,186},{3,187},{4,188},{5,189},{6,190},{7,191},{8... | collective-permute-start | bytes 442376 | tf_op jit(solution)/shard_map/ppermute | solution.py:40
  8.6 11.4 %collective-permute-start = (bf16[64,1152]{1,0:T(8,128)(2,1)S(1)}, bf16[64,1152]{1,0:T(8,128)(2,1)S(1)}, u32[]{:S(2)}, u32[]{:S(2)}) collective-permute-start(bf16[64,1152]{1,0:T(8,128)(2,1)S(1)} %get-tuple-element.42), channel_id=1, source_target_pairs={{0,4},{1,5},{2,6},{3,7},{4,0},{5,1},{6,2},{7,3},{8,12},{9,13},{10,... | collective-permute-start | bytes 442376 | tf_op jit(solution)/shard_map/ppermute | solution.py:40
  20.0 6.8 %collective-permute-start.4 = (bf16[128,1152]{1,0:T(8,128)(2,1)S(1)}, bf16[128,1152]{1,0:T(8,128)(2,1)S(1)}, u32[]{:S(2)}, u32[]{:S(2)}) collective-permute-start(bf16[128,1152]{1,0:T(8,128)(2,1)S(1)} %pad_maximum_fusion.2), channel_id=1, source_target_pairs={{0,1},{1,0},{2,3},{3,2},{4,5},{5,4},{6,7},{7,6},{8,9},{9,8},{10,11... | collective-permute-start | bytes 884744 | tf_op jit(solution)/shard_map/ppermute | solution.py:40
  21.2 6.8 %collective-permute-start.5 = (bf16[128,1152]{1,0:T(8,128)(2,1)S(1)}, bf16[128,1152]{1,0:T(8,128)(2,1)S(1)}, u32[]{:S(2)}, u32[]{:S(2)}) collective-permute-start(bf16[128,1152]{1,0:T(8,128)(2,1)S(1)} %pad_maximum_fusion.3), channel_id=1, source_target_pairs={{0,8},{1,9},{2,10},{3,11},{4,12},{5,13},{6,14},{7,15},{8,0},{9,1},... | collective-permute-start | bytes 884744 | tf_op jit(solution)/shard_map/ppermute | solution.py:40
  21.4 6.8 %collective-permute-start.6 = (bf16[128,1152]{1,0:T(8,128)(2,1)S(1)}, bf16[128,1152]{1,0:T(8,128)(2,1)S(1)}, u32[]{:S(2)}, u32[]{:S(2)}) collective-permute-start(bf16[128,1152]{1,0:T(8,128)(2,1)S(1)} %pad_maximum_fusion.4), channel_id=1, source_target_pairs={{0,16},{1,17},{2,18},{3,19},{4,20},{5,21},{6,22},{7,23},{8,24},{9,... | collective-permute-start | bytes 884744 | tf_op jit(solution)/shard_map/ppermute | solution.py:40
  28.2 10.0 %collective-permute-start.7 = (bf16[256,1152]{1,0:T(8,128)(2,1)S(1)}, bf16[256,1152]{1,0:T(8,128)(2,1)S(1)}, u32[]{:S(2)}, u32[]{:S(2)}) collective-permute-start(bf16[256,1152]{1,0:T(8,128)(2,1)S(1)} %pad_maximum_fusion), channel_id=1, source_target_pairs={{0,16},{1,17},{2,18},{3,19},{4,20},{5,21},{6,22},{7,23},{8,24},{9,... | collective-permute-start | bytes 1769480 | tf_op jit(solution)/shard_map/ppermute | solution.py:40
  29.7 10.0 %collective-permute-start.8 = (bf16[256,1152]{1,0:T(8,128)(2,1)S(1)}, bf16[256,1152]{1,0:T(8,128)(2,1)S(1)}, u32[]{:S(2)}, u32[]{:S(2)}) collective-permute-start(bf16[256,1152]{1,0:T(8,128)(2,1)S(1)} %pad_maximum_fusion.1), channel_id=1, source_target_pairs={{0,8},{1,9},{2,10},{3,11},{4,12},{5,13},{6,14},{7,15},{8,0},{9,1},... | collective-permute-start | bytes 1769480 | tf_op jit(solution)/shard_map/ppermute | solution.py:40
  30.5 12.0 %collective-permute-start.9 = (bf16[256,1152]{1,0:T(8,128)(2,1)S(1)}, bf16[256,1152]{1,0:T(8,128)(2,1)S(1)}, u32[]{:S(2)}, u32[]{:S(2)}) collective-permute-start(bf16[256,1152]{1,0:T(8,128)(2,1)S(1)} %get-tuple-element.88), channel_id=1, source_target_pairs={{0,7},{1,2},{2,1},{3,4},{4,3},{5,6},{6,5},{7,0},{8,15},{9,10},{10,... | collective-permute-start | bytes 1769480 | tf_op jit(solution)/shard_map/ppermute | solution.py:40
  42.7 3.4 %collective-permute-start.10 = (bf16[512,1152]{1,0:T(8,128)(2,1)S(1)}, bf16[512,1152]{1,0:T(8,128)(2,1)S(1)}, u32[]{:S(2)}, u32[]{:S(2)}) collective-permute-start(bf16[512,1152]{1,0:T(8,128)(2,1)S(1)} %constant_dynamic-update-slice_fusion.3), channel_id=1, source_target_pairs={{0,64},{1,65},{2,66},{3,67},{4,68},{5,69},{6,70},{7,71},{8,72},{9,... | collective-permute-start | bytes 3538952 | tf_op jit(solution)/shard_map/ppermute | solution.py:40
  50.0 4.2 %collective-permute-start.11 = (f16[256,1152]{1,0:T(8,128)(2,1)S(1)}, f16[256,1152]{1,0:T(8,128)(2,1)S(1)}, u32[]{:S(2)}, u32[]{:S(2)}) collective-permute-start(f16[256,1152]{1,0:T(8,128)(2,1)S(1)} %fusion.4), channel_id=1, source_target_pairs={{0,64},{1,65},{2,66},{3,67},{4,68},{5,69},{6,70},{7,71},{8,72},{9,... | collective-permute-start | bytes 1769480 | tf_op jit(solution)/shard_map/ppermute | solution.py:40
  50.8 10.0 %collective-permute-start.12 = (f16[256,1152]{1,0:T(8,128)(2,1)S(1)}, f16[256,1152]{1,0:T(8,128)(2,1)S(1)}, u32[]{:S(2)}, u32[]{:S(2)}) collective-permute-start(f16[256,1152]{1,0:T(8,128)(2,1)S(1)} %get-tuple-element.85), channel_id=1, source_target_pairs={{0,16},{1,17},{2,18},{3,19},{4,20},{5,21},{6,22},{7,23},{8,24},{9,... | collective-permute-start | bytes 1769480 | tf_op jit(solution)/shard_map/ppermute | solution.py:40
  52.4 9.9 %collective-permute-start.13 = (f16[256,1152]{1,0:T(8,128)(2,1)S(1)}, f16[256,1152]{1,0:T(8,128)(2,1)S(1)}, u32[]{:S(2)}, u32[]{:S(2)}) collective-permute-start(f16[256,1152]{1,0:T(8,128)(2,1)S(1)} %get-tuple-element.84), channel_id=1, source_target_pairs={{0,8},{1,9},{2,10},{3,11},{4,12},{5,13},{6,14},{7,15},{8,0},{9,1},... | collective-permute-start | bytes 1769480 | tf_op jit(solution)/shard_map/ppermute | solution.py:40
  54.4 11.2 %collective-permute-start.14 = (f16[256,1152]{1,0:T(8,128)(2,1)S(1)}, f16[256,1152]{1,0:T(8,128)(2,1)S(1)}, u32[]{:S(2)}, u32[]{:S(2)}) collective-permute-start(f16[256,1152]{1,0:T(8,128)(2,1)S(1)} %multiply_convert_fusion.1), channel_id=1, source_target_pairs={{0,7},{1,2},{2,1},{3,4},{4,3},{5,6},{6,5},{7,0},{8,15},{9,10},{10,... | collective-permute-start | bytes 1769480 | tf_op jit(solution)/shard_map/ppermute | solution.py:40
  59.4 8.3 %collective-permute-start.17 = (f16[256,1152]{1,0:T(8,128)(2,1)S(1)}, f16[256,1152]{1,0:T(8,128)(2,1)S(1)}, u32[]{:S(2)}, u32[]{:S(2)}) collective-permute-start(f16[256,1152]{1,0:T(8,128)(2,1)S(1)} %fusion.5), channel_id=1, source_target_pairs={{0,64},{1,65},{2,66},{3,67},{4,68},{5,69},{6,70},{7,71},{8,72},{9,... | collective-permute-start | bytes 1769480 | tf_op jit(solution)/shard_map/ppermute | solution.py:40
  65.9 6.8 %collective-permute-start.15 = (f16[128,1152]{1,0:T(8,128)(2,1)S(1)}, f16[128,1152]{1,0:T(8,128)(2,1)S(1)}, u32[]{:S(2)}, u32[]{:S(2)}) collective-permute-start(f16[128,1152]{1,0:T(8,128)(2,1)S(1)} %fusion.59), channel_id=1, source_target_pairs={{0,8},{1,9},{2,10},{3,11},{4,12},{5,13},{6,14},{7,15},{8,0},{9,1},... | collective-permute-start | bytes 884744 | tf_op jit(solution)/shard_map/ppermute | solution.py:40
  66.8 7.0 %collective-permute-start.16 = (f16[128,1152]{1,0:T(8,128)(2,1)S(1)}, f16[128,1152]{1,0:T(8,128)(2,1)S(1)}, u32[]{:S(2)}, u32[]{:S(2)}) collective-permute-start(f16[128,1152]{1,0:T(8,128)(2,1)S(1)} %fusion.58), channel_id=1, source_target_pairs={{0,16},{1,17},{2,18},{3,19},{4,20},{5,21},{6,22},{7,23},{8,24},{9,... | collective-permute-start | bytes 884744 | tf_op jit(solution)/shard_map/ppermute | solution.py:40
  68.3 6.8 %collective-permute-start.18 = (f16[128,1152]{1,0:T(8,128)(2,1)S(1)}, f16[128,1152]{1,0:T(8,128)(2,1)S(1)}, u32[]{:S(2)}, u32[]{:S(2)}) collective-permute-start(f16[128,1152]{1,0:T(8,128)(2,1)S(1)} %fusion.57), channel_id=1, source_target_pairs={{0,1},{1,0},{2,3},{3,2},{4,5},{5,4},{6,7},{7,6},{8,9},{9,8},{10,11... | collective-permute-start | bytes 884744 | tf_op jit(solution)/shard_map/ppermute | solution.py:40
  75.3 12.1 %collective-permute-start.19 = (f16[64,1152]{1,0:T(8,128)(2,1)S(1)}, f16[64,1152]{1,0:T(8,128)(2,1)S(1)}, u32[]{:S(2)}, u32[]{:S(2)}) collective-permute-start(f16[64,1152]{1,0:T(8,128)(2,1)S(1)} %fusion.66), channel_id=1, source_target_pairs={{0,136},{1,137},{2,138},{3,139},{4,140},{5,141},{6,142},{7,143},{8... | collective-permute-start | bytes 442376 | tf_op jit(solution)/shard_map/ppermute | solution.py:40
  78.3 12.7 %copy-start.1 = (bf16[64,1152]{1,0:T(8,128)(2,1)S(1)}, bf16[64,1152]{1,0:T(8,128)(2,1)}, u32[]{:S(2)}) copy-start(bf16[64,1152]{1,0:T(8,128)(2,1)} %images.3) | copy-start | bytes 442372
  78.3 12.7 %copy-start.3 = (bf16[64,1152]{1,0:T(8,128)(2,1)S(1)}, bf16[64,1152]{1,0:T(8,128)(2,1)}, u32[]{:S(2)}) copy-start(bf16[64,1152]{1,0:T(8,128)(2,1)} %texts.3) | copy-start | bytes 442372
  78.3 9.1 %collective-permute-start.20 = (f16[64,1152]{1,0:T(8,128)(2,1)S(1)}, f16[64,1152]{1,0:T(8,128)(2,1)S(1)}, u32[]{:S(2)}, u32[]{:S(2)}) collective-permute-start(f16[64,1152]{1,0:T(8,128)(2,1)S(1)} %get-tuple-element.87), channel_id=1, source_target_pairs={{0,48},{1,49},{2,50},{3,51},{4,52},{5,53},{6,54},{7,55},{8,56},{9,... | collective-permute-start | bytes 442376 | tf_op jit(solution)/shard_map/ppermute | solution.py:40
  79.5 8.5 %collective-permute-start.21 = (f16[64,1152]{1,0:T(8,128)(2,1)S(1)}, f16[64,1152]{1,0:T(8,128)(2,1)S(1)}, u32[]{:S(2)}, u32[]{:S(2)}) collective-permute-start(f16[64,1152]{1,0:T(8,128)(2,1)S(1)} %get-tuple-element.86), channel_id=1, source_target_pairs={{0,184},{1,185},{2,186},{3,187},{4,188},{5,189},{6,190},{7,191},{8... | collective-permute-start | bytes 442376 | tf_op jit(solution)/shard_map/ppermute | solution.py:40
  81.6 9.2 %collective-permute-start.22 = (f16[64,1152]{1,0:T(8,128)(2,1)S(1)}, f16[64,1152]{1,0:T(8,128)(2,1)S(1)}, u32[]{:S(2)}, u32[]{:S(2)}) collective-permute-start(f16[64,1152]{1,0:T(8,128)(2,1)S(1)} %fusion.63), channel_id=1, source_target_pairs={{0,4},{1,5},{2,6},{3,7},{4,0},{5,1},{6,2},{7,3},{8,12},{9,13},{10,... | collective-permute-start | bytes 442376 | tf_op jit(solution)/shard_map/ppermute | solution.py:40

commit v5 on v4

--- a/solution.py
+++ b/solution.py
@@ -72,19 +72,16 @@
     return part.astype(jnp.float32) * (1 / SHRINK)
 
 
-def grads_kernel(images, texts, image_sum, text_sum, image_out, text_out):
-    for rows, summed, out in ((images, image_sum, image_out), (texts, text_sum, text_out)):
-        unit, inverse = unit_of(rows[...])
-        total = summed[...]
-        along = jnp.sum(unit * total, axis=-1, keepdims=True)
-        out[...] = (total - unit * along) * inverse
+def grad_kernel(rows, summed, out):
+    unit, inverse = unit_of(rows[...])
+    total = summed[...]
+    along = jnp.sum(unit * total, axis=-1, keepdims=True)
+    out[...] = (total - unit * along) * inverse
 
 
-def grads(images, texts, *sums):
-    out = jax.ShapeDtypeStruct(images.shape, jnp.float32)
-    return pl.pallas_call(grads_kernel, out_shape=(out, out), compiler_params=SMALL)(
-        images, texts, *sums
-    )
+def grad_rows(rows, summed):
+    out = jax.ShapeDtypeStruct(rows.shape, jnp.float32)
+    return pl.pallas_call(grad_kernel, out_shape=out, compiler_params=SMALL)(rows, summed)
 
 
 def weights_of(texts, images, factor, offset, own=None):
@@ -113,14 +110,13 @@
     n = images.shape[0]
     text_low, image_low = low_rows(texts, images)
 
-    t1, x1, y1, xy1 = step(
-        swap(text_low, ZFAR), swap(image_low, X0), swap(image_low, Y0), swap(image_low, XY)
-    )
+    t1 = swap(text_low, ZFAR)
+    x1, y1, xy1 = step(swap(image_low, X0), swap(image_low, Y0), swap(image_low, XY))
     t, a, b = join(text_low, t1), join(image_low, x1), join(y1, xy1)
-    got_t, got_a, got_b = step(swap(t, Z0), swap(a, X1), swap(b, Y1))
+    got_t, got_a, got_b = swap(t, Z0), swap(a, X1), swap(b, Y1)
     own_a, a, b = join(t, got_t), join(a, got_a), join(b, got_b)
     first = join(a, b)
-    got_a, got_b, own_b = step(swap(a, Y1), swap(b, X1), swap(own_a, Z1))
+    got_a, got_b, own_b = swap(a, Y1), swap(b, X1), swap(own_a, Z1)
 
     first_own_a = weights_of(own_a, first, factor, offset, n)
     text_own_a = dot(first_own_a, first)
@@ -168,18 +164,13 @@
     got_a, got_b, got_t = step(got_a, got_b, got_t)
     a, b, t = sum_first[:h] + grown(got_a), sum_first[h:] + grown(got_b), t + grown(got_t)
     m = 2 * n
-    got_a, got_b, got_t = step(
-        swap(shrunk(a[m:]), X1), swap(shrunk(b[m:]), Y1), swap(shrunk(t[m:]), Z0)
-    )
+    got_a, got_b = step(swap(shrunk(a[m:]), X1), swap(shrunk(b[m:]), Y1))
+    got_t = swap(shrunk(t[m:]), Z0)
     a, b, t = a[:m] + grown(got_a), b[:m] + grown(got_b), t[:m] + grown(got_t)
-    got_x, got_y, got_xy, got_t = step(
-        swap(shrunk(a[n:]), X0),
-        swap(shrunk(b[:n]), Y0),
-        swap(shrunk(b[n:]), XY),
-        swap(shrunk(t[n:]), ZFAR),
-    )
-    image_sum = a[:n] + grown(got_x) + grown(got_y) + grown(got_xy)
-    return grads(images, texts, image_sum, t[:n] + grown(got_t))
+    got_b, got_t = swap(shrunk(b), Y0), swap(shrunk(t[n:]), ZFAR)
+    a = a + grown(got_b)
+    image_sum = a[:n] + grown(swap(shrunk(a[n:]), X0))
+    return grad_rows(images, image_sum), grad_rows(texts, t[:n] + grown(got_t))
 
 
 def solution(mesh):

time: 93 us -> 88.1 us (0.947)
  starting transfers between devices: 43.1 us -> 36.3 us
  waiting for transfers between devices: 29.2 us -> 30.4 us
    ppermute x23 -> x22, starting transfers between devices: 43.1 us -> 36.3 us  [swap(): return lax.ppermute(array, AXES, list(enumerate(partner)))]
    ppermute x23 -> x22, waiting for transfers between devices: 29.2 us -> 30.4 us  [swap(): return lax.ppermute(array, AXES, list(enumerate(partner)))]
    pallas_call x1 -> x2, Pallas kernels: 1.03 us -> 1.86 us  [grad_rows(): pl.pallas_call(grad_kernel, out_shape=out, compiler_params=SMALL)]
    unnamed x16 -> x15, local copies, waits for them, and re-layouts: 2.03 us -> 2.02 us
  transfers between devices with their start and end apart: 23 -> 22, of which waited for: 14 -> 13; matrix products, arithmetic and copies ran while one was open for 11% -> 12% of each run, Pallas kernels for 0% -> 1%
where the time goes in v5:
time: 88.1 us; the launch traced here: 87.6 us
  starting transfers between devices  36.3 us (41%)
  waiting for transfers between devices  30.4 us (35%)
  matrix products  12.1 us (14%)
  local copies, waits for them, and re-layouts  2.46 us (3%)
  between operations  2.33 us (3%)
  other arithmetic  2.09 us (2%)
  Pallas kernels  2.01 us (2%)
    ppermute x22, starting transfers between devices, swap(): return lax.ppermute(array, AXES, list(enumerate(partner)))  36.3 us
    ppermute x22, waiting for transfers between devices, swap(): return lax.ppermute(array, AXES, list(enumerate(partner)))  30.4 us
    dot_general x6, matrix products, weights_of(): lax.dot_general(texts, images, (((1,), (1,)), ((), ())), preferred_elemen...  4.53 us
    dot_general x8, matrix products, dot(): return jnp.dot(a, b, preferred_element_type=jnp.float32)  4.06 us
    dot_general x4, matrix products, dot_t(): lax.dot_general(a, b, (((0,), (0,)), ((), ())), preferred_element_type=jn...  3.48 us
    unnamed x15, local copies, waits for them, and re-layouts  2.02 us
    pallas_call x2, Pallas kernels, grad_rows(): pl.pallas_call(grad_kernel, out_shape=out, compiler_params=SMALL)  1.86 us
  transfers between devices with their start and end apart: 22, of which 13 were waited for; matrix products, arithmetic and copies ran while one was open for 12% of the time, Pallas kernels for 1%

profile of v5, /device:TPU:24, one launch (start us, length us, event | category | flops | bytes accessed | tf_op | source)
XLA Modules:
  0.0 87.6 jit_solution(6147287860898881013)
XLA Ops:
  0.6 0.9 %copy-done = bf16[64,1152]{1,0:T(8,128)(2,1)S(1)} copy-done((bf16[64,1152]{1,0:T(8,128)(2,1)S(1)}, bf16[64,1152]{1,0:T(8,128)(2,1)}, u32[]{:S(2)}) %copy-start) | copy-done | bytes 147480
  1.5 0.9 %copy-done.2 = bf16[64,1152]{1,0:T(8,128)(2,1)S(1)} copy-done((bf16[64,1152]{1,0:T(8,128)(2,1)S(1)}, bf16[64,1152]{1,0:T(8,128)(2,1)}, u32[]{:S(2)}) %copy-start.2) | copy-done | bytes 147480
  2.6 2.8 %collective-permute-start.3 = (bf16[64,1152]{1,0:T(8,128)(2,1)S(1)}, bf16[64,1152]{1,0:T(8,128)(2,1)S(1)}, u32[]{:S(2)}, u32[]{:S(2)}) collective-permute-start(bf16[64,1152]{1,0:T(8,128)(2,1)S(1)} %get-tuple-element.31), channel_id=1, source_target_pairs={{0,136},{1,137},{2,138},{3,139},{4,140},{5,141},{6,142},{7,143},{8... | collective-permute-start | bytes 442376 | tf_op jit(solution)/shard_map/ppermute | solution.py:40
  5.7 2.9 %collective-permute-start.5 = (bf16[64,1152]{1,0:T(8,128)(2,1)S(1)}, bf16[64,1152]{1,0:T(8,128)(2,1)S(1)}, u32[]{:S(2)}, u32[]{:S(2)}) collective-permute-start(bf16[64,1152]{1,0:T(8,128)(2,1)S(1)} %get-tuple-element.31), channel_id=1, source_target_pairs={{0,184},{1,185},{2,186},{3,187},{4,188},{5,189},{6,190},{7,191},{8... | collective-permute-start | bytes 442376 | tf_op jit(solution)/shard_map/ppermute | solution.py:40
  8.6 7.2 %collective-permute-start = (bf16[64,1152]{1,0:T(8,128)(2,1)S(1)}, bf16[64,1152]{1,0:T(8,128)(2,1)S(1)}, u32[]{:S(2)}, u32[]{:S(2)}) collective-permute-start(bf16[64,1152]{1,0:T(8,128)(2,1)S(1)} %get-tuple-element.30), channel_id=1, source_target_pairs={{0,4},{1,5},{2,6},{3,7},{4,0},{5,1},{6,2},{7,3},{8,12},{9,13},{10,... | collective-permute-start | bytes 442376 | tf_op jit(solution)/shard_map/ppermute | solution.py:40
  17.1 2.9 %collective-permute-done = bf16[64,1152]{1,0:T(8,128)(2,1)S(1)} collective-permute-done((bf16[64,1152]{1,0:T(8,128)(2,1)S(1)}, bf16[64,1152]{1,0:T(8,128)(2,1)S(1)}, u32[]{:S(2)}, u32[]{:S(2)}) %collective-permute-start) | collective-permute-done | bytes 147488 | tf_op jit(solution)/shard_map/ppermute | solution.py:40
  20.0 1.2 %collective-permute-start.1 = (bf16[128,1152]{1,0:T(8,128)(2,1)S(1)}, bf16[128,1152]{1,0:T(8,128)(2,1)S(1)}, u32[]{:S(2)}, u32[]{:S(2)}) collective-permute-start(bf16[128,1152]{1,0:T(8,128)(2,1)S(1)} %pad_maximum_fusion.2), channel_id=1, source_target_pairs={{0,1},{1,0},{2,3},{3,2},{4,5},{5,4},{6,7},{7,6},{8,9},{9,8},{10,11... | collective-permute-start | bytes 884744 | tf_op jit(solution)/shard_map/ppermute | solution.py:40
  21.4 1.5 %collective-permute-start.8 = (bf16[128,1152]{1,0:T(8,128)(2,1)S(1)}, bf16[128,1152]{1,0:T(8,128)(2,1)S(1)}, u32[]{:S(2)}, u32[]{:S(2)}) collective-permute-start(bf16[128,1152]{1,0:T(8,128)(2,1)S(1)} %pad_maximum_fusion.4), channel_id=1, source_target_pairs={{0,16},{1,17},{2,18},{3,19},{4,20},{5,21},{6,22},{7,23},{8,24},{9,... | collective-permute-start | bytes 884744 | tf_op jit(solution)/shard_map/ppermute | solution.py:40
  22.9 4.2 %collective-permute-done.1 = bf16[128,1152]{1,0:T(8,128)(2,1)S(1)} collective-permute-done((bf16[128,1152]{1,0:T(8,128)(2,1)S(1)}, bf16[128,1152]{1,0:T(8,128)(2,1)S(1)}, u32[]{:S(2)}, u32[]{:S(2)}) %collective-permute-start.1) | collective-permute-done | bytes 294944 | tf_op jit(solution)/shard_map/ppermute | solution.py:40
  27.2 4.3 %collective-permute-start.2 = (bf16[256,1152]{1,0:T(8,128)(2,1)S(1)}, bf16[256,1152]{1,0:T(8,128)(2,1)S(1)}, u32[]{:S(2)}, u32[]{:S(2)}) collective-permute-start(bf16[256,1152]{1,0:T(8,128)(2,1)S(1)} %get-tuple-element.62), channel_id=1, source_target_pairs={{0,7},{1,2},{2,1},{3,4},{4,3},{5,6},{6,5},{7,0},{8,15},{9,10},{10,... | collective-permute-start | bytes 1769480 | tf_op jit(solution)/shard_map/ppermute | solution.py:40
  31.5 0.6 collective-permute-start.7
  32.1 0.9 collective-permute-start.9
  33.1 0.6 fusion.47
  33.8 0.5 fusion.81
  34.3 0.5 fusion.80
  34.8 4.5 %collective-permute-done.2 = bf16[256,1152]{1,0:T(8,128)(2,1)S(1)} collective-permute-done((bf16[256,1152]{1,0:T(8,128)(2,1)S(1)}, bf16[256,1152]{1,0:T(8,128)(2,1)S(1)}, u32[]{:S(2)}, u32[]{:S(2)}) %collective-permute-start.2) | collective-permute-done | bytes 589856 | tf_op jit(solution)/shard_map/ppermute | solution.py:40
  39.7 1.8 %collective-permute-done.7 = bf16[256,1152]{1,0:T(8,128)(2,1)S(1)} collective-permute-done((bf16[256,1152]{1,0:T(8,128)(2,1)S(1)}, bf16[256,1152]{1,0:T(8,128)(2,1)S(1)}, u32[]{:S(2)}, u32[]{:S(2)}) %collective-permute-start.7) | collective-permute-done | bytes 589856 | tf_op jit(solution)/shard_map/ppermute | solution.py:40
  41.5 0.6 fusion.50
  42.2 0.5 fusion.78
  42.7 1.0 %fusion.21 = bf16[512,512]{1,0:T(8,128)(2,1)S(1)} fusion(bf16[512,1152]{1,0:T(8,128)(2,1)S(1)} %constant_dynamic-update-slice_fusion.3, bf16[512,1152]{1,0:T(8,128)(2,1)S(1)} %constant_dynamic-update-slice_fusion.7, f32[]{:T(128)} %bitcast.36, f32[]{:T(128)} %bitcast.32), kind=kOutput, calls=%fused_computation.26 | convolution fusion | flops 605814784 | bytes 2883592 | tf_op jit(solution)/shard_map/dot_general | solution.py:88
  43.8 0.9 fusion.77
  44.7 1.0 %fusion.20 = bf16[512,512]{1,0:T(8,128)(2,1)S(1)} fusion(bf16[512,1152]{1,0:T(8,128)(2,1)S(1)} %collective-permute-done.10, bf16[512,1152]{1,0:T(8,128)(2,1)S(1)} %constant_dynamic-update-slice_fusion.7, f32[]{:T(128)} %bitcast.38, f32[]{:T(128)} %bitcast.30), kind=kOutput, calls=%fused_computation.25 | convolution fusion | flops 605814784 | bytes 2883592 | tf_op jit(solution)/shard_map/dot_general | solution.py:88
  45.7 0.9 fusion.79
  46.6 0.5 fusion.67
  47.4 0.6 fusion.49
  48.0 0.5 fusion.2
  48.8 1.6 %collective-permute-start.12 = (f16[256,1152]{1,0:T(8,128)(2,1)S(1)}, f16[256,1152]{1,0:T(8,128)(2,1)S(1)}, u32[]{:S(2)}, u32[]{:S(2)}) collective-permute-start(f16[256,1152]{1,0:T(8,128)(2,1)S(1)} %get-tuple-element.61), channel_id=1, source_target_pairs={{0,16},{1,17},{2,18},{3,19},{4,20},{5,21},{6,22},{7,23},{8,24},{9,... | collective-permute-start | bytes 1769480 | tf_op jit(solution)/shard_map/ppermute | solution.py:40
  50.4 1.2 %collective-permute-start.13 = (f16[256,1152]{1,0:T(8,128)(2,1)S(1)}, f16[256,1152]{1,0:T(8,128)(2,1)S(1)}, u32[]{:S(2)}, u32[]{:S(2)}) collective-permute-start(f16[256,1152]{1,0:T(8,128)(2,1)S(1)} %get-tuple-element.60), channel_id=1, source_target_pairs={{0,8},{1,9},{2,10},{3,11},{4,12},{5,13},{6,14},{7,15},{8,0},{9,1},... | collective-permute-start | bytes 1769480 | tf_op jit(solution)/shard_map/ppermute | solution.py:40
  52.4 0.6 collective-permute-start.14
  53.5 0.6 fusion.48
  54.2 0.5 fusion.3
  54.7 0.5 collective-permute-start.19
  55.2 1.2 %fusion.4 = f32[512,1152]{1,0:T(8,128)S(1)} fusion(bf16[512,1152]{1,0:T(8,128)(2,1)S(1)} %collective-permute-done.10, bf16[256,1152]{1,0:T(8,128)(2,1)S(1)} %collective-permute-done.2, bf16[256,512]{1,0:T(8,128)(2,1)S(1)} %fusion.49, bf16[256,512]{1,0:T(8,128)(2,1)S(1)} %fusion.48, bf16[256,512]{1,0:T(8,128)(2,1)S(1)} %fusion.50), kind=kOutput, calls=%fused_computation.7 | convolution fusion | flops 911867904 | bytes 4915200 | tf_op jit(solution)/shard_map/dot_general | solution.py:104
  56.7 0.5 fusion.71
  57.2 1.6 %collective-permute-done.12 = f16[256,1152]{1,0:T(8,128)(2,1)S(1)} collective-permute-done((f16[256,1152]{1,0:T(8,128)(2,1)S(1)}, f16[256,1152]{1,0:T(8,128)(2,1)S(1)}, u32[]{:S(2)}, u32[]{:S(2)}) %collective-permute-start.12) | collective-permute-done | bytes 589856 | tf_op jit(solution)/shard_map/ppermute | solution.py:40
  58.8 1.5 %collective-permute-done.13 = f16[256,1152]{1,0:T(8,128)(2,1)S(1)} collective-permute-done((f16[256,1152]{1,0:T(8,128)(2,1)S(1)}, f16[256,1152]{1,0:T(8,128)(2,1)S(1)}, u32[]{:S(2)}, u32[]{:S(2)}) %collective-permute-start.13) | collective-permute-done | bytes 589856 | tf_op jit(solution)/shard_map/ppermute | solution.py:40
  60.3 3.3 %collective-permute-done.14 = f16[256,1152]{1,0:T(8,128)(2,1)S(1)} collective-permute-done((f16[256,1152]{1,0:T(8,128)(2,1)S(1)}, f16[256,1152]{1,0:T(8,128)(2,1)S(1)}, u32[]{:S(2)}, u32[]{:S(2)}) %collective-permute-start.14) | collective-permute-done | bytes 589856 | tf_op jit(solution)/shard_map/ppermute | solution.py:40
  63.9 1.1 %collective-permute-start.15 = (f16[128,1152]{1,0:T(8,128)(2,1)S(1)}, f16[128,1152]{1,0:T(8,128)(2,1)S(1)}, u32[]{:S(2)}, u32[]{:S(2)}) collective-permute-start(f16[128,1152]{1,0:T(8,128)(2,1)S(1)} %fusion.60), channel_id=1, source_target_pairs={{0,8},{1,9},{2,10},{3,11},{4,12},{5,13},{6,14},{7,15},{8,0},{9,1},... | collective-permute-start | bytes 884744 | tf_op jit(solution)/shard_map/ppermute | solution.py:40
  65.1 0.6 collective-permute-start.16
  66.1 4.8 %collective-permute-done.15 = f16[128,1152]{1,0:T(8,128)(2,1)S(1)} collective-permute-done((f16[128,1152]{1,0:T(8,128)(2,1)S(1)}, f16[128,1152]{1,0:T(8,128)(2,1)S(1)}, u32[]{:S(2)}, u32[]{:S(2)}) %collective-permute-start.15) | collective-permute-done | bytes 294944 | tf_op jit(solution)/shard_map/ppermute | solution.py:40
  70.9 0.9 %collective-permute-done.16 = f16[128,1152]{1,0:T(8,128)(2,1)S(1)} collective-permute-done((f16[128,1152]{1,0:T(8,128)(2,1)S(1)}, f16[128,1152]{1,0:T(8,128)(2,1)S(1)}, u32[]{:S(2)}, u32[]{:S(2)}) %collective-permute-start.16) | collective-permute-done | bytes 294944 | tf_op jit(solution)/shard_map/ppermute | solution.py:40
  72.3 0.6 collective-permute-done.20
  73.0 5.4 %collective-permute-start.21 = (f16[64,1152]{1,0:T(8,128)(2,1)S(1)}, f16[64,1152]{1,0:T(8,128)(2,1)S(1)}, u32[]{:S(2)}, u32[]{:S(2)}) collective-permute-start(f16[64,1152]{1,0:T(8,128)(2,1)S(1)} %fusion.65), channel_id=1, source_target_pairs={{0,4},{1,5},{2,6},{3,7},{4,0},{5,1},{6,2},{7,3},{8,12},{9,13},{10,... | collective-permute-start | bytes 442376 | tf_op jit(solution)/shard_map/ppermute | solution.py:40
  78.3 1.7 %collective-permute-done.17 = f16[128,1152]{1,0:T(8,128)(2,1)S(1)} collective-permute-done((f16[128,1152]{1,0:T(8,128)(2,1)S(1)}, f16[128,1152]{1,0:T(8,128)(2,1)S(1)}, u32[]{:S(2)}, u32[]{:S(2)}) %collective-permute-start.17) | collective-permute-done | bytes 294944 | tf_op jit(solution)/shard_map/ppermute | solution.py:40
  80.2 2.8 %collective-permute-start.18 = (f16[64,1152]{1,0:T(8,128)(2,1)S(1)}, f16[64,1152]{1,0:T(8,128)(2,1)S(1)}, u32[]{:S(2)}, u32[]{:S(2)}) collective-permute-start(f16[64,1152]{1,0:T(8,128)(2,1)S(1)} %fusion.66), channel_id=1, source_target_pairs={{0,136},{1,137},{2,138},{3,139},{4,140},{5,141},{6,142},{7,143},{8... | collective-permute-start | bytes 442376 | tf_op jit(solution)/shard_map/ppermute | solution.py:40
  83.0 2.3 %collective-permute-done.21 = f16[64,1152]{1,0:T(8,128)(2,1)S(1)} collective-permute-done((f16[64,1152]{1,0:T(8,128)(2,1)S(1)}, f16[64,1152]{1,0:T(8,128)(2,1)S(1)}, u32[]{:S(2)}, u32[]{:S(2)}) %collective-permute-start.21) | collective-permute-done | bytes 147488 | tf_op jit(solution)/shard_map/ppermute | solution.py:40
  85.4 0.9 %shard_map.61 = f32[64,1152]{1,0:T(8,128)} custom-call(bf16[64,1152]{1,0:T(8,128)(2,1)S(1)} %copy-done.1, f32[64,1152]{1,0:T(8,128)S(1)} %slice_add_fusion.5.summed), custom_call_target="tpu_custom_call" | custom-call | tf_op jit(solution)/shard_map/pallas_call | solution.py:84
  86.7 0.9 %shard_map.60 = f32[64,1152]{1,0:T(8,128)} custom-call(bf16[64,1152]{1,0:T(8,128)(2,1)S(1)} %copy-done.3, f32[64,1152]{1,0:T(8,128)S(1)} %slice_add_fusion.6.summed), custom_call_target="tpu_custom_call" | custom-call | tf_op jit(solution)/shard_map/pallas_call | solution.py:84
  (58 shorter events, 5.4 us)
Async XLA Ops:
  0.6 0.9 %copy-start = (bf16[64,1152]{1,0:T(8,128)(2,1)S(1)}, bf16[64,1152]{1,0:T(8,128)(2,1)}, u32[]{:S(2)}) copy-start(bf16[64,1152]{1,0:T(8,128)(2,1)} %rows.3) | copy-start | bytes 442372
  1.5 0.9 %copy-start.2 = (bf16[64,1152]{1,0:T(8,128)(2,1)S(1)}, bf16[64,1152]{1,0:T(8,128)(2,1)}, u32[]{:S(2)}) copy-start(bf16[64,1152]{1,0:T(8,128)(2,1)} %rows.2) | copy-start | bytes 442372
  2.6 18.6 %collective-permute-start.3 = (bf16[64,1152]{1,0:T(8,128)(2,1)S(1)}, bf16[64,1152]{1,0:T(8,128)(2,1)S(1)}, u32[]{:S(2)}, u32[]{:S(2)}) collective-permute-start(bf16[64,1152]{1,0:T(8,128)(2,1)S(1)} %get-tuple-element.31), channel_id=1, source_target_pairs={{0,136},{1,137},{2,138},{3,139},{4,140},{5,141},{6,142},{7,143},{8... | collective-permute-start | bytes 442376 | tf_op jit(solution)/shard_map/ppermute | solution.py:40
  5.4 15.8 %collective-permute-start.4 = (bf16[64,1152]{1,0:T(8,128)(2,1)S(1)}, bf16[64,1152]{1,0:T(8,128)(2,1)S(1)}, u32[]{:S(2)}, u32[]{:S(2)}) collective-permute-start(bf16[64,1152]{1,0:T(8,128)(2,1)S(1)} %get-tuple-element.31), channel_id=1, source_target_pairs={{0,48},{1,49},{2,50},{3,51},{4,52},{5,53},{6,54},{7,55},{8,56},{9,... | collective-permute-start | bytes 442376 | tf_op jit(solution)/shard_map/ppermute | solution.py:40
  5.7 15.5 %collective-permute-start.5 = (bf16[64,1152]{1,0:T(8,128)(2,1)S(1)}, bf16[64,1152]{1,0:T(8,128)(2,1)S(1)}, u32[]{:S(2)}, u32[]{:S(2)}) collective-permute-start(bf16[64,1152]{1,0:T(8,128)(2,1)S(1)} %get-tuple-element.31), channel_id=1, source_target_pairs={{0,184},{1,185},{2,186},{3,187},{4,188},{5,189},{6,190},{7,191},{8... | collective-permute-start | bytes 442376 | tf_op jit(solution)/shard_map/ppermute | solution.py:40
  8.6 11.4 %collective-permute-start = (bf16[64,1152]{1,0:T(8,128)(2,1)S(1)}, bf16[64,1152]{1,0:T(8,128)(2,1)S(1)}, u32[]{:S(2)}, u32[]{:S(2)}) collective-permute-start(bf16[64,1152]{1,0:T(8,128)(2,1)S(1)} %get-tuple-element.30), channel_id=1, source_target_pairs={{0,4},{1,5},{2,6},{3,7},{4,0},{5,1},{6,2},{7,3},{8,12},{9,13},{10,... | collective-permute-start | bytes 442376 | tf_op jit(solution)/shard_map/ppermute | solution.py:40
  20.0 7.1 %collective-permute-start.1 = (bf16[128,1152]{1,0:T(8,128)(2,1)S(1)}, bf16[128,1152]{1,0:T(8,128)(2,1)S(1)}, u32[]{:S(2)}, u32[]{:S(2)}) collective-permute-start(bf16[128,1152]{1,0:T(8,128)(2,1)S(1)} %pad_maximum_fusion.2), channel_id=1, source_target_pairs={{0,1},{1,0},{2,3},{3,2},{4,5},{5,4},{6,7},{7,6},{8,9},{9,8},{10,11... | collective-permute-start | bytes 884744 | tf_op jit(solution)/shard_map/ppermute | solution.py:40
  21.2 10.2 %collective-permute-start.6 = (bf16[128,1152]{1,0:T(8,128)(2,1)S(1)}, bf16[128,1152]{1,0:T(8,128)(2,1)S(1)}, u32[]{:S(2)}, u32[]{:S(2)}) collective-permute-start(bf16[128,1152]{1,0:T(8,128)(2,1)S(1)} %pad_maximum_fusion.3), channel_id=1, source_target_pairs={{0,8},{1,9},{2,10},{3,11},{4,12},{5,13},{6,14},{7,15},{8,0},{9,1},... | collective-permute-start | bytes 884744 | tf_op jit(solution)/shard_map/ppermute | solution.py:40
  21.4 10.7 %collective-permute-start.8 = (bf16[128,1152]{1,0:T(8,128)(2,1)S(1)}, bf16[128,1152]{1,0:T(8,128)(2,1)S(1)}, u32[]{:S(2)}, u32[]{:S(2)}) collective-permute-start(bf16[128,1152]{1,0:T(8,128)(2,1)S(1)} %pad_maximum_fusion.4), channel_id=1, source_target_pairs={{0,16},{1,17},{2,18},{3,19},{4,20},{5,21},{6,22},{7,23},{8,24},{9,... | collective-permute-start | bytes 884744 | tf_op jit(solution)/shard_map/ppermute | solution.py:40
  27.2 12.1 %collective-permute-start.2 = (bf16[256,1152]{1,0:T(8,128)(2,1)S(1)}, bf16[256,1152]{1,0:T(8,128)(2,1)S(1)}, u32[]{:S(2)}, u32[]{:S(2)}) collective-permute-start(bf16[256,1152]{1,0:T(8,128)(2,1)S(1)} %get-tuple-element.62), channel_id=1, source_target_pairs={{0,7},{1,2},{2,1},{3,4},{4,3},{5,6},{6,5},{7,0},{8,15},{9,10},{10,... | collective-permute-start | bytes 1769480 | tf_op jit(solution)/shard_map/ppermute | solution.py:40
  31.5 10.0 %collective-permute-start.7 = (bf16[256,1152]{1,0:T(8,128)(2,1)S(1)}, bf16[256,1152]{1,0:T(8,128)(2,1)S(1)}, u32[]{:S(2)}, u32[]{:S(2)}) collective-permute-start(bf16[256,1152]{1,0:T(8,128)(2,1)S(1)} %pad_maximum_fusion), channel_id=1, source_target_pairs={{0,16},{1,17},{2,18},{3,19},{4,20},{5,21},{6,22},{7,23},{8,24},{9,... | collective-permute-start | bytes 1769480 | tf_op jit(solution)/shard_map/ppermute | solution.py:40
  32.1 10.0 %collective-permute-start.9 = (bf16[256,1152]{1,0:T(8,128)(2,1)S(1)}, bf16[256,1152]{1,0:T(8,128)(2,1)S(1)}, u32[]{:S(2)}, u32[]{:S(2)}) collective-permute-start(bf16[256,1152]{1,0:T(8,128)(2,1)S(1)} %pad_maximum_fusion.1), channel_id=1, source_target_pairs={{0,8},{1,9},{2,10},{3,11},{4,12},{5,13},{6,14},{7,15},{8,0},{9,1},... | collective-permute-start | bytes 1769480 | tf_op jit(solution)/shard_map/ppermute | solution.py:40
  39.4 5.3 %collective-permute-start.10 = (bf16[512,1152]{1,0:T(8,128)(2,1)S(1)}, bf16[512,1152]{1,0:T(8,128)(2,1)S(1)}, u32[]{:S(2)}, u32[]{:S(2)}) collective-permute-start(bf16[512,1152]{1,0:T(8,128)(2,1)S(1)} %constant_dynamic-update-slice_fusion.3), channel_id=1, source_target_pairs={{0,64},{1,65},{2,66},{3,67},{4,68},{5,69},{6,70},{7,71},{8,72},{9,... | collective-permute-start | bytes 3538952 | tf_op jit(solution)/shard_map/ppermute | solution.py:40
  48.5 3.6 %collective-permute-start.11 = (f16[256,1152]{1,0:T(8,128)(2,1)S(1)}, f16[256,1152]{1,0:T(8,128)(2,1)S(1)}, u32[]{:S(2)}, u32[]{:S(2)}) collective-permute-start(f16[256,1152]{1,0:T(8,128)(2,1)S(1)} %fusion.2), channel_id=1, source_target_pairs={{0,64},{1,65},{2,66},{3,67},{4,68},{5,69},{6,70},{7,71},{8,72},{9,... | collective-permute-start | bytes 1769480 | tf_op jit(solution)/shard_map/ppermute | solution.py:40
  48.8 10.0 %collective-permute-start.12 = (f16[256,1152]{1,0:T(8,128)(2,1)S(1)}, f16[256,1152]{1,0:T(8,128)(2,1)S(1)}, u32[]{:S(2)}, u32[]{:S(2)}) collective-permute-start(f16[256,1152]{1,0:T(8,128)(2,1)S(1)} %get-tuple-element.61), channel_id=1, source_target_pairs={{0,16},{1,17},{2,18},{3,19},{4,20},{5,21},{6,22},{7,23},{8,24},{9,... | collective-permute-start | bytes 1769480 | tf_op jit(solution)/shard_map/ppermute | solution.py:40
  50.4 9.9 %collective-permute-start.13 = (f16[256,1152]{1,0:T(8,128)(2,1)S(1)}, f16[256,1152]{1,0:T(8,128)(2,1)S(1)}, u32[]{:S(2)}, u32[]{:S(2)}) collective-permute-start(f16[256,1152]{1,0:T(8,128)(2,1)S(1)} %get-tuple-element.60), channel_id=1, source_target_pairs={{0,8},{1,9},{2,10},{3,11},{4,12},{5,13},{6,14},{7,15},{8,0},{9,1},... | collective-permute-start | bytes 1769480 | tf_op jit(solution)/shard_map/ppermute | solution.py:40
  52.4 11.2 %collective-permute-start.14 = (f16[256,1152]{1,0:T(8,128)(2,1)S(1)}, f16[256,1152]{1,0:T(8,128)(2,1)S(1)}, u32[]{:S(2)}, u32[]{:S(2)}) collective-permute-start(f16[256,1152]{1,0:T(8,128)(2,1)S(1)} %multiply_convert_fusion.1), channel_id=1, source_target_pairs={{0,7},{1,2},{2,1},{3,4},{4,3},{5,6},{6,5},{7,0},{8,15},{9,10},{10,... | collective-permute-start | bytes 1769480 | tf_op jit(solution)/shard_map/ppermute | solution.py:40
  54.7 11.0 %collective-permute-start.19 = (f16[256,1152]{1,0:T(8,128)(2,1)S(1)}, f16[256,1152]{1,0:T(8,128)(2,1)S(1)}, u32[]{:S(2)}, u32[]{:S(2)}) collective-permute-start(f16[256,1152]{1,0:T(8,128)(2,1)S(1)} %fusion.3), channel_id=1, source_target_pairs={{0,64},{1,65},{2,66},{3,67},{4,68},{5,69},{6,70},{7,71},{8,72},{9,... | collective-permute-start | bytes 1769480 | tf_op jit(solution)/shard_map/ppermute | solution.py:40
  63.9 7.0 %collective-permute-start.15 = (f16[128,1152]{1,0:T(8,128)(2,1)S(1)}, f16[128,1152]{1,0:T(8,128)(2,1)S(1)}, u32[]{:S(2)}, u32[]{:S(2)}) collective-permute-start(f16[128,1152]{1,0:T(8,128)(2,1)S(1)} %fusion.60), channel_id=1, source_target_pairs={{0,8},{1,9},{2,10},{3,11},{4,12},{5,13},{6,14},{7,15},{8,0},{9,1},... | collective-permute-start | bytes 884744 | tf_op jit(solution)/shard_map/ppermute | solution.py:40
  65.1 6.8 %collective-permute-start.16 = (f16[128,1152]{1,0:T(8,128)(2,1)S(1)}, f16[128,1152]{1,0:T(8,128)(2,1)S(1)}, u32[]{:S(2)}, u32[]{:S(2)}) collective-permute-start(f16[128,1152]{1,0:T(8,128)(2,1)S(1)} %fusion.59), channel_id=1, source_target_pairs={{0,16},{1,17},{2,18},{3,19},{4,20},{5,21},{6,22},{7,23},{8,24},{9,... | collective-permute-start | bytes 884744 | tf_op jit(solution)/shard_map/ppermute | solution.py:40
  66.0 6.8 %collective-permute-start.20 = (f16[128,1152]{1,0:T(8,128)(2,1)S(1)}, f16[128,1152]{1,0:T(8,128)(2,1)S(1)}, u32[]{:S(2)}, u32[]{:S(2)}) collective-permute-start(f16[128,1152]{1,0:T(8,128)(2,1)S(1)} %fusion.56), channel_id=1, source_target_pairs={{0,1},{1,0},{2,3},{3,2},{4,5},{5,4},{6,7},{7,6},{8,9},{9,8},{10,11... | collective-permute-start | bytes 884744 | tf_op jit(solution)/shard_map/ppermute | solution.py:40
  72.0 8.0 %collective-permute-start.17 = (f16[128,1152]{1,0:T(8,128)(2,1)S(1)}, f16[128,1152]{1,0:T(8,128)(2,1)S(1)}, u32[]{:S(2)}, u32[]{:S(2)}) collective-permute-start(f16[128,1152]{1,0:T(8,128)(2,1)S(1)} %fusion.58), channel_id=1, source_target_pairs={{0,48},{1,49},{2,50},{3,51},{4,52},{5,53},{6,54},{7,55},{8,56},{9,... | collective-permute-start | bytes 884744 | tf_op jit(solution)/shard_map/ppermute | solution.py:40
  73.0 12.4 %copy-start.1 = (bf16[64,1152]{1,0:T(8,128)(2,1)S(1)}, bf16[64,1152]{1,0:T(8,128)(2,1)}, u32[]{:S(2)}) copy-start(bf16[64,1152]{1,0:T(8,128)(2,1)} %rows.3) | copy-start | bytes 442372
  73.0 12.3 %collective-permute-start.21 = (f16[64,1152]{1,0:T(8,128)(2,1)S(1)}, f16[64,1152]{1,0:T(8,128)(2,1)S(1)}, u32[]{:S(2)}, u32[]{:S(2)}) collective-permute-start(f16[64,1152]{1,0:T(8,128)(2,1)S(1)} %fusion.65), channel_id=1, source_target_pairs={{0,4},{1,5},{2,6},{3,7},{4,0},{5,1},{6,2},{7,3},{8,12},{9,13},{10,... | collective-permute-start | bytes 442376 | tf_op jit(solution)/shard_map/ppermute | solution.py:40
  80.2 6.5 %copy-start.3 = (bf16[64,1152]{1,0:T(8,128)(2,1)S(1)}, bf16[64,1152]{1,0:T(8,128)(2,1)}, u32[]{:S(2)}) copy-start(bf16[64,1152]{1,0:T(8,128)(2,1)} %rows.2) | copy-start | bytes 442372
  80.2 6.4 %collective-permute-start.18 = (f16[64,1152]{1,0:T(8,128)(2,1)S(1)}, f16[64,1152]{1,0:T(8,128)(2,1)S(1)}, u32[]{:S(2)}, u32[]{:S(2)}) collective-permute-start(f16[64,1152]{1,0:T(8,128)(2,1)S(1)} %fusion.66), channel_id=1, source_target_pairs={{0,136},{1,137},{2,138},{3,139},{4,140},{5,141},{6,142},{7,143},{8... | collective-permute-start | bytes 442376 | tf_op jit(solution)/shard_map/ppermute | solution.py:40

commit v6 on v5

--- a/solution.py
+++ b/solution.py
@@ -113,7 +113,7 @@
     t1 = swap(text_low, ZFAR)
     x1, y1, xy1 = step(swap(image_low, X0), swap(image_low, Y0), swap(image_low, XY))
     t, a, b = join(text_low, t1), join(image_low, x1), join(y1, xy1)
-    got_t, got_a, got_b = swap(t, Z0), swap(a, X1), swap(b, Y1)
+    got_a, got_b, got_t = swap(a, X1), swap(b, Y1), swap(t, Z0)
     own_a, a, b = join(t, got_t), join(a, got_a), join(b, got_b)
     first = join(a, b)
     got_a, got_b, own_b = swap(a, Y1), swap(b, X1), swap(own_a, Z1)
@@ -161,7 +161,7 @@
         join(first_own_b, first_other_a, first_other_b), join(own_b, other)
     )
 
-    got_a, got_b, got_t = step(got_a, got_b, got_t)
+    got_a, got_t = step(got_a, got_t)
     a, b, t = sum_first[:h] + grown(got_a), sum_first[h:] + grown(got_b), t + grown(got_t)
     m = 2 * n
     got_a, got_b = step(swap(shrunk(a[m:]), X1), swap(shrunk(b[m:]), Y1))

time: 88.1 us -> 88.2 us (level)
  transfers between devices with their start and end apart: 22 -> 22, of which waited for: 13 -> 12; matrix products, arithmetic and copies ran while one was open for 12% -> 12% of each run, Pallas kernels for 1% -> 1%
where the time goes in v6:
time: 88.2 us; the launch traced here: 87.6 us
  starting transfers between devices  36.3 us (41%)
  waiting for transfers between devices  30.4 us (34%)
  matrix products  12.1 us (14%)
  local copies, waits for them, and re-layouts  2.46 us (3%)
  between operations  2.33 us (3%)
  other arithmetic  2.09 us (2%)
  Pallas kernels  2.01 us (2%)
    ppermute x22, starting transfers between devices, swap(): return lax.ppermute(array, AXES, list(enumerate(partner)))  36.3 us
    ppermute x22, waiting for transfers between devices, swap(): return lax.ppermute(array, AXES, list(enumerate(partner)))  30.4 us
    dot_general x6, matrix products, weights_of(): lax.dot_general(texts, images, (((1,), (1,)), ((), ())), preferred_elemen...  4.52 us
    dot_general x8, matrix products, dot(): return jnp.dot(a, b, preferred_element_type=jnp.float32)  4.06 us
    dot_general x4, matrix products, dot_t(): lax.dot_general(a, b, (((0,), (0,)), ((), ())), preferred_element_type=jn...  3.48 us
    unnamed x15, local copies, waits for them, and re-layouts  2.02 us
    pallas_call x2, Pallas kernels, grad_rows(): pl.pallas_call(grad_kernel, out_shape=out, compiler_params=SMALL)  1.86 us
  transfers between devices with their start and end apart: 22, of which 12 were waited for; matrix products, arithmetic and copies ran while one was open for 12% of the time, Pallas kernels for 1%

profile of v6, /device:TPU:24, one launch (start us, length us, event | category | flops | bytes accessed | tf_op | source)
XLA Modules:
  0.0 87.6 jit_solution(15257740681391087656)
XLA Ops:
  0.6 0.9 %copy-done = bf16[64,1152]{1,0:T(8,128)(2,1)S(1)} copy-done((bf16[64,1152]{1,0:T(8,128)(2,1)S(1)}, bf16[64,1152]{1,0:T(8,128)(2,1)}, u32[]{:S(2)}) %copy-start) | copy-done | bytes 147480
  1.5 0.9 %copy-done.2 = bf16[64,1152]{1,0:T(8,128)(2,1)S(1)} copy-done((bf16[64,1152]{1,0:T(8,128)(2,1)S(1)}, bf16[64,1152]{1,0:T(8,128)(2,1)}, u32[]{:S(2)}) %copy-start.2) | copy-done | bytes 147480
  2.6 2.8 %collective-permute-start.3 = (bf16[64,1152]{1,0:T(8,128)(2,1)S(1)}, bf16[64,1152]{1,0:T(8,128)(2,1)S(1)}, u32[]{:S(2)}, u32[]{:S(2)}) collective-permute-start(bf16[64,1152]{1,0:T(8,128)(2,1)S(1)} %get-tuple-element.30), channel_id=1, source_target_pairs={{0,136},{1,137},{2,138},{3,139},{4,140},{5,141},{6,142},{7,143},{8... | collective-permute-start | bytes 442376 | tf_op jit(solution)/shard_map/ppermute | solution.py:40
  5.7 2.9 %collective-permute-start.5 = (bf16[64,1152]{1,0:T(8,128)(2,1)S(1)}, bf16[64,1152]{1,0:T(8,128)(2,1)S(1)}, u32[]{:S(2)}, u32[]{:S(2)}) collective-permute-start(bf16[64,1152]{1,0:T(8,128)(2,1)S(1)} %get-tuple-element.30), channel_id=1, source_target_pairs={{0,184},{1,185},{2,186},{3,187},{4,188},{5,189},{6,190},{7,191},{8... | collective-permute-start | bytes 442376 | tf_op jit(solution)/shard_map/ppermute | solution.py:40
  8.6 7.2 %collective-permute-start = (bf16[64,1152]{1,0:T(8,128)(2,1)S(1)}, bf16[64,1152]{1,0:T(8,128)(2,1)S(1)}, u32[]{:S(2)}, u32[]{:S(2)}) collective-permute-start(bf16[64,1152]{1,0:T(8,128)(2,1)S(1)} %get-tuple-element.29), channel_id=1, source_target_pairs={{0,4},{1,5},{2,6},{3,7},{4,0},{5,1},{6,2},{7,3},{8,12},{9,13},{10,... | collective-permute-start | bytes 442376 | tf_op jit(solution)/shard_map/ppermute | solution.py:40
  17.1 2.9 %collective-permute-done = bf16[64,1152]{1,0:T(8,128)(2,1)S(1)} collective-permute-done((bf16[64,1152]{1,0:T(8,128)(2,1)S(1)}, bf16[64,1152]{1,0:T(8,128)(2,1)S(1)}, u32[]{:S(2)}, u32[]{:S(2)}) %collective-permute-start) | collective-permute-done | bytes 147488 | tf_op jit(solution)/shard_map/ppermute | solution.py:40
  20.0 1.2 %collective-permute-start.1 = (bf16[128,1152]{1,0:T(8,128)(2,1)S(1)}, bf16[128,1152]{1,0:T(8,128)(2,1)S(1)}, u32[]{:S(2)}, u32[]{:S(2)}) collective-permute-start(bf16[128,1152]{1,0:T(8,128)(2,1)S(1)} %pad_maximum_fusion.2), channel_id=1, source_target_pairs={{0,1},{1,0},{2,3},{3,2},{4,5},{5,4},{6,7},{7,6},{8,9},{9,8},{10,11... | collective-permute-start | bytes 884744 | tf_op jit(solution)/shard_map/ppermute | solution.py:40
  21.4 1.5 %collective-permute-start.8 = (bf16[128,1152]{1,0:T(8,128)(2,1)S(1)}, bf16[128,1152]{1,0:T(8,128)(2,1)S(1)}, u32[]{:S(2)}, u32[]{:S(2)}) collective-permute-start(bf16[128,1152]{1,0:T(8,128)(2,1)S(1)} %pad_maximum_fusion.4), channel_id=1, source_target_pairs={{0,16},{1,17},{2,18},{3,19},{4,20},{5,21},{6,22},{7,23},{8,24},{9,... | collective-permute-start | bytes 884744 | tf_op jit(solution)/shard_map/ppermute | solution.py:40
  22.9 4.2 %collective-permute-done.1 = bf16[128,1152]{1,0:T(8,128)(2,1)S(1)} collective-permute-done((bf16[128,1152]{1,0:T(8,128)(2,1)S(1)}, bf16[128,1152]{1,0:T(8,128)(2,1)S(1)}, u32[]{:S(2)}, u32[]{:S(2)}) %collective-permute-start.1) | collective-permute-done | bytes 294944 | tf_op jit(solution)/shard_map/ppermute | solution.py:40
  27.2 4.3 %collective-permute-start.2 = (bf16[256,1152]{1,0:T(8,128)(2,1)S(1)}, bf16[256,1152]{1,0:T(8,128)(2,1)S(1)}, u32[]{:S(2)}, u32[]{:S(2)}) collective-permute-start(bf16[256,1152]{1,0:T(8,128)(2,1)S(1)} %get-tuple-element.60), channel_id=1, source_target_pairs={{0,7},{1,2},{2,1},{3,4},{4,3},{5,6},{6,5},{7,0},{8,15},{9,10},{10,... | collective-permute-start | bytes 1769480 | tf_op jit(solution)/shard_map/ppermute | solution.py:40
  31.5 0.6 collective-permute-start.7
  32.1 0.9 collective-permute-start.9
  33.1 0.6 fusion.47
  33.8 0.5 fusion.81
  34.3 0.5 fusion.80
  34.8 4.5 %collective-permute-done.2 = bf16[256,1152]{1,0:T(8,128)(2,1)S(1)} collective-permute-done((bf16[256,1152]{1,0:T(8,128)(2,1)S(1)}, bf16[256,1152]{1,0:T(8,128)(2,1)S(1)}, u32[]{:S(2)}, u32[]{:S(2)}) %collective-permute-start.2) | collective-permute-done | bytes 589856 | tf_op jit(solution)/shard_map/ppermute | solution.py:40
  39.7 1.8 %collective-permute-done.7 = bf16[256,1152]{1,0:T(8,128)(2,1)S(1)} collective-permute-done((bf16[256,1152]{1,0:T(8,128)(2,1)S(1)}, bf16[256,1152]{1,0:T(8,128)(2,1)S(1)}, u32[]{:S(2)}, u32[]{:S(2)}) %collective-permute-start.7) | collective-permute-done | bytes 589856 | tf_op jit(solution)/shard_map/ppermute | solution.py:40
  41.5 0.6 fusion.50
  42.2 0.5 fusion.78
  42.7 1.0 %fusion.21 = bf16[512,512]{1,0:T(8,128)(2,1)S(1)} fusion(bf16[512,1152]{1,0:T(8,128)(2,1)S(1)} %constant_dynamic-update-slice_fusion.3, bf16[512,1152]{1,0:T(8,128)(2,1)S(1)} %constant_dynamic-update-slice_fusion.7, f32[]{:T(128)} %bitcast.36, f32[]{:T(128)} %bitcast.32), kind=kOutput, calls=%fused_computation.26 | convolution fusion | flops 605814784 | bytes 2883592 | tf_op jit(solution)/shard_map/dot_general | solution.py:88
  43.8 0.9 fusion.77
  44.7 1.0 %fusion.20 = bf16[512,512]{1,0:T(8,128)(2,1)S(1)} fusion(bf16[512,1152]{1,0:T(8,128)(2,1)S(1)} %collective-permute-done.10, bf16[512,1152]{1,0:T(8,128)(2,1)S(1)} %constant_dynamic-update-slice_fusion.7, f32[]{:T(128)} %bitcast.38, f32[]{:T(128)} %bitcast.30), kind=kOutput, calls=%fused_computation.25 | convolution fusion | flops 605814784 | bytes 2883592 | tf_op jit(solution)/shard_map/dot_general | solution.py:88
  45.7 0.9 fusion.79
  46.6 0.5 fusion.67
  47.4 0.6 fusion.49
  48.0 0.5 fusion.2
  48.8 1.3 %collective-permute-start.15 = (f16[256,1152]{1,0:T(8,128)(2,1)S(1)}, f16[256,1152]{1,0:T(8,128)(2,1)S(1)}, u32[]{:S(2)}, u32[]{:S(2)}) collective-permute-start(f16[256,1152]{1,0:T(8,128)(2,1)S(1)} %get-tuple-element.58), channel_id=1, source_target_pairs={{0,8},{1,9},{2,10},{3,11},{4,12},{5,13},{6,14},{7,15},{8,0},{9,1},... | collective-permute-start | bytes 1769480 | tf_op jit(solution)/shard_map/ppermute | solution.py:40
  50.2 1.5 %collective-permute-start.12 = (f16[256,1152]{1,0:T(8,128)(2,1)S(1)}, f16[256,1152]{1,0:T(8,128)(2,1)S(1)}, u32[]{:S(2)}, u32[]{:S(2)}) collective-permute-start(f16[256,1152]{1,0:T(8,128)(2,1)S(1)} %get-tuple-element.59), channel_id=1, source_target_pairs={{0,16},{1,17},{2,18},{3,19},{4,20},{5,21},{6,22},{7,23},{8,24},{9,... | collective-permute-start | bytes 1769480 | tf_op jit(solution)/shard_map/ppermute | solution.py:40
  52.4 0.5 collective-permute-start.13
  52.9 0.5 fusion.69
  53.4 0.6 fusion.48
  54.1 0.5 fusion.3
  54.6 0.6 collective-permute-start.19
  55.2 1.2 %fusion.4 = f32[512,1152]{1,0:T(8,128)S(1)} fusion(bf16[512,1152]{1,0:T(8,128)(2,1)S(1)} %collective-permute-done.10, bf16[256,1152]{1,0:T(8,128)(2,1)S(1)} %collective-permute-done.2, bf16[256,512]{1,0:T(8,128)(2,1)S(1)} %fusion.49, bf16[256,512]{1,0:T(8,128)(2,1)S(1)} %fusion.48, bf16[256,512]{1,0:T(8,128)(2,1)S(1)} %fusion.50), kind=kOutput, calls=%fused_computation.7 | convolution fusion | flops 911867904 | bytes 4915200 | tf_op jit(solution)/shard_map/dot_general | solution.py:104
  56.7 0.5 fusion.71
  57.2 2.8 %collective-permute-done.12 = f16[256,1152]{1,0:T(8,128)(2,1)S(1)} collective-permute-done((f16[256,1152]{1,0:T(8,128)(2,1)S(1)}, f16[256,1152]{1,0:T(8,128)(2,1)S(1)}, u32[]{:S(2)}, u32[]{:S(2)}) %collective-permute-start.12) | collective-permute-done | bytes 589856 | tf_op jit(solution)/shard_map/ppermute | solution.py:40
  60.0 3.5 %collective-permute-done.13 = f16[256,1152]{1,0:T(8,128)(2,1)S(1)} collective-permute-done((f16[256,1152]{1,0:T(8,128)(2,1)S(1)}, f16[256,1152]{1,0:T(8,128)(2,1)S(1)}, u32[]{:S(2)}, u32[]{:S(2)}) %collective-permute-start.13) | collective-permute-done | bytes 589856 | tf_op jit(solution)/shard_map/ppermute | solution.py:40
  63.9 1.1 %collective-permute-start.14 = (f16[128,1152]{1,0:T(8,128)(2,1)S(1)}, f16[128,1152]{1,0:T(8,128)(2,1)S(1)}, u32[]{:S(2)}, u32[]{:S(2)}) collective-permute-start(f16[128,1152]{1,0:T(8,128)(2,1)S(1)} %fusion.60), channel_id=1, source_target_pairs={{0,8},{1,9},{2,10},{3,11},{4,12},{5,13},{6,14},{7,15},{8,0},{9,1},... | collective-permute-start | bytes 884744 | tf_op jit(solution)/shard_map/ppermute | solution.py:40
  65.1 0.6 collective-permute-start.16
  66.1 4.8 %collective-permute-done.14 = f16[128,1152]{1,0:T(8,128)(2,1)S(1)} collective-permute-done((f16[128,1152]{1,0:T(8,128)(2,1)S(1)}, f16[128,1152]{1,0:T(8,128)(2,1)S(1)}, u32[]{:S(2)}, u32[]{:S(2)}) %collective-permute-start.14) | collective-permute-done | bytes 294944 | tf_op jit(solution)/shard_map/ppermute | solution.py:40
  70.9 0.9 %collective-permute-done.16 = f16[128,1152]{1,0:T(8,128)(2,1)S(1)} collective-permute-done((f16[128,1152]{1,0:T(8,128)(2,1)S(1)}, f16[128,1152]{1,0:T(8,128)(2,1)S(1)}, u32[]{:S(2)}, u32[]{:S(2)}) %collective-permute-start.16) | collective-permute-done | bytes 294944 | tf_op jit(solution)/shard_map/ppermute | solution.py:40
  72.3 0.6 collective-permute-done.20
  73.0 5.4 %collective-permute-start.21 = (f16[64,1152]{1,0:T(8,128)(2,1)S(1)}, f16[64,1152]{1,0:T(8,128)(2,1)S(1)}, u32[]{:S(2)}, u32[]{:S(2)}) collective-permute-start(f16[64,1152]{1,0:T(8,128)(2,1)S(1)} %fusion.65), channel_id=1, source_target_pairs={{0,4},{1,5},{2,6},{3,7},{4,0},{5,1},{6,2},{7,3},{8,12},{9,13},{10,... | collective-permute-start | bytes 442376 | tf_op jit(solution)/shard_map/ppermute | solution.py:40
  78.3 1.7 %collective-permute-done.17 = f16[128,1152]{1,0:T(8,128)(2,1)S(1)} collective-permute-done((f16[128,1152]{1,0:T(8,128)(2,1)S(1)}, f16[128,1152]{1,0:T(8,128)(2,1)S(1)}, u32[]{:S(2)}, u32[]{:S(2)}) %collective-permute-start.17) | collective-permute-done | bytes 294944 | tf_op jit(solution)/shard_map/ppermute | solution.py:40
  80.2 2.8 %collective-permute-start.18 = (f16[64,1152]{1,0:T(8,128)(2,1)S(1)}, f16[64,1152]{1,0:T(8,128)(2,1)S(1)}, u32[]{:S(2)}, u32[]{:S(2)}) collective-permute-start(f16[64,1152]{1,0:T(8,128)(2,1)S(1)} %fusion.66), channel_id=1, source_target_pairs={{0,136},{1,137},{2,138},{3,139},{4,140},{5,141},{6,142},{7,143},{8... | collective-permute-start | bytes 442376 | tf_op jit(solution)/shard_map/ppermute | solution.py:40
  83.0 2.4 %collective-permute-done.21 = f16[64,1152]{1,0:T(8,128)(2,1)S(1)} collective-permute-done((f16[64,1152]{1,0:T(8,128)(2,1)S(1)}, f16[64,1152]{1,0:T(8,128)(2,1)S(1)}, u32[]{:S(2)}, u32[]{:S(2)}) %collective-permute-start.21) | collective-permute-done | bytes 147488 | tf_op jit(solution)/shard_map/ppermute | solution.py:40
  85.5 0.9 %shard_map.61 = f32[64,1152]{1,0:T(8,128)} custom-call(bf16[64,1152]{1,0:T(8,128)(2,1)S(1)} %copy-done.1, f32[64,1152]{1,0:T(8,128)S(1)} %slice_add_fusion.5.summed), custom_call_target="tpu_custom_call" | custom-call | tf_op jit(solution)/shard_map/pallas_call | solution.py:84
  86.7 0.9 %shard_map.60 = f32[64,1152]{1,0:T(8,128)} custom-call(bf16[64,1152]{1,0:T(8,128)(2,1)S(1)} %copy-done.3, f32[64,1152]{1,0:T(8,128)S(1)} %slice_add_fusion.6.summed), custom_call_target="tpu_custom_call" | custom-call | tf_op jit(solution)/shard_map/pallas_call | solution.py:84
  (58 shorter events, 4.7 us)
Async XLA Ops:
  0.6 0.9 %copy-start = (bf16[64,1152]{1,0:T(8,128)(2,1)S(1)}, bf16[64,1152]{1,0:T(8,128)(2,1)}, u32[]{:S(2)}) copy-start(bf16[64,1152]{1,0:T(8,128)(2,1)} %rows.3) | copy-start | bytes 442372
  1.5 0.9 %copy-start.2 = (bf16[64,1152]{1,0:T(8,128)(2,1)S(1)}, bf16[64,1152]{1,0:T(8,128)(2,1)}, u32[]{:S(2)}) copy-start(bf16[64,1152]{1,0:T(8,128)(2,1)} %rows.2) | copy-start | bytes 442372
  2.6 18.6 %collective-permute-start.3 = (bf16[64,1152]{1,0:T(8,128)(2,1)S(1)}, bf16[64,1152]{1,0:T(8,128)(2,1)S(1)}, u32[]{:S(2)}, u32[]{:S(2)}) collective-permute-start(bf16[64,1152]{1,0:T(8,128)(2,1)S(1)} %get-tuple-element.30), channel_id=1, source_target_pairs={{0,136},{1,137},{2,138},{3,139},{4,140},{5,141},{6,142},{7,143},{8... | collective-permute-start | bytes 442376 | tf_op jit(solution)/shard_map/ppermute | solution.py:40
  5.4 15.8 %collective-permute-start.4 = (bf16[64,1152]{1,0:T(8,128)(2,1)S(1)}, bf16[64,1152]{1,0:T(8,128)(2,1)S(1)}, u32[]{:S(2)}, u32[]{:S(2)}) collective-permute-start(bf16[64,1152]{1,0:T(8,128)(2,1)S(1)} %get-tuple-element.30), channel_id=1, source_target_pairs={{0,48},{1,49},{2,50},{3,51},{4,52},{5,53},{6,54},{7,55},{8,56},{9,... | collective-permute-start | bytes 442376 | tf_op jit(solution)/shard_map/ppermute | solution.py:40
  5.7 15.5 %collective-permute-start.5 = (bf16[64,1152]{1,0:T(8,128)(2,1)S(1)}, bf16[64,1152]{1,0:T(8,128)(2,1)S(1)}, u32[]{:S(2)}, u32[]{:S(2)}) collective-permute-start(bf16[64,1152]{1,0:T(8,128)(2,1)S(1)} %get-tuple-element.30), channel_id=1, source_target_pairs={{0,184},{1,185},{2,186},{3,187},{4,188},{5,189},{6,190},{7,191},{8... | collective-permute-start | bytes 442376 | tf_op jit(solution)/shard_map/ppermute | solution.py:40
  8.6 11.4 %collective-permute-start = (bf16[64,1152]{1,0:T(8,128)(2,1)S(1)}, bf16[64,1152]{1,0:T(8,128)(2,1)S(1)}, u32[]{:S(2)}, u32[]{:S(2)}) collective-permute-start(bf16[64,1152]{1,0:T(8,128)(2,1)S(1)} %get-tuple-element.29), channel_id=1, source_target_pairs={{0,4},{1,5},{2,6},{3,7},{4,0},{5,1},{6,2},{7,3},{8,12},{9,13},{10,... | collective-permute-start | bytes 442376 | tf_op jit(solution)/shard_map/ppermute | solution.py:40
  20.0 7.1 %collective-permute-start.1 = (bf16[128,1152]{1,0:T(8,128)(2,1)S(1)}, bf16[128,1152]{1,0:T(8,128)(2,1)S(1)}, u32[]{:S(2)}, u32[]{:S(2)}) collective-permute-start(bf16[128,1152]{1,0:T(8,128)(2,1)S(1)} %pad_maximum_fusion.2), channel_id=1, source_target_pairs={{0,1},{1,0},{2,3},{3,2},{4,5},{5,4},{6,7},{7,6},{8,9},{9,8},{10,11... | collective-permute-start | bytes 884744 | tf_op jit(solution)/shard_map/ppermute | solution.py:40
  21.2 10.2 %collective-permute-start.6 = (bf16[128,1152]{1,0:T(8,128)(2,1)S(1)}, bf16[128,1152]{1,0:T(8,128)(2,1)S(1)}, u32[]{:S(2)}, u32[]{:S(2)}) collective-permute-start(bf16[128,1152]{1,0:T(8,128)(2,1)S(1)} %pad_maximum_fusion.3), channel_id=1, source_target_pairs={{0,8},{1,9},{2,10},{3,11},{4,12},{5,13},{6,14},{7,15},{8,0},{9,1},... | collective-permute-start | bytes 884744 | tf_op jit(solution)/shard_map/ppermute | solution.py:40
  21.4 10.7 %collective-permute-start.8 = (bf16[128,1152]{1,0:T(8,128)(2,1)S(1)}, bf16[128,1152]{1,0:T(8,128)(2,1)S(1)}, u32[]{:S(2)}, u32[]{:S(2)}) collective-permute-start(bf16[128,1152]{1,0:T(8,128)(2,1)S(1)} %pad_maximum_fusion.4), channel_id=1, source_target_pairs={{0,16},{1,17},{2,18},{3,19},{4,20},{5,21},{6,22},{7,23},{8,24},{9,... | collective-permute-start | bytes 884744 | tf_op jit(solution)/shard_map/ppermute | solution.py:40
  27.2 12.1 %collective-permute-start.2 = (bf16[256,1152]{1,0:T(8,128)(2,1)S(1)}, bf16[256,1152]{1,0:T(8,128)(2,1)S(1)}, u32[]{:S(2)}, u32[]{:S(2)}) collective-permute-start(bf16[256,1152]{1,0:T(8,128)(2,1)S(1)} %get-tuple-element.60), channel_id=1, source_target_pairs={{0,7},{1,2},{2,1},{3,4},{4,3},{5,6},{6,5},{7,0},{8,15},{9,10},{10,... | collective-permute-start | bytes 1769480 | tf_op jit(solution)/shard_map/ppermute | solution.py:40
  31.5 10.0 %collective-permute-start.7 = (bf16[256,1152]{1,0:T(8,128)(2,1)S(1)}, bf16[256,1152]{1,0:T(8,128)(2,1)S(1)}, u32[]{:S(2)}, u32[]{:S(2)}) collective-permute-start(bf16[256,1152]{1,0:T(8,128)(2,1)S(1)} %pad_maximum_fusion), channel_id=1, source_target_pairs={{0,16},{1,17},{2,18},{3,19},{4,20},{5,21},{6,22},{7,23},{8,24},{9,... | collective-permute-start | bytes 1769480 | tf_op jit(solution)/shard_map/ppermute | solution.py:40
  32.1 10.0 %collective-permute-start.9 = (bf16[256,1152]{1,0:T(8,128)(2,1)S(1)}, bf16[256,1152]{1,0:T(8,128)(2,1)S(1)}, u32[]{:S(2)}, u32[]{:S(2)}) collective-permute-start(bf16[256,1152]{1,0:T(8,128)(2,1)S(1)} %pad_maximum_fusion.1), channel_id=1, source_target_pairs={{0,8},{1,9},{2,10},{3,11},{4,12},{5,13},{6,14},{7,15},{8,0},{9,1},... | collective-permute-start | bytes 1769480 | tf_op jit(solution)/shard_map/ppermute | solution.py:40
  39.4 5.3 %collective-permute-start.10 = (bf16[512,1152]{1,0:T(8,128)(2,1)S(1)}, bf16[512,1152]{1,0:T(8,128)(2,1)S(1)}, u32[]{:S(2)}, u32[]{:S(2)}) collective-permute-start(bf16[512,1152]{1,0:T(8,128)(2,1)S(1)} %constant_dynamic-update-slice_fusion.3), channel_id=1, source_target_pairs={{0,64},{1,65},{2,66},{3,67},{4,68},{5,69},{6,70},{7,71},{8,72},{9,... | collective-permute-start | bytes 3538952 | tf_op jit(solution)/shard_map/ppermute | solution.py:40
  48.5 3.6 %collective-permute-start.11 = (f16[256,1152]{1,0:T(8,128)(2,1)S(1)}, f16[256,1152]{1,0:T(8,128)(2,1)S(1)}, u32[]{:S(2)}, u32[]{:S(2)}) collective-permute-start(f16[256,1152]{1,0:T(8,128)(2,1)S(1)} %fusion.2), channel_id=1, source_target_pairs={{0,64},{1,65},{2,66},{3,67},{4,68},{5,69},{6,70},{7,71},{8,72},{9,... | collective-permute-start | bytes 1769480 | tf_op jit(solution)/shard_map/ppermute | solution.py:40
  48.8 14.8 %collective-permute-start.15 = (f16[256,1152]{1,0:T(8,128)(2,1)S(1)}, f16[256,1152]{1,0:T(8,128)(2,1)S(1)}, u32[]{:S(2)}, u32[]{:S(2)}) collective-permute-start(f16[256,1152]{1,0:T(8,128)(2,1)S(1)} %get-tuple-element.58), channel_id=1, source_target_pairs={{0,8},{1,9},{2,10},{3,11},{4,12},{5,13},{6,14},{7,15},{8,0},{9,1},... | collective-permute-start | bytes 1769480 | tf_op jit(solution)/shard_map/ppermute | solution.py:40
  50.2 9.9 %collective-permute-start.12 = (f16[256,1152]{1,0:T(8,128)(2,1)S(1)}, f16[256,1152]{1,0:T(8,128)(2,1)S(1)}, u32[]{:S(2)}, u32[]{:S(2)}) collective-permute-start(f16[256,1152]{1,0:T(8,128)(2,1)S(1)} %get-tuple-element.59), channel_id=1, source_target_pairs={{0,16},{1,17},{2,18},{3,19},{4,20},{5,21},{6,22},{7,23},{8,24},{9,... | collective-permute-start | bytes 1769480 | tf_op jit(solution)/shard_map/ppermute | solution.py:40
  52.4 11.2 %collective-permute-start.13 = (f16[256,1152]{1,0:T(8,128)(2,1)S(1)}, f16[256,1152]{1,0:T(8,128)(2,1)S(1)}, u32[]{:S(2)}, u32[]{:S(2)}) collective-permute-start(f16[256,1152]{1,0:T(8,128)(2,1)S(1)} %multiply_convert_fusion.1), channel_id=1, source_target_pairs={{0,7},{1,2},{2,1},{3,4},{4,3},{5,6},{6,5},{7,0},{8,15},{9,10},{10,... | collective-permute-start | bytes 1769480 | tf_op jit(solution)/shard_map/ppermute | solution.py:40
  54.6 11.1 %collective-permute-start.19 = (f16[256,1152]{1,0:T(8,128)(2,1)S(1)}, f16[256,1152]{1,0:T(8,128)(2,1)S(1)}, u32[]{:S(2)}, u32[]{:S(2)}) collective-permute-start(f16[256,1152]{1,0:T(8,128)(2,1)S(1)} %fusion.3), channel_id=1, source_target_pairs={{0,64},{1,65},{2,66},{3,67},{4,68},{5,69},{6,70},{7,71},{8,72},{9,... | collective-permute-start | bytes 1769480 | tf_op jit(solution)/shard_map/ppermute | solution.py:40
  63.9 7.0 %collective-permute-start.14 = (f16[128,1152]{1,0:T(8,128)(2,1)S(1)}, f16[128,1152]{1,0:T(8,128)(2,1)S(1)}, u32[]{:S(2)}, u32[]{:S(2)}) collective-permute-start(f16[128,1152]{1,0:T(8,128)(2,1)S(1)} %fusion.60), channel_id=1, source_target_pairs={{0,8},{1,9},{2,10},{3,11},{4,12},{5,13},{6,14},{7,15},{8,0},{9,1},... | collective-permute-start | bytes 884744 | tf_op jit(solution)/shard_map/ppermute | solution.py:40
  65.1 6.8 %collective-permute-start.16 = (f16[128,1152]{1,0:T(8,128)(2,1)S(1)}, f16[128,1152]{1,0:T(8,128)(2,1)S(1)}, u32[]{:S(2)}, u32[]{:S(2)}) collective-permute-start(f16[128,1152]{1,0:T(8,128)(2,1)S(1)} %fusion.59), channel_id=1, source_target_pairs={{0,16},{1,17},{2,18},{3,19},{4,20},{5,21},{6,22},{7,23},{8,24},{9,... | collective-permute-start | bytes 884744 | tf_op jit(solution)/shard_map/ppermute | solution.py:40
  66.0 6.8 %collective-permute-start.20 = (f16[128,1152]{1,0:T(8,128)(2,1)S(1)}, f16[128,1152]{1,0:T(8,128)(2,1)S(1)}, u32[]{:S(2)}, u32[]{:S(2)}) collective-permute-start(f16[128,1152]{1,0:T(8,128)(2,1)S(1)} %fusion.56), channel_id=1, source_target_pairs={{0,1},{1,0},{2,3},{3,2},{4,5},{5,4},{6,7},{7,6},{8,9},{9,8},{10,11... | collective-permute-start | bytes 884744 | tf_op jit(solution)/shard_map/ppermute | solution.py:40
  72.0 8.0 %collective-permute-start.17 = (f16[128,1152]{1,0:T(8,128)(2,1)S(1)}, f16[128,1152]{1,0:T(8,128)(2,1)S(1)}, u32[]{:S(2)}, u32[]{:S(2)}) collective-permute-start(f16[128,1152]{1,0:T(8,128)(2,1)S(1)} %fusion.58), channel_id=1, source_target_pairs={{0,48},{1,49},{2,50},{3,51},{4,52},{5,53},{6,54},{7,55},{8,56},{9,... | collective-permute-start | bytes 884744 | tf_op jit(solution)/shard_map/ppermute | solution.py:40
  73.0 12.5 %copy-start.1 = (bf16[64,1152]{1,0:T(8,128)(2,1)S(1)}, bf16[64,1152]{1,0:T(8,128)(2,1)}, u32[]{:S(2)}) copy-start(bf16[64,1152]{1,0:T(8,128)(2,1)} %rows.3) | copy-start | bytes 442372
  73.0 12.5 %collective-permute-start.21 = (f16[64,1152]{1,0:T(8,128)(2,1)S(1)}, f16[64,1152]{1,0:T(8,128)(2,1)S(1)}, u32[]{:S(2)}, u32[]{:S(2)}) collective-permute-start(f16[64,1152]{1,0:T(8,128)(2,1)S(1)} %fusion.65), channel_id=1, source_target_pairs={{0,4},{1,5},{2,6},{3,7},{4,0},{5,1},{6,2},{7,3},{8,12},{9,13},{10,... | collective-permute-start | bytes 442376 | tf_op jit(solution)/shard_map/ppermute | solution.py:40
  80.2 6.5 %copy-start.3 = (bf16[64,1152]{1,0:T(8,128)(2,1)S(1)}, bf16[64,1152]{1,0:T(8,128)(2,1)}, u32[]{:S(2)}) copy-start(bf16[64,1152]{1,0:T(8,128)(2,1)} %rows.2) | copy-start | bytes 442372
  80.2 6.4 %collective-permute-start.18 = (f16[64,1152]{1,0:T(8,128)(2,1)S(1)}, f16[64,1152]{1,0:T(8,128)(2,1)S(1)}, u32[]{:S(2)}, u32[]{:S(2)}) collective-permute-start(f16[64,1152]{1,0:T(8,128)(2,1)S(1)} %fusion.66), channel_id=1, source_target_pairs={{0,136},{1,137},{2,138},{3,139},{4,140},{5,141},{6,142},{7,143},{8... | collective-permute-start | bytes 442376 | tf_op jit(solution)/shard_map/ppermute | solution.py:40
